TPU v7x, 32 devices: a whole 2x2x4 slice. The times are simulated.
32 devices in a mesh: dp: 16 (over z, y, x), mp: 2 (over core).
Axes of the slice: x: 2, y: 2, z: 4, core: 2. Of those that a mesh axis runs over, the one named last changes fastest.
Arguments:
- tokens: bfloat16 [16384, 768], P(('dp', 'mp')), may hold values from -6 to 6
- cotangent: bfloat16 [16384, 768], P(('dp', 'mp')), may hold values from -6 to 6
- gain_attn: float32 [768], replicated, may hold values from 0.1 to 1.9
- w_query: bfloat16 [768, 768], P('dp', 'mp'), may hold values from -0.0546875 to 0.0546875
- w_key: bfloat16 [768, 768], P('dp', 'mp'), may hold values from -0.21875 to 0.21875
- w_value: bfloat16 [768, 768], P('dp', 'mp'), may hold values from -0.21875 to 0.21875
- w_out: bfloat16 [768, 768], P('mp', 'dp'), may hold values from -1.75 to 1.75
- rel_table: float32 [32, 12], replicated, may hold values from -5 to 5
- buckets: int32 [2047], replicated, may hold values from 0 to 31
- gain_ffn: float32 [768], replicated, may hold values from 0.1 to 1.9
- w_gate: bfloat16 [768, 2048], P('dp', 'mp'), may hold values from -0.21875 to 0.21875
- w_up: bfloat16 [768, 2048], P('dp', 'mp'), may hold values from -0.21875 to 0.21875
- w_down: bfloat16 [2048, 768], P('mp', 'dp'), may hold values from -0.125 to 0.125
Outputs:
- output: bfloat16 [16384, 768], P(('dp', 'mp'))
- d_tokens: bfloat16 [16384, 768], P(('dp', 'mp'))
- d_gain_attn: float32 [768], replicated
- d_w_query: float32 [768, 768], P('dp', 'mp')
- d_w_key: float32 [768, 768], P('dp', 'mp')
- d_w_value: float32 [768, 768], P('dp', 'mp')
- d_w_out: float32 [768, 768], P('mp', 'dp')
- d_rel_table: float32 [32, 12], replicated
- d_gain_ffn: float32 [768], replicated
- d_w_gate: float32 [768, 2048], P('dp', 'mp')
- d_w_up: float32 [768, 2048], P('dp', 'mp')
- d_w_down: float32 [2048, 768], P('mp', 'dp')
Inputs may be any that keep to these rules, and one draw needn't show every extreme that they name: `buckets`: entry o is the bucket of the offset key position minus query position = o - 1023.
All inputs are finite; a program needn't handle non-finite values.
Results may differ from a plain program's by a relative error of at most 0.02.
Values may be sent and summed in bfloat16 or wider, within the bound.
No kernel may reach another device: no remote copies, remote signals or barrier semaphores. Data moves between devices by JAX's collectives and lax.ppermute only.
A program may use at most 256 MiB of HBM per device.

v0:
```python
import jax
import jax.numpy as jnp
from jax import lax
from jax.sharding import PartitionSpec as P

epsilon = 1e-06
block_limit = 512
precise = lax.Precision.HIGHEST


def as_sent(array):

    def short(part):
        return part.astype(jnp.bfloat16) if part.dtype == jnp.float32 else part

    return jax.tree.map(short, array)


def matmul_nn(left, right):
    return jnp.dot(left, right, preferred_element_type=jnp.float32)


def matmul_nt(left, right):
    return lax.dot_general(
        left, right, (((1,), (1,)), ((), ())), preferred_element_type=jnp.float32
    )


def matmul_tn(left, right):
    return lax.dot_general(
        left, right, (((0,), (0,)), ((), ())), preferred_element_type=jnp.float32
    )


def rms_parts(inputs):
    scale = lax.rsqrt(jnp.mean(inputs * inputs, axis=-1, keepdims=True) + epsilon)
    return (inputs * scale, scale)


def rms_back(d_normed, unit, scale, gain):
    d_unit = d_normed * gain
    return scale * (d_unit - unit * jnp.mean(d_unit * unit, axis=-1, keepdims=True))


def gated(gate_pre, up_pre):
    return jax.nn.gelu(gate_pre, approximate=True) * up_pre


def window_base(first_query, first_key, row_count, seq_len):
    return first_key - first_query - row_count + seq_len


def make_bias(bias_full, base, row_count, width):
    span = width + row_count - 1
    head_count = bias_full.shape[0]
    strip = lax.dynamic_slice_in_dim(bias_full, base, span, 1)
    tiled = jnp.tile(strip, (1, row_count + 1))
    window = tiled[:, row_count - 1 : row_count - 1 + row_count * (span - 1)]
    return window.reshape(head_count, row_count, span - 1)[:, :, :width]


def skew_sum(d_block, row_count, width):
    head_count = d_block.shape[0]
    span = width + row_count - 1
    padded = jnp.pad(d_block, ((0, 0), (0, 0), (row_count - 1, 0)))
    flat = padded.reshape(head_count, row_count * span)
    flat = jnp.pad(flat, ((0, 0), (0, row_count)))
    skewed = flat.reshape(head_count, row_count, span + 1)[:, :, :span]
    return jnp.sum(skewed, axis=1)


def add_window(d_bias, piece, base):
    current = lax.dynamic_slice_in_dim(d_bias, base, piece.shape[1], 1)
    return lax.dynamic_update_slice_in_dim(d_bias, current + piece, base, 1)


def sum_rows(partial_value):
    return lax.psum_scatter(
        partial_value.astype(jnp.bfloat16), "mp", scatter_dimension=0, tiled=True
    ).astype(jnp.float32)


def split_heads(queries, keys_all, values, head_count):
    row_count = queries.shape[0]
    seq_len = keys_all.shape[0]
    head_dim = queries.shape[1] // head_count
    width = min(block_limit, seq_len)
    blocks = seq_len // width
    heads_q = queries.reshape(row_count, head_count, head_dim)
    heads_k = keys_all.reshape(blocks, width, head_count, head_dim)
    heads_v = values.reshape(blocks, width, head_count, head_dim)
    starts = jnp.arange(blocks, dtype=jnp.int32) * width
    return (heads_q, heads_k, heads_v, starts, width)


def attend_forward(queries, keys_all, values, bias_full, head_count, first_row):
    row_count = queries.shape[0]
    seq_len = keys_all.shape[0]
    heads_q, heads_k, heads_v, starts, width = split_heads(queries, keys_all, values, head_count)

    def block_scores(key_block, first_key):
        raw_scores = jnp.einsum(
            "qhd,khd->hqk", heads_q, key_block, preferred_element_type=jnp.float32
        )
        base = window_base(first_row, first_key, row_count, seq_len)
        return raw_scores + make_bias(bias_full, base, row_count, width)

    def stats_step(running, pieces):
        top_now, total = running
        scores = block_scores(pieces[0], pieces[1])
        top_new = jnp.maximum(top_now, jnp.max(scores, axis=-1))
        total = total * jnp.exp(top_now - top_new) + jnp.sum(
            jnp.exp(scores - top_new[..., None]), axis=-1
        )
        return ((top_new, total), None)

    start_top = jnp.full((head_count, row_count), -jnp.inf, jnp.float32)
    start_total = jnp.zeros((head_count, row_count), jnp.float32)
    (top_all, total), _ = lax.scan(stats_step, (start_top, start_total), (heads_k, starts))
    log_total = top_all + jnp.log(total)

    def mix_step(running, pieces):
        scores = block_scores(pieces[0], pieces[2])
        probs_low = jnp.exp(scores - log_total[..., None]).astype(jnp.bfloat16)
        update = jnp.einsum(
            "hqk,khd->qhd", probs_low, pieces[1], preferred_element_type=jnp.float32
        )
        return (running + update, None)

    start_mix = jnp.zeros(heads_q.shape, jnp.float32)
    mixed_f, _ = lax.scan(mix_step, start_mix, (heads_k, heads_v, starts))
    return (mixed_f.reshape(row_count, queries.shape[1]), log_total)


def attend_backward(
    queries, keys_all, values, bias_full, head_count, first_row, log_total, deltas, d_mixed
):
    row_count = queries.shape[0]
    seq_len = keys_all.shape[0]
    heads_q, heads_k, heads_v, starts, width = split_heads(queries, keys_all, values, head_count)
    heads_d = d_mixed.reshape(heads_q.shape)

    def back_step(running, pieces):
        d_query, d_bias = running
        key_block, value_block, first_key = pieces
        base = window_base(first_row, first_key, row_count, seq_len)
        scores = jnp.einsum("qhd,khd->hqk", heads_q, key_block, preferred_element_type=jnp.float32)
        scores = scores + make_bias(bias_full, base, row_count, width)
        probs = jnp.exp(scores - log_total[..., None])
        d_probs = jnp.einsum(
            "qhd,khd->hqk", heads_d, value_block, preferred_element_type=jnp.float32
        )
        d_scores = (probs * (d_probs - deltas[..., None])).astype(jnp.bfloat16)
        d_query = d_query + jnp.einsum(
            "hqk,khd->qhd", d_scores, key_block, preferred_element_type=jnp.float32
        )
        d_bias = add_window(d_bias, skew_sum(d_scores.astype(jnp.float32), row_count, width), base)
        probs_low = probs.astype(jnp.bfloat16)
        d_value = jnp.einsum("hqk,qhd->khd", probs_low, heads_d, preferred_element_type=jnp.float32)
        d_key = jnp.einsum("hqk,qhd->khd", d_scores, heads_q, preferred_element_type=jnp.float32)
        return ((d_query, d_bias), (d_key, d_value))

    start_query = jnp.zeros(heads_q.shape, jnp.float32)
    (d_query, d_bias), kv_parts = lax.scan(
        back_step, (start_query, jnp.zeros_like(bias_full)), (heads_k, heads_v, starts)
    )
    feature_count = queries.shape[1]
    d_query = d_query.reshape(row_count, feature_count)
    return (
        d_query,
        d_bias,
        kv_parts[0].reshape(seq_len, feature_count),
        kv_parts[1].reshape(seq_len, feature_count),
    )


def on_device(
    tokens,
    cotangent,
    gain_attn,
    w_query,
    w_key,
    w_value,
    w_out,
    rel_table,
    buckets,
    gain_ffn,
    w_gate,
    w_up,
    w_down,
):
    head_count = rel_table.shape[1]
    bucket_count = rel_table.shape[0]
    inputs = tokens.astype(jnp.float32)
    row_count = inputs.shape[0]
    feature_count = inputs.shape[1]
    first_row = lax.axis_index("mp") * row_count
    attn_parts = (w_query, w_key, w_value, w_out.T)
    ffn_parts = (w_gate, w_up, w_down.T)
    ffn_cols = ()
    col_parts = lax.all_gather(as_sent(attn_parts + ffn_cols), "mp", axis=1, tiled=True)
    full_parts = lax.all_gather(as_sent(tuple(col_parts) + ffn_parts), "dp", axis=0, tiled=True)
    query_full, key_full, value_full, out_full, gate_full, up_full, down_full = full_parts
    unit_a, scale_a = rms_parts(inputs)
    normed_a = (unit_a * gain_attn).astype(jnp.bfloat16)
    queries = matmul_nn(normed_a, query_full).astype(jnp.bfloat16)
    own_keys = matmul_nn(normed_a, key_full).astype(jnp.bfloat16)
    own_values = matmul_nn(normed_a, value_full).astype(jnp.bfloat16)
    keys_all, values = (
        lax.all_gather(own_keys, "mp", axis=0, tiled=True),
        lax.all_gather(own_values, "mp", axis=0, tiled=True),
    )
    one_hot = (buckets[:, None] == jnp.arange(bucket_count, dtype=jnp.int32)[None, :]).astype(
        jnp.float32
    )
    bias_full = jnp.dot(one_hot, rel_table, precision=precise).T
    mixed_f, log_total = attend_forward(queries, keys_all, values, bias_full, head_count, first_row)
    mixed_out = mixed_f.astype(jnp.bfloat16)
    attended = inputs + matmul_nt(mixed_out, out_full)
    unit_f, scale_f = rms_parts(attended)
    normed_f = (unit_f * gain_ffn).astype(jnp.bfloat16)
    normed_seq, cot_seq = (
        lax.all_gather(normed_f, "mp", axis=0, tiled=True),
        lax.all_gather(cotangent, "mp", axis=0, tiled=True),
    )
    gate_pre = matmul_nn(normed_seq, gate_full)
    up_pre = matmul_nn(normed_seq, up_full)
    hidden = gated(gate_pre, up_pre).astype(jnp.bfloat16)
    output = attended + sum_rows(matmul_nt(hidden, down_full))
    d_hidden = matmul_nn(cot_seq, down_full)
    d_down = matmul_tn(cot_seq, hidden)
    _, pull_gate = jax.vjp(gated, gate_pre, up_pre)
    d_gate, d_up = pull_gate(d_hidden)
    d_gate = d_gate.astype(jnp.bfloat16)
    d_up = d_up.astype(jnp.bfloat16)
    d_normed_f = sum_rows(matmul_nt(d_gate, gate_full) + matmul_nt(d_up, up_full))
    d_gate_w = matmul_tn(normed_seq, d_gate)
    d_up_w = matmul_tn(normed_seq, d_up)
    d_gain_f = jnp.sum(d_normed_f * unit_f, axis=0)
    d_attended = cotangent.astype(jnp.float32) + rms_back(d_normed_f, unit_f, scale_f, gain_ffn)
    d_att_low = d_attended.astype(jnp.bfloat16)
    d_out_w = matmul_tn(d_att_low, mixed_out)
    d_mixed = matmul_nn(d_att_low, out_full).astype(jnp.bfloat16)
    head_dim = feature_count // head_count
    deltas = jnp.sum(
        (d_mixed.astype(jnp.float32) * mixed_f).reshape(row_count, head_count, head_dim), axis=-1
    ).T
    d_query, d_bias, d_keys_part, d_values_part = attend_backward(
        queries, keys_all, values, bias_full, head_count, first_row, log_total, deltas, d_mixed
    )
    d_keys_own, d_values_own = (
        lax.psum_scatter(
            d_keys_part.astype(jnp.bfloat16), "mp", scatter_dimension=0, tiled=True
        ).astype(jnp.float32),
        lax.psum_scatter(
            d_values_part.astype(jnp.bfloat16), "mp", scatter_dimension=0, tiled=True
        ).astype(jnp.float32),
    )
    d_keys_own = d_keys_own.astype(jnp.bfloat16)
    d_values_own = d_values_own.astype(jnp.bfloat16)
    d_query = d_query.astype(jnp.bfloat16)
    d_normed_a = (
        matmul_nt(d_query, query_full)
        + matmul_nt(d_keys_own, key_full)
        + matmul_nt(d_values_own, value_full)
    )
    d_query_w = matmul_tn(normed_a, d_query)
    d_key_w = matmul_tn(normed_a, d_keys_own)
    d_value_w = matmul_tn(normed_a, d_values_own)
    d_gain_a = jnp.sum(d_normed_a * unit_a, axis=0)
    d_tokens = (d_attended + rms_back(d_normed_a, unit_a, scale_a, gain_attn)).astype(jnp.bfloat16)
    d_table = jnp.dot(d_bias, one_hot, precision=precise).T
    row_grads = (
        lax.psum_scatter(
            d_query_w.astype(jnp.bfloat16), "dp", scatter_dimension=0, tiled=True
        ).astype(jnp.float32),
        lax.psum_scatter(
            d_key_w.astype(jnp.bfloat16), "dp", scatter_dimension=0, tiled=True
        ).astype(jnp.float32),
        lax.psum_scatter(
            d_value_w.astype(jnp.bfloat16), "dp", scatter_dimension=0, tiled=True
        ).astype(jnp.float32),
        lax.psum_scatter(
            d_out_w.astype(jnp.bfloat16), "dp", scatter_dimension=0, tiled=True
        ).astype(jnp.float32),
        lax.psum_scatter(
            d_gate_w.astype(jnp.bfloat16), "dp", scatter_dimension=0, tiled=True
        ).astype(jnp.float32),
        lax.psum_scatter(d_up_w.astype(jnp.bfloat16), "dp", scatter_dimension=0, tiled=True).astype(
            jnp.float32
        ),
        lax.psum_scatter(d_down.astype(jnp.bfloat16), "dp", scatter_dimension=0, tiled=True).astype(
            jnp.float32
        ),
    )
    row_grads = tuple(row_grads)
    ffn_late = ()
    col_grads = tuple(
        jax.tree.map(
            lambda part: part.astype(jnp.float32),
            lax.psum_scatter(
                as_sent(row_grads[:4] + ffn_late), "mp", scatter_dimension=1, tiled=True
            ),
        )
    )
    ffn_done = row_grads[4:]
    small_sums = lax.psum((d_gain_a, d_gain_f, d_table), ("dp", "mp"))
    return (
        output.astype(jnp.bfloat16),
        d_tokens,
        small_sums[0],
        col_grads[0],
        col_grads[1],
        col_grads[2],
        col_grads[3].T,
        small_sums[2],
        small_sums[1],
        ffn_done[0],
        ffn_done[1],
        ffn_done[2].T,
    )


def solution(mesh):
    placed = (
        P(("dp", "mp"), None),
        P(("dp", "mp"), None),
        P(),
        P("dp", "mp"),
        P("dp", "mp"),
        P("dp", "mp"),
        P("mp", "dp"),
        P(),
        P(),
        P(),
        P("dp", "mp"),
        P("dp", "mp"),
        P("mp", "dp"),
    )
    return jax.shard_map(
        on_device,
        mesh=mesh,
        in_specs=placed,
        out_specs=(
            P(("dp", "mp"), None),
            P(("dp", "mp"), None),
            P(),
            P("dp", "mp"),
            P("dp", "mp"),
            P("dp", "mp"),
            P("mp", "dp"),
            P(),
            P(),
            P("dp", "mp"),
            P("dp", "mp"),
            P("mp", "dp"),
        ),
        check_vma=False,
    )
```

profile of v0, /device:TPU:0, one launch (start us, length us, event | category | flops | bytes accessed | tf_op | source)
XLA Modules:
  0.0 2528.1 jit_solution(8026352907383313406)
XLA Ops:
  19.7 50.0 %all-gather.12.cloned.1.call-done = bf16[768,768]{1,0:T(8,128)(2,1)} async-done(((bf16[48,768]{1,0:T(8,128)(2,1)}), bf16[768,768]{1,0:T(8,128)(2,1)}) %all-gather.12.cloned.1.call-update) | async-done | bytes 1179664 | tf_op jit(solution)/shard_map/all_gather | solution.py:202
  73.0 54.5 %all-gather.16.cloned.1.call-done = bf16[768,768]{1,0:T(8,128)(2,1)} async-done(((bf16[48,768]{1,0:T(8,128)(2,1)}), bf16[768,768]{1,0:T(8,128)(2,1)}) %all-gather.16.cloned.1.call-update) | async-done | bytes 1179664 | tf_op jit(solution)/shard_map/all_gather | solution.py:202
  134.5 50.9 %all-gather.20.cloned.1.call-done = bf16[768,768]{1,0:T(8,128)(2,1)} async-done(((bf16[48,768]{1,0:T(8,128)(2,1)}), bf16[768,768]{1,0:T(8,128)(2,1)}) %all-gather.20.cloned.1.call-update) | async-done | bytes 1179664 | tf_op jit(solution)/shard_map/all_gather | solution.py:202
  218.5 331.5 %while.53 = (s32[]{:T(128)}, f32[12,512]{1,0:T(8,128)S(1)}, f32[12,512]{1,0:T(8,128)S(1)}, bf16[2,512,12,64]{1,3,2,0:T(8,128)(2,1)}, bf16[512,12,64]{0,2,1:T(8,1...) while((s32[]{:T(128)}, f32[12,512]{1,0:T(8,128)S(1)}, ...), condition=%wide.region_4.5_spmd.clone, body=%wide.region_1.4_spmd.clone.sunk | while | flops 418412544 | bytes 329072608 | solution.py:119
  255.5 38.4 %tile.58 = f32[12,524799]{1,0:T(8,128)} reshape(f32[12,513,1023]{2,1,0:T(8,128)} %tile.57) | data formatting | bytes 50380704 | tf_op jit(solution)/shard_map/while/body/eval_jaxpr/tile | solution.py:57
  319.6 41.8 %reshape.166 = f32[12,512,1022]{2,1,0:T(8,128)} reshape(f32[12,523264]{1,0:T(8,128)} %slice.93) | data formatting | bytes 50233344 | tf_op jit(solution)/shard_map/while/body/eval_jaxpr/reshape | solution.py:59
  409.4 38.4 %tile.58 = f32[12,524799]{1,0:T(8,128)} reshape(f32[12,513,1023]{2,1,0:T(8,128)} %tile.57) | data formatting | bytes 50380704 | tf_op jit(solution)/shard_map/while/body/eval_jaxpr/tile | solution.py:57
  473.4 41.8 %reshape.166 = f32[12,512,1022]{2,1,0:T(8,128)} reshape(f32[12,523264]{1,0:T(8,128)} %slice.93) | data formatting | bytes 50233344 | tf_op jit(solution)/shard_map/while/body/eval_jaxpr/reshape | solution.py:59
  550.1 334.8 %while.54 = (s32[]{:T(128)}, f32[512,12,64]{0,2,1:T(8,128)}, bf16[2,512,12,64]{1,3,2,0:T(8,128)(2,1)}, bf16[2,512,12,64]{1,3,2,0:T(8,128)(2,1)}, bf16[512,12,64]...) while((s32[]{:T(128)}, f32[512,12,64]{0,2,1:T(8,128)}, ...), condition=%wide.region_6.7_spmd.clone, body=%wide.region_5.6_spmd.clone.sunk | while | flops 815529984 | bytes 244630992 | solution.py:131
  587.1 38.4 %tile.60 = f32[12,524799]{1,0:T(8,128)} reshape(f32[12,513,1023]{2,1,0:T(8,128)} %tile.59) | data formatting | bytes 50380704 | tf_op jit(solution)/shard_map/while/body/eval_jaxpr/tile | solution.py:57
  651.0 41.8 %reshape.167 = f32[12,512,1022]{2,1,0:T(8,128)} reshape(f32[12,523264]{1,0:T(8,128)} %slice.95) | data formatting | bytes 50233344 | tf_op jit(solution)/shard_map/while/body/eval_jaxpr/reshape | solution.py:59
  802.6 41.8 %reshape.167 = f32[12,512,1022]{2,1,0:T(8,128)} reshape(f32[12,523264]{1,0:T(8,128)} %slice.95) | data formatting | bytes 50233344 | tf_op jit(solution)/shard_map/while/body/eval_jaxpr/reshape | solution.py:59
  906.6 56.2 %all-gather.26.cloned.1.call-done = bf16[768,1024]{1,0:T(8,128)(2,1)} async-done(((bf16[48,1024]{1,0:T(8,128)(2,1)}), bf16[768,1024]{1,0:T(8,128)(2,1)}) %all-gather.26.cloned.1.call-update) | async-done | bytes 1572880 | tf_op jit(solution)/shard_map/all_gather | solution.py:202
  972.8 61.8 %all-gather.30.cloned.1.call-done = bf16[768,1024]{1,0:T(8,128)(2,1)} async-done(((bf16[48,1024]{1,0:T(8,128)(2,1)}), bf16[768,1024]{1,0:T(8,128)(2,1)}) %all-gather.30.cloned.1.call-update) | async-done | bytes 1572880 | tf_op jit(solution)/shard_map/all_gather | solution.py:202
  1088.4 567.6 %while.55 = (s32[]{:T(128)}, f32[512,12,64]{0,2,1:T(8,128)}, f32[12,2047]{1,0:T(8,128)S(1)}, bf16[2,512,12,64]{1,3,2,0:T(8,128)(2,1)}, bf16[2,512,12,64]{1,3,2,0...) while((s32[]{:T(128)}, f32[512,12,64]{0,2,1:T(8,128)}, ...), condition=%wide.region_14.15_spmd.clone, body=%wide.region_12.14_spmd.clone.sunk | while | flops 2045497344 | bytes 501796704 | solution.py:164
  1166.1 55.1 %reshape.168 = f32[12,512,1022]{2,1,0:T(8,128)} reshape(f32[12,523264]{1,0:T(8,128)} %slice.99) | data formatting | bytes 50233344 | tf_op jit(solution)/shard_map/while/body/eval_jaxpr/reshape | solution.py:59
  1444.6 54.9 %reshape.168 = f32[12,512,1022]{2,1,0:T(8,128)} reshape(f32[12,523264]{1,0:T(8,128)} %slice.99) | data formatting | bytes 50233344 | tf_op jit(solution)/shard_map/while/body/eval_jaxpr/reshape | solution.py:59
  1686.2 99.7 %reduce-scatter.34.cloned.1.call-done = bf16[48,768]{1,0:T(8,128)(2,1)} async-done(((bf16[768,768]{1,0:T(8,128)(2,1)}), bf16[48,768]{1,0:T(8,128)(2,1)}) %reduce-scatter.34.cloned.1.call-update) | async-done | bytes 73744 | tf_op jit(solution)/shard_map/reduce_scatter | solution.py:274
  1811.8 127.1 %reduce-scatter.54.cloned.1.call-done = bf16[48,1024]{1,0:T(8,128)(2,1)} async-done(((bf16[768,1024]{1,0:T(8,128)(2,1)}), bf16[48,1024]{1,0:T(8,128)(2,1)}) %reduce-scatter.54.cloned.1.call-update) | async-done | bytes 98320
  1940.9 126.3 %reduce-scatter.44.cloned.1.call-done = bf16[48,1024]{1,0:T(8,128)(2,1)} async-done(((bf16[768,1024]{1,0:T(8,128)(2,1)}), bf16[48,1024]{1,0:T(8,128)(2,1)}) %reduce-scatter.44.cloned.1.call-update) | async-done | bytes 98320 | tf_op jit(solution)/shard_map/reduce_scatter | solution.py:289
  2068.8 126.5 %reduce-scatter.42.cloned.1.call-done = bf16[48,1024]{1,0:T(8,128)(2,1)} async-done(((bf16[768,1024]{1,0:T(8,128)(2,1)}), bf16[48,1024]{1,0:T(8,128)(2,1)}) %reduce-scatter.42.cloned.1.call-update) | async-done | bytes 98320 | tf_op jit(solution)/shard_map/reduce_scatter | solution.py:286
  2222.1 123.4 %reduce-scatter.38.cloned.1.call-done = bf16[48,768]{1,0:T(8,128)(2,1)} async-done(((bf16[768,768]{1,0:T(8,128)(2,1)}), bf16[48,768]{1,0:T(8,128)(2,1)}) %reduce-scatter.38.cloned.1.call-update) | async-done | bytes 73744 | tf_op jit(solution)/shard_map/reduce_scatter | solution.py:280
  2347.3 126.2 %reduce-scatter.36.cloned.1.call-done = bf16[48,768]{1,0:T(8,128)(2,1)} async-done(((bf16[768,768]{1,0:T(8,128)(2,1)}), bf16[48,768]{1,0:T(8,128)(2,1)}) %reduce-scatter.36.cloned.1.call-update) | async-done | bytes 73744 | tf_op jit(solution)/shard_map/reduce_scatter | solution.py:277
  2478.0 40.1 %all-reduce.2 = (f32[768]{0:T(1024)}, f32[32,12]{0,1:T(8,128)}, f32[768]{0:T(1024)}) all-reduce(f32[768]{0:T(1024)S(1)} %get-tuple-element.919, f32[32,12]{0,1:T(8,128)S(1)} %fusion.66, f32[768]{0:T(1024)S(1)} %copy-done.32), channel_id=1, replica_groups=mesh['dp'=16,'mp'=2] {'dp','mp'}, use_global_device_ids=true, to_apply=%region_19.20 | all-reduce | flops 1920 | bytes 15360 | tf_op jit(solution)/shard_map/psum | solution.py:307
  (317 shorter events, 1009.4 us)
Async XLA Ops:
  11.0 116.5 %all-gather.16.cloned.1.call-start = ((), (), s32[]{:S(2)}) async-start(), calls=%async_computation.17 | async-start | bytes 1253376 | tf_op jit(solution)/shard_map/all_gather | solution.py:202
  14.5 170.9 %all-gather.20.cloned.1.call-start = ((), (), s32[]{:S(2)}) async-start(), calls=%async_computation.19 | async-start | bytes 1253376 | tf_op jit(solution)/shard_map/all_gather | solution.py:202
  18.2 177.9 %all-gather.14.cloned.1.call-start = ((), (), s32[]{:S(2)}) async-start(), calls=%async_computation.16 | async-start | bytes 2359296 | tf_op jit(solution)/shard_map/all_gather | solution.py:211
  73.0 136.1 %all-gather.18.cloned.1.call-start = ((), (), s32[]{:S(2)}) async-start(), calls=%async_computation.18 | async-start | bytes 2359296 | tf_op jit(solution)/shard_map/all_gather | solution.py:210
  130.6 754.4 %all-gather.22.cloned.1.call-start = ((), (), s32[]{:S(2)}) async-start(), calls=%async_computation.20 | async-start | bytes 1253376 | tf_op jit(solution)/shard_map/all_gather | solution.py:202
  132.7 759.4 %all-gather.28.cloned.1.call-start = ((), (), s32[]{:S(2)}) async-start(), calls=%async_computation.23 | async-start | bytes 1671168 | tf_op jit(solution)/shard_map/all_gather | solution.py:202
  133.4 767.6 %all-gather.24.cloned.1.call-start = ((), (), s32[]{:S(2)}) async-start(), calls=%async_computation.21 | async-start | bytes 2359296 | tf_op jit(solution)/shard_map/all_gather | solution.py:223
  889.9 73.0 %all-gather.26.cloned.1.call-start = ((), (), s32[]{:S(2)}) async-start(), calls=%async_computation.22 | async-start | bytes 1671168 | tf_op jit(solution)/shard_map/all_gather | solution.py:202
  890.6 82.2 %all-gather.32.cloned.1.call-start = ((), (), s32[]{:S(2)}) async-start(), calls=%async_computation.26 | async-start | bytes 2359296 | tf_op jit(solution)/shard_map/all_gather | solution.py:224
  891.2 143.4 %all-gather.30.cloned.1.call-start = ((), (), s32[]{:S(2)}) async-start(), calls=%async_computation.24 | async-start | bytes 1671168 | tf_op jit(solution)/shard_map/all_gather | solution.py:202
  892.0 168.3 %reduce-scatter.28.cloned.1.call-start = ((), (), s32[]{:S(2)}) async-start(), calls=%async_computation.27 | async-start | bytes 2359296 | tf_op jit(solution)/shard_map/reduce_scatter | solution.py:78
  1056.9 627.5 %reduce-scatter.40.cloned.1.call-start = ((), (), s32[]{:S(2)}) async-start(), calls=%async_computation.33 | async-start | bytes 1253376 | tf_op jit(solution)/shard_map/reduce_scatter | solution.py:283
  1085.5 700.3 %reduce-scatter.34.cloned.1.call-start = ((), (), s32[]{:S(2)}) async-start(), calls=%async_computation.30 | async-start | bytes 1253376 | tf_op jit(solution)/shard_map/reduce_scatter | solution.py:274
  1659.8 136.3 %reduce-scatter.32.cloned.1.call-start = ((), (), s32[]{:S(2)}) async-start(), calls=%async_computation.29 | async-start | bytes 2359296 | tf_op jit(solution)/shard_map/reduce_scatter | solution.py:255
  1663.2 145.4 %reduce-scatter.30.cloned.1.call-start = ((), (), s32[]{:S(2)}) async-start(), calls=%async_computation.28 | async-start | bytes 2359296 | tf_op jit(solution)/shard_map/reduce_scatter | solution.py:252
  1667.9 271.1 %reduce-scatter.54.cloned.1.call-start = ((), (), s32[]{:S(2)}) async-start(), calls=%async_computation.40 | async-start | bytes 1671168
  1673.6 393.7 %reduce-scatter.44.cloned.1.call-start = ((), (), s32[]{:S(2)}) async-start(), calls=%async_computation.35 | async-start | bytes 1671168 | tf_op jit(solution)/shard_map/reduce_scatter | solution.py:289
  1679.6 515.8 %reduce-scatter.42.cloned.1.call-start = ((), (), s32[]{:S(2)}) async-start(), calls=%async_computation.34 | async-start | bytes 1671168 | tf_op jit(solution)/shard_map/reduce_scatter | solution.py:286
  1684.3 519.8 %reduce-scatter.52.cloned.1.call-start = ((), (), s32[]{:S(2)}) async-start(), calls=%async_computation.39 | async-start | bytes 294912
  1686.1 529.0 %reduce-scatter.46.cloned.1.call-start = ((), (), s32[]{:S(2)}) async-start(), calls=%async_computation.36 | async-start | bytes 294912
  1787.6 557.9 %reduce-scatter.38.cloned.1.call-start = ((), (), s32[]{:S(2)}) async-start(), calls=%async_computation.32 | async-start | bytes 1253376 | tf_op jit(solution)/shard_map/reduce_scatter | solution.py:280
  1799.2 674.2 %reduce-scatter.36.cloned.1.call-start = ((), (), s32[]{:S(2)}) async-start(), calls=%async_computation.31 | async-start | bytes 1253376 | tf_op jit(solution)/shard_map/reduce_scatter | solution.py:277
  1811.8 706.3 %reduce-scatter.50.cloned.1.call-start = ((), (), s32[]{:S(2)}) async-start(), calls=%async_computation.38 | async-start | bytes 294912
  2347.2 172.5 %reduce-scatter.48.cloned.1.call-start = ((), (), s32[]{:S(2)}) async-start(), calls=%async_computation.37 | async-start | bytes 294912
  (48 other events, 2309.8 us)
Sparse Core Ops, SparseCore 0:
  11.1 58.5 all-gather.11
  72.5 54.9 all-gather.15
  130.3 54.9 all-gather.19
  187.4 8.6 all-gather.13
  198.0 10.9 all-gather.17
  211.7 57.2 all-gather.21
  271.8 56.7 all-gather.27
  890.0 10.9 all-gather.23
  903.8 59.0 all-gather.25
  964.2 8.5 all-gather.31
  975.6 59.0 all-gather.29
  1051.9 7.7 reduce-scatter.27
  1062.1 10.2 reduce-scatter.25
  1085.7 125.6 reduce-scatter.39
  1659.9 125.9 reduce-scatter.33
  1788.0 8.0 reduce-scatter.31
  1798.2 10.2 reduce-scatter.29
  1813.2 125.7 reduce-scatter.53
  1943.7 123.4 reduce-scatter.43
  2071.9 123.4 reduce-scatter.41
  2206.4 8.7 reduce-scatter.45
  2219.9 125.5 reduce-scatter.37
  2350.1 123.3 reduce-scatter.35
  2484.3 8.7 reduce-scatter.47
  (2 shorter events, 12.9 us)
where the time goes:
time: 2540 us; the launch traced here: 2530 us
  local copies, waits for them, and re-layouts  1120 us (44%)
  waiting for transfers between devices  1070 us (42%)
  matrix products  158 us (6%)
  loops' own time  68.7 us (3%)
  blocking collectives  52.9 us (2%)
  other arithmetic  42.6 us (2%)
    another operation x12, local copies, waits for them, and re-layouts, make_bias(): tiled = jnp.tile(strip, (1, row_count + 1))  301 us
    reshape x6, local copies, waits for them, and re-layouts, make_bias(): return window.reshape(head_count, row_count, span - 1)[:, :, :width]  277 us
    all_gather x7, waiting for transfers between devices, on_device(): lax.all_gather(as_sent(tuple(col_parts) + ffn_parts), 'dp', axis=0, tiled...  274 us
    slice x6, local copies, waits for them, and re-layouts, make_bias(): window = tiled[:, row_count - 1:row_count - 1 + row_count * (span - 1)]  154 us
    while x36, local copies, waits for them, and re-layouts  148 us
    unnamed x31, waiting for transfers between devices  143 us
    reduce_scatter x1, waiting for transfers between devices, on_device(): lax.psum_scatter(d_gate_w.astype(jnp.bfloat16), 'dp', scatter_dimension=0...  127 us
    reduce_scatter x1, waiting for transfers between devices, on_device(): lax.psum_scatter(d_up_w.astype(jnp.bfloat16), 'dp', scatter_dimension=0,...  126 us
  transfers between devices with their start and end apart: 26, of which 20 were waited for; matrix products, arithmetic and copies ran while one was open for 51% of the time, Pallas kernels for 0%

commit v1 on v0

--- a/solution.py
+++ b/solution.py
@@ -1,6 +1,8 @@
 import jax
 import jax.numpy as jnp
 from jax import lax
+from jax.experimental import pallas as pl
+from jax.experimental.pallas import tpu as pltpu
 from jax.sharding import PartitionSpec as P
 
 epsilon = 1e-06
@@ -321,6 +323,552 @@
     )
 
 
+MXU_ROWS = 256
+LANES = 128
+VMEM_LIMIT = 56 * 2**20
+
+
+def call(body, grid, in_specs, out_specs, out_shape, scratch=(), prefetch=0, flops=0, moved=0):
+    return pl.pallas_call(
+        body,
+        grid_spec=pltpu.PrefetchScalarGridSpec(
+            num_scalar_prefetch=prefetch,
+            grid=grid,
+            in_specs=in_specs,
+            out_specs=out_specs,
+            scratch_shapes=list(scratch),
+        ),
+        out_shape=out_shape,
+        compiler_params=pltpu.CompilerParams(vmem_limit_bytes=VMEM_LIMIT),
+        cost_estimate=pl.CostEstimate(flops=flops, bytes_accessed=moved, transcendentals=0),
+    )
+
+
+def shaped(shape, dtype):
+    return jax.ShapeDtypeStruct(shape, dtype)
+
+
+def whole(shape):
+    return pl.BlockSpec(shape, lambda *_: (0,) * len(shape))
+
+
+def head_masks(dtype):
+    lane = lax.broadcasted_iota(jnp.int32, (1, LANES), 1)
+    first = (lane < LANES // 2).astype(jnp.float32)
+    return (first.astype(dtype), (1.0 - first).astype(dtype))
+
+
+def project_body(x_ref, gain_ref, wq_ref, wk_ref, wv_ref, normed_ref, q_ref, k_ref, v_ref):
+    unit, _ = rms_parts(x_ref[...].astype(jnp.float32))
+    normed = (unit * gain_ref[...]).astype(jnp.bfloat16)
+    normed_ref[...] = normed
+    q_ref[...] = matmul_nn(normed, wq_ref[...]).astype(jnp.bfloat16)
+    k_ref[...] = matmul_nn(normed, wk_ref[...]).astype(jnp.bfloat16)
+    v_ref[...] = matmul_nn(normed, wv_ref[...]).astype(jnp.bfloat16)
+
+
+def attend_body(
+    q_ref, k_ref, v_ref, strip_ref, wo_ref, e_ref, mixed_ref, inv_ref, part_ref, table_ref, acc_ref
+):
+    pair = pl.program_id(0)
+    seq_len = k_ref.shape[0]
+    rows = table_ref.shape[1]
+    low_masks = head_masks(jnp.bfloat16)
+    masks = head_masks(jnp.float32)
+    for head in range(2):
+        row = jnp.broadcast_to(strip_ref[0, head : head + 1, :], (rows, 2 * seq_len))
+        table_ref[head] = pltpu.roll(row, 0, 1, stride=1, stride_axis=0)
+    keys = k_ref[...]
+    values = v_ref[...]
+    values_h = tuple(values * low_masks[h] + low_masks[1 - h] for h in range(2))
+    own_lanes = tuple(mask > 0.5 for mask in masks)
+    for block in range(seq_len // rows):
+        at = slice(block * rows, (block + 1) * rows)
+        queries = q_ref[at, :]
+        mixed = jnp.zeros((rows, LANES), jnp.float32)
+        inverse = jnp.zeros((rows, LANES), jnp.float32)
+        for head in range(2):
+            scores = matmul_nt(queries * low_masks[head], keys)
+            scores = scores + table_ref[head, :, seq_len - block * rows : 2 * seq_len - block * rows]
+            top = jnp.max(scores, axis=-1, keepdims=True)
+            weights = jnp.exp(scores - top).astype(jnp.bfloat16)
+            e_ref[head, at, :] = weights
+            summed = matmul_nn(weights, values_h[head])
+            total = jnp.where(own_lanes[head], pltpu.roll(summed, LANES // 2, 1), 1.0)
+            inv = masks[head] / total
+            mixed = mixed + summed * inv
+            inverse = inverse + inv
+        mixed_ref[at, :] = mixed
+        inv_ref[at, :] = inverse
+        update = matmul_nt(mixed.astype(jnp.bfloat16), wo_ref[...])
+
+        @pl.when(pair == 0)
+        def _():
+            acc_ref[at, :] = update
+
+        @pl.when(pair != 0)
+        def _():
+            acc_ref[at, :] += update
+
+    @pl.when(pair == pl.num_programs(0) - 1)
+    def _():
+        part_ref[...] = acc_ref[...].astype(jnp.bfloat16)
+
+
+def feed_body(
+    me_ref,
+    x_ref,
+    p_ref,
+    r_ref,
+    g_ref,
+    gain_ref,
+    wg_ref,
+    wu_ref,
+    wd_ref,
+    normed_ref,
+    hidden_ref,
+    dgate_ref,
+    dup_ref,
+    dn_ref,
+    send_ref,
+    own_ref,
+):
+    step = pl.program_id(0)
+    attended = x_ref[...].astype(jnp.float32) + (
+        p_ref[...].astype(jnp.float32) + r_ref[...].astype(jnp.float32)
+    )
+    unit, _ = rms_parts(attended)
+    normed = (unit * gain_ref[...]).astype(jnp.bfloat16)
+    normed_ref[...] = normed
+    gate = matmul_nn(normed, wg_ref[...])
+    up = matmul_nn(normed, wu_ref[...])
+    d_hidden = matmul_nn(g_ref[...], wd_ref[...])
+    square = gate * gate
+    root = 0.7978845608028654
+    bend = jnp.tanh(gate * (root + (root * 0.044715) * square))
+    half = 0.5 + 0.5 * bend
+    gelu = gate * half
+    slope = half + (0.5 * gate) * (1.0 - bend * bend) * (root + (3 * root * 0.044715) * square)
+    hidden = (gelu * up).astype(jnp.bfloat16)
+    d_gate = (d_hidden * up * slope).astype(jnp.bfloat16)
+    d_up = (d_hidden * gelu).astype(jnp.bfloat16)
+    hidden_ref[...] = hidden
+    dgate_ref[...] = d_gate
+    dup_ref[...] = d_up
+    dn_ref[...] = (matmul_nt(d_gate, wg_ref[...]) + matmul_nt(d_up, wu_ref[...])).astype(
+        jnp.bfloat16
+    )
+    out = matmul_nt(hidden, wd_ref[...])
+
+    @pl.when(step < pl.num_programs(0) // 2)
+    def _():
+        send_ref[...] = out.astype(jnp.bfloat16)
+
+    @pl.when(step >= pl.num_programs(0) // 2)
+    def _():
+        own_ref[...] = attended + out
+
+
+def grads_body(left_ref, right_ref, out_ref, turned_ref):
+    @pl.when(pl.program_id(0) == 0)
+    def _():
+        turned_ref[...] = left_ref[...].T
+
+    out_ref[...] = matmul_nn(turned_ref[...], right_ref[...]).astype(jnp.bfloat16)
+
+
+def turn_body(
+    x_ref,
+    p_ref,
+    r_ref,
+    g_ref,
+    a_ref,
+    b_ref,
+    gain_ref,
+    wo_ref,
+    datt_ref,
+    low_ref,
+    dmix_ref,
+    dgain_ref,
+):
+    attended = x_ref[...].astype(jnp.float32) + (
+        p_ref[...].astype(jnp.float32) + r_ref[...].astype(jnp.float32)
+    )
+    unit, scale = rms_parts(attended)
+    d_normed = a_ref[...].astype(jnp.float32) + b_ref[...].astype(jnp.float32)
+    d_gain = jnp.sum(d_normed * unit, axis=0, keepdims=True)
+    d_attended = g_ref[...].astype(jnp.float32) + rms_back(d_normed, unit, scale, gain_ref[...])
+    d_low = d_attended.astype(jnp.bfloat16)
+    datt_ref[...] = d_attended
+    low_ref[...] = d_low
+    dmix_ref[...] = matmul_nn(d_low, wo_ref[...]).astype(jnp.bfloat16)
+
+    @pl.when(pl.program_id(0) == 0)
+    def _():
+        dgain_ref[...] = d_gain
+
+    @pl.when(pl.program_id(0) != 0)
+    def _():
+        dgain_ref[...] += d_gain
+
+
+def backward_body(
+    q_ref,
+    k_ref,
+    v_ref,
+    e_ref,
+    dmix_ref,
+    mixed_ref,
+    inv_ref,
+    dq_ref,
+    dk_ref,
+    dv_ref,
+    strip_ref,
+    table_ref,
+    dkt_ref,
+    dvt_ref,
+):
+    seq_len = k_ref.shape[0]
+    rows = table_ref.shape[1]
+    low_masks = head_masks(jnp.bfloat16)
+    masks = head_masks(jnp.float32)
+    keys = k_ref[...]
+    values = v_ref[...]
+    keys_h = tuple(keys * low_masks[h] for h in range(2))
+    table_ref[...] = jnp.zeros_like(table_ref)
+    for block in range(seq_len // rows):
+        at = slice(block * rows, (block + 1) * rows)
+        queries = q_ref[at, :]
+        scaled = (dmix_ref[at, :].astype(jnp.float32) * inv_ref[at, :]).astype(jnp.bfloat16)
+        product = scaled.astype(jnp.float32) * mixed_ref[at, :]
+        d_query = jnp.zeros((rows, LANES), jnp.float32)
+        d_key = jnp.zeros((LANES, seq_len), jnp.float32)
+        d_value = jnp.zeros((LANES, seq_len), jnp.float32)
+        for head in range(2):
+            scaled_h = scaled * low_masks[head]
+            delta = jnp.sum(product * masks[head], axis=-1, keepdims=True)
+            weights = e_ref[head, at, :]
+            d_scores = weights.astype(jnp.float32) * (matmul_nt(scaled_h, values) - delta)
+            d_low = d_scores.astype(jnp.bfloat16)
+            window = slice(seq_len - block * rows, 2 * seq_len - block * rows)
+            table_ref[head, :, window] += d_scores
+            d_query = d_query + matmul_nn(d_low, keys_h[head])
+            d_key = d_key + matmul_tn(queries * low_masks[head], d_low)
+            d_value = d_value + matmul_tn(scaled_h, weights)
+        dq_ref[at, :] = d_query.astype(jnp.bfloat16)
+        if block == 0:
+            dkt_ref[...] = d_key
+            dvt_ref[...] = d_value
+        else:
+            dkt_ref[...] += d_key
+            dvt_ref[...] += d_value
+    dk_ref[...] = dkt_ref[...].T.astype(jnp.bfloat16)
+    dv_ref[...] = dvt_ref[...].T.astype(jnp.bfloat16)
+    width = 2 * seq_len
+    sub = lax.broadcasted_iota(jnp.int32, (8, 1), 0)
+    for head in range(2):
+        total = table_ref[head, 0:8, :]
+        for group in range(1, rows // 8):
+            part = table_ref[head, 8 * group : 8 * group + 8, :]
+            total = total + pltpu.roll(part, width - 8 * group, 1)
+        for bit in (1, 2, 4):
+            total = jnp.where((sub & bit) != 0, pltpu.roll(total, width - bit, 1), total)
+        strip_ref[0, head : head + 1, :] = jnp.sum(total, axis=0, keepdims=True)
+
+
+def spread_body(
+    me_ref,
+    x_ref,
+    dq_ref,
+    dk_ref,
+    dv_ref,
+    wq_ref,
+    wk_ref,
+    wv_ref,
+    send_ref,
+    own_ref,
+    dgain_ref,
+):
+    step = pl.program_id(0)
+    unit, _ = rms_parts(x_ref[...].astype(jnp.float32))
+    d_normed = (
+        matmul_nt(dq_ref[...], wq_ref[...])
+        + matmul_nt(dk_ref[...], wk_ref[...])
+        + matmul_nt(dv_ref[...], wv_ref[...])
+    )
+    d_gain = jnp.sum(d_normed * unit, axis=0, keepdims=True)
+
+    @pl.when(step == 0)
+    def _():
+        dgain_ref[...] = d_gain
+
+    @pl.when(step != 0)
+    def _():
+        dgain_ref[...] += d_gain
+
+    @pl.when(step < pl.num_programs(0) // 2)
+    def _():
+        send_ref[...] = d_normed.astype(jnp.bfloat16)
+
+    @pl.when(step >= pl.num_programs(0) // 2)
+    def _():
+        own_ref[...] = d_normed
+
+
+def finish_body(me_ref, x_ref, own_ref, other_ref, datt_ref, gain_ref, out_ref):
+    unit, scale = rms_parts(x_ref[...].astype(jnp.float32))
+    d_normed = own_ref[...] + other_ref[...].astype(jnp.float32)
+    out_ref[...] = (datt_ref[...] + rms_back(d_normed, unit, scale, gain_ref[...])).astype(
+        jnp.bfloat16
+    )
+
+
+def weight_grads(left, right, columns):
+    depth, height = left.shape
+    width = right.shape[1]
+    return call(
+        grads_body,
+        (width // columns,),
+        [whole((depth, height)), pl.BlockSpec((depth, columns), lambda i: (0, i))],
+        pl.BlockSpec((height, columns), lambda i: (0, i)),
+        shaped((height, width), jnp.bfloat16),
+        [pltpu.VMEM((height, depth), jnp.bfloat16)],
+        flops=2 * depth * height * width,
+        moved=2 * (depth * height + depth * width + height * width),
+    )(left, right)
+
+
+def on_core_pair(
+    tokens,
+    cotangent,
+    gain_attn,
+    w_query,
+    w_key,
+    w_value,
+    w_out,
+    rel_table,
+    buckets,
+    gain_ffn,
+    w_gate,
+    w_up,
+    w_down,
+):
+    low = jnp.bfloat16
+    high = jnp.float32
+    own_rows, features = tokens.shape
+    seq_len = 2 * own_rows
+    width = w_query.shape[1]
+    units = w_gate.shape[1]
+    pairs = width // LANES
+    bucket_count = rel_table.shape[0]
+    me = lax.axis_index("mp")
+    me_arg = me.astype(jnp.int32).reshape(1)
+    rows = MXU_ROWS
+    steps = seq_len // rows
+    half_steps = steps // 2
+    swap = [(0, 1), (1, 0)]
+
+    def swapped(array):
+        return lax.ppermute(array, "mp", swap)
+
+    def in_order(array):
+        other = swapped(array)
+        first = jnp.where(me == 0, array, other)
+        second = jnp.where(me == 0, other, array)
+        return jnp.concatenate([first, second], axis=0)
+
+    parts = (w_gate, w_up, w_down.T, w_query, w_key, w_value, w_out.T)
+    gathered = lax.all_gather(jnp.concatenate(parts, axis=1), "dp", axis=0, tiled=True)
+    at_query = 3 * units // width
+
+    def unit_block(index):
+        return pl.BlockSpec((features, units), lambda *_: (0, index))
+
+    def head_block(index):
+        return pl.BlockSpec((features, width), lambda *_: (0, at_query + index))
+
+    x_all = in_order(tokens)
+    g_all = in_order(cotangent)
+    gain_a = gain_attn.reshape(1, features)
+    gain_f = gain_ffn.reshape(1, features)
+
+    one_hot = (buckets[:, None] == jnp.arange(bucket_count, dtype=jnp.int32)[None, :]).astype(high)
+    one_hot = jnp.pad(one_hot, ((1, 0), (0, 0)))
+    head_count = rel_table.shape[1]
+    local_heads = head_count // 2
+    my_table = lax.dynamic_slice_in_dim(rel_table, me * local_heads, local_heads, 1)
+    strip = lax.dot_general(my_table, one_hot, (((0,), (1,)), ((), ())), precision=precise)
+    strip = strip.reshape(pairs, 2, 2 * seq_len)
+
+    def row_block(columns):
+        return pl.BlockSpec((rows, columns), lambda i, *_: (i, 0))
+
+    normed_a, queries, keys, values = call(
+        project_body,
+        (steps,),
+        [row_block(features), whole((1, features)), head_block(0), head_block(1), head_block(2)],
+        [row_block(features)] + [row_block(width)] * 3,
+        [shaped((seq_len, features), low)] + [shaped((seq_len, width), low)] * 3,
+        flops=6 * seq_len * features * width,
+        moved=4 * seq_len * features + 6 * (features + seq_len) * width,
+    )(x_all, gain_a, gathered, gathered, gathered)
+
+    pair_block = pl.BlockSpec((seq_len, LANES), lambda p: (0, p))
+    e_block = pl.BlockSpec((2, seq_len, seq_len), lambda p: (p, 0, 0))
+    strip_block = pl.BlockSpec((1, 2, 2 * seq_len), lambda p: (p, 0, 0))
+    table_scratch = pltpu.VMEM((2, rows, 2 * seq_len), high)
+    attend_flops = 8 * 2 * pairs * seq_len * seq_len * LANES
+    e_bytes = 4 * pairs * seq_len * seq_len
+    weights_e, mixed, inverse, part = call(
+        attend_body,
+        (pairs,),
+        [
+            pair_block,
+            pair_block,
+            pair_block,
+            strip_block,
+            pl.BlockSpec((features, LANES), lambda p: (0, (at_query + 3) * pairs + p)),
+        ],
+        [e_block, pair_block, pair_block, whole((seq_len, features))],
+        [
+            shaped((2 * pairs, seq_len, seq_len), low),
+            shaped((seq_len, width), high),
+            shaped((seq_len, width), high),
+            shaped((seq_len, features), low),
+        ],
+        [table_scratch, pltpu.VMEM((seq_len, features), high)],
+        flops=attend_flops,
+        moved=e_bytes + 20 * seq_len * width,
+    )(queries, keys, values, strip, gathered)
+    part_other = swapped(part)
+
+    turned_row = lambda columns: pl.BlockSpec(
+        (rows, columns), lambda i, m: ((i + half_steps * (1 - m[0])) % steps, 0)
+    )
+    send_row = pl.BlockSpec((rows, features), lambda i, m: (jnp.minimum(i, half_steps - 1), 0))
+    keep_row = pl.BlockSpec((rows, features), lambda i, m: (jnp.maximum(i - half_steps, 0), 0))
+    normed_f, hidden, d_gate, d_up, dn_part, out_send, out_own = call(
+        feed_body,
+        (steps,),
+        [turned_row(features)] * 4
+        + [whole((1, features)), unit_block(0), unit_block(1), unit_block(2)],
+        [turned_row(features)]
+        + [turned_row(units)] * 3
+        + [turned_row(features), send_row, keep_row],
+        [
+            shaped((seq_len, features), low),
+            shaped((seq_len, units), low),
+            shaped((seq_len, units), low),
+            shaped((seq_len, units), low),
+            shaped((seq_len, features), low),
+            shaped((own_rows, features), low),
+            shaped((own_rows, features), high),
+        ],
+        prefetch=1,
+        flops=12 * seq_len * features * units,
+        moved=6 * features * units + 16 * seq_len * features + 6 * seq_len * units,
+    )(me_arg, x_all, part, part_other, g_all, gain_f, gathered, gathered, gathered)
+    dn_other = swapped(dn_part)
+    out_other = swapped(out_send)
+    output = (out_own + out_other.astype(high)).astype(low)
+
+    d_gate_w = weight_grads(normed_f, d_gate, units // 2)
+    d_up_w = weight_grads(normed_f, d_up, units // 2)
+    d_down_w = weight_grads(g_all, hidden, units // 2)
+
+    d_attended, d_low, d_mixed, d_gain_f = call(
+        turn_body,
+        (steps,),
+        [row_block(features)] * 6 + [whole((1, features)), head_block(3)],
+        [row_block(features), row_block(features), row_block(width), whole((1, features))],
+        [
+            shaped((seq_len, features), high),
+            shaped((seq_len, features), low),
+            shaped((seq_len, width), low),
+            shaped((1, features), high),
+        ],
+        flops=2 * seq_len * features * width,
+        moved=20 * seq_len * features + 2 * seq_len * width,
+    )(x_all, part, part_other, g_all, dn_part, dn_other, gain_f, gathered)
+
+    d_query, d_key, d_value, d_strip = call(
+        backward_body,
+        (pairs,),
+        [pair_block, pair_block, pair_block, e_block, pair_block, pair_block, pair_block],
+        [pair_block, pair_block, pair_block, strip_block],
+        [shaped((seq_len, width), low)] * 3 + [shaped((pairs, 2, 2 * seq_len), high)],
+        [table_scratch, pltpu.VMEM((LANES, seq_len), high), pltpu.VMEM((LANES, seq_len), high)],
+        flops=2 * attend_flops,
+        moved=e_bytes + 22 * seq_len * width,
+    )(queries, keys, values, weights_e, d_mixed, mixed, inverse)
+    d_out_w = weight_grads(d_low, mixed.astype(low), width)
+
+    dna_send, dna_own, d_gain_a = call(
+        spread_body,
+        (steps,),
+        [turned_row(features)] + [turned_row(width)] * 3 + [head_block(0), head_block(1), head_block(2)],
+        [send_row, keep_row, whole((1, features))],
+        [
+            shaped((own_rows, features), low),
+            shaped((own_rows, features), high),
+            shaped((1, features), high),
+        ],
+        prefetch=1,
+        flops=6 * seq_len * features * width,
+        moved=8 * seq_len * features + 6 * seq_len * width,
+    )(me_arg, x_all, d_query, d_key, d_value, gathered, gathered, gathered)
+    dna_other = swapped(dna_send)
+    d_query_w = weight_grads(normed_a, d_query, width)
+    d_key_w = weight_grads(normed_a, d_key, width)
+    d_value_w = weight_grads(normed_a, d_value, width)
+
+    grads = jnp.concatenate(
+        [d_gate_w, d_up_w, d_down_w, d_query_w, d_key_w, d_value_w, d_out_w], axis=1
+    )
+    grads = lax.psum_scatter(grads, "dp", scatter_dimension=0, tiled=True).astype(high)
+
+    d_tokens = call(
+        finish_body,
+        (half_steps,),
+        [
+            row_block(features),
+            row_block(features),
+            row_block(features),
+            pl.BlockSpec((rows, features), lambda i, m: (i + m[0] * half_steps, 0)),
+            whole((1, features)),
+        ],
+        row_block(features),
+        shaped((own_rows, features), low),
+        prefetch=1,
+        flops=0,
+        moved=14 * own_rows * features,
+    )(me_arg, tokens, dna_own, dna_other, d_attended, gain_a)
+
+    d_bias = d_strip.reshape(local_heads, 2 * seq_len)
+    my_d_table = lax.dot_general(one_hot, d_bias, (((0,), (1,)), ((), ())), precision=precise)
+    d_table = lax.dynamic_update_slice_in_dim(
+        jnp.zeros_like(rel_table), my_d_table, me * local_heads, 1
+    )
+    small = lax.psum((d_gain_a, 0.5 * d_gain_f, d_table), ("dp", "mp"))
+    head_grads = [
+        grads[:, 3 * units + i * width : 3 * units + (i + 1) * width] for i in range(4)
+    ]
+    return (
+        output,
+        d_tokens,
+        small[0].reshape(features),
+        head_grads[0],
+        head_grads[1],
+        head_grads[2],
+        head_grads[3].T,
+        small[2],
+        small[1].reshape(features),
+        grads[:, :units],
+        grads[:, units : 2 * units],
+        grads[:, 2 * units : 3 * units].T,
+    )
+
+
 def solution(mesh):
     placed = (
         P(("dp", "mp"), None),
@@ -337,8 +885,9 @@
         P("dp", "mp"),
         P("mp", "dp"),
     )
+    body = on_device if mesh.shape["mp"] != 2 else on_core_pair
     return jax.shard_map(
-        on_device,
+        body,
         mesh=mesh,
         in_specs=placed,
         out_specs=(

time: 2540 us -> 397 us (0.16)
  local copies, waits for them, and re-layouts: 1120 us -> 27.2 us
  waiting for transfers between devices: 1070 us -> 194 us
  matrix products: 158 us -> 1.11 us
  Pallas kernels: 0 us -> 111 us
  loops' own time: 68.7 us -> 0 us
  other arithmetic: 42.6 us -> 8.51 us
    reduce_scatter x10 -> x1, waiting for transfers between devices: 629 us -> 95.9 us  [on_core_pair(): lax.psum_scatter(grads, 'dp', scatter_dimension=0, tiled=True).astype(high)]
    reshape x13 -> x4, local copies, waits for them, and re-layouts: 368 us -> 2.55 us  [the longest x1 1.27 us: on_core_pair(): gain_a = gain_attn.reshape(1, features)]
    another operation x12 -> x0, local copies, waits for them, and re-layouts: 301 us -> none  [make_bias(): tiled = jnp.tile(strip, (1, row_count + 1))]
    slice x12 -> x2, local copies, waits for them, and re-layouts: 217 us -> 2.27 us  [the longest x1 1.49 us: on_core_pair(): grads[:, 3 * units + i * width:3 * units + (i + 1) * width]]
    all_gather x11 -> x1, waiting for transfers between devices: 297 us -> 96.1 us  [on_core_pair(): lax.all_gather(jnp.concatenate(parts, axis=1), 'dp', axis=0, tiled=True)]
    dot_general x37 -> x2, matrix products: 158 us -> 1.11 us  [the longest x1 0.64 us: on_core_pair(): lax.dot_general(my_table, one_hot, (((0,), (1,)), ((), ())), precision=pr...]
    while x36 -> x0, local copies, waits for them, and re-layouts: 148 us -> none
    unnamed x31 -> x2, waiting for transfers between devices: 143 us -> 0.03 us
  transfers between devices with their start and end apart: 26 -> 8, of which waited for: 20 -> 3; matrix products, arithmetic and copies ran while one was open for 51% -> 4% of each run, Pallas kernels for 0% -> 7%
where the time goes in v1:
time: 397 us; the launch traced here: 396 us
  waiting for transfers between devices  194 us (49%)
  Pallas kernels  111 us (28%)
  blocking collectives  39 us (10%)
  local copies, waits for them, and re-layouts  27.2 us (7%)
  between operations  14.2 us (4%)
  other arithmetic  8.51 us (2%)
    all_gather x1, waiting for transfers between devices, on_core_pair(): lax.all_gather(jnp.concatenate(parts, axis=1), 'dp', axis=0, tiled=True)  96.1 us
    reduce_scatter x1, waiting for transfers between devices, on_core_pair(): lax.psum_scatter(grads, 'dp', scatter_dimension=0, tiled=True).astype(high)  95.9 us
    psum x1, blocking collectives, on_core_pair(): small = lax.psum((d_gain_a, 0.5 * d_gain_f, d_table), ('dp', 'mp'))  39 us
    pallas_call x7, Pallas kernels, weight_grads(): call(grads_body, (width // columns,), [whole((depth, height)), pl.BlockSp...  29.4 us
    pallas_call x1, Pallas kernels, on_core_pair(): call(attend_body, (pairs,), [pair_block, pair_block, pair_block, strip_bl...  21.9 us
    unnamed x60, local copies, waits for them, and re-layouts  19.3 us
    pallas_call x1, Pallas kernels, on_core_pair(): call(feed_body, (steps,), [turned_row(features)] * 4 + [whole((1, feature...  17.9 us
    pallas_call x1, Pallas kernels, on_core_pair(): call(backward_body, (pairs,), [pair_block, pair_block, pair_block, e_bloc...  16.4 us
  transfers between devices with their start and end apart: 8, of which 3 were waited for; matrix products, arithmetic and copies ran while one was open for 4% of the time, Pallas kernels for 7%

profile of v1, /device:TPU:0, one launch (start us, length us, event | category | flops | bytes accessed | tf_op | source)
XLA Modules:
  0.0 396.2 jit_solution(5853851440994337743)
XLA Ops:
  19.1 1.7 broadcast_select_fusion.1
  22.1 96.1 %all-gather.2.cloned.1.call-done.wq_ref.wk_ref.wv_ref.wo_ref.wg_ref.wu_ref.wd_ref = bf16[768,4608]{1,0:T(8,128)(2,1)} async-done(((bf16[48,4608]{1,0:T(8,128)(2,1)}), bf16[768,4608]{1,0:T(8,128)(2,1)}) %all-gather.2.cloned.1.call-update) | async-done | bytes 7077904 | tf_op jit(solution)/shard_map/all_gather | solution.py:681
  118.2 6.0 %shard_map.220 = (bf16[1024,768]{1,0:T(8,128)(2,1)}, bf16[1024,384]{1,0:T(8,128)(2,1)}, bf16[1024,384]{1,0:T(8,128)(2,1)}, bf16[1024,384]{1,0:T(8,128)(2,1)}) custom-call(bf16[1024,768]{1,0:T(8,128)(2,1)} %pad_maximum_fusion.x_ref, f32[1,768]{1,0:T(1,128)} %reshape.47.gain_ref, ...), custom_call_target="tpu_custom_call" | custom-call | flops 1811939328 | bytes 7274496 | tf_op jit(solution)/shard_map/pallas_call | solution.py:706
  124.2 21.9 %shard_map.221 = (bf16[6,1024,1024]{2,1,0:T(8,128)(2,1)}, f32[1024,384]{1,0:T(8,128)}, f32[1024,384]{1,0:T(8,128)}, bf16[1024,768]{1,0:T(8,128)(2,1)}) custom-call(bf16[1024,384]{1,0:T(8,128)(2,1)} %get-tuple-element.38.q_ref, bf16[1024,384]{1,0:T(8,128)(2,1)} %get-tuple-element.39.k_ref, bf16[1024,384]{1,0:T(8,128)(2,1)} %get-tuple-element.40.v_ref, ...), custom_call_target="tpu_custom_call" | custom-call | flops 6442450944 | bytes 20447232 | tf_op jit(solution)/shard_map/pallas_call | solution.py:722
  146.7 1.3 pad_maximum_fusion.1.g_ref.left_ref
  148.0 1.7 collective-permute-done.1.r_ref
  150.9 17.9 %shard_map.222 = (bf16[1024,768]{1,0:T(8,128)(2,1)}, bf16[1024,1024]{1,0:T(8,128)(2,1)}, bf16[1024,1024]{1,0:T(8,128)(2,1)}, bf16[1024,1024]{1,0:T(8,128)(2,1)},...) custom-call(s32[1]{0:T(128)} %bitcast.me_ref, bf16[1024,768]{1,0:T(8,128)(2,1)} %pad_maximum_fusion.x_ref, ...), custom_call_target="tpu_custom_call" | custom-call | flops 9663676416 | bytes 23592960 | tf_op jit(solution)/shard_map/pallas_call | solution.py:750
  170.2 5.1 %shard_map.227 = bf16[768,1024]{1,0:T(8,128)(2,1)} custom-call(bf16[1024,768]{1,0:T(8,128)(2,1)} %get-tuple-element.56.left_ref, bf16[1024,1024]{1,0:T(8,128)(2,1)} %get-tuple-element.57.right_ref), custom_call_target="tpu_custom_call" | custom-call | flops 1610612736 | bytes 5242880 | tf_op jit(solution)/shard_map/pallas_call | solution.py:629
  175.4 5.1 %shard_map.228 = bf16[768,1024]{1,0:T(8,128)(2,1)} custom-call(bf16[1024,768]{1,0:T(8,128)(2,1)} %get-tuple-element.56.left_ref, bf16[1024,1024]{1,0:T(8,128)(2,1)} %get-tuple-element.58.right_ref), custom_call_target="tpu_custom_call" | custom-call | flops 1610612736 | bytes 5242880 | tf_op jit(solution)/shard_map/pallas_call | solution.py:629
  180.5 5.3 %shard_map.229 = bf16[768,1024]{1,0:T(8,128)(2,1)} custom-call(bf16[1024,768]{1,0:T(8,128)(2,1)} %pad_maximum_fusion.1.g_ref.left_ref, bf16[1024,1024]{1,0:T(8,128)(2,1)} %get-tuple-element.59.right_ref), custom_call_target="tpu_custom_call" | custom-call | flops 1610612736 | bytes 5242880 | tf_op jit(solution)/shard_map/pallas_call | solution.py:629
  185.8 1.3 constant_dynamic-update-slice_fusion.11
  187.7 1.3 constant_dynamic-update-slice_fusion.10
  189.7 1.3 constant_dynamic-update-slice_fusion.9
  192.2 8.4 %shard_map.223 = (f32[1024,768]{1,0:T(8,128)}, bf16[1024,768]{1,0:T(8,128)(2,1)}, bf16[1024,384]{1,0:T(8,128)(2,1)}, f32[1,768]{1,0:T(1,128)}) custom-call(bf16[1024,768]{1,0:T(8,128)(2,1)} %pad_maximum_fusion.x_ref, bf16[1024,768]{1,0:T(8,128)(2,1)} %get-tuple-element.41.p_ref, bf16[1024,768]{1,0:T(8,128)(2,1)} %copy-done.8, ...), custom_call_target="tpu_custom_call" | custom-call | flops 603979776 | bytes 16515072 | tf_op jit(solution)/shard_map/pallas_call | solution.py:779
  200.5 16.4 %shard_map.224 = (bf16[1024,384]{1,0:T(8,128)(2,1)}, bf16[1024,384]{1,0:T(8,128)(2,1)}, bf16[1024,384]{1,0:T(8,128)(2,1)}, f32[3,2,2048]{2,1,0:T(2,128)}) custom-call(bf16[1024,384]{1,0:T(8,128)(2,1)} %get-tuple-element.38.q_ref, bf16[1024,384]{1,0:T(8,128)(2,1)} %get-tuple-element.39.k_ref, bf16[1024,384]{1,0:T(8,128)(2,1)} %get-tuple-element.40.v_ref, ...), custom_call_target="tpu_custom_call" | custom-call | flops 12884901888 | bytes 21233664 | tf_op jit(solution)/shard_map/pallas_call | solution.py:794
  216.9 3.4 shard_map.230
  220.3 3.4 shard_map.231
  223.7 3.5 shard_map.232
  227.2 3.6 shard_map.233
  235.9 7.2 %shard_map.225 = (bf16[512,768]{1,0:T(8,128)(2,1)}, f32[512,768]{1,0:T(8,128)}, f32[1,768]{1,0:T(1,128)}) custom-call(s32[1]{0:T(128)} %bitcast.me_ref, bf16[1024,768]{1,0:T(8,128)(2,1)} %pad_maximum_fusion.x_ref, bf16[1024,384]{1,0:T(8,128)(2,1)} %get-tuple-element.49.dq_ref.right_ref, bf16[1024,384]{1,0:T(8,128)(2,1)} %get-tuple-element.50.dk_ref.right_ref, ...), custom_call_target="tpu_custom_call" | custom-call | flops 1811939328 | bytes 8650752 | tf_op jit(solution)/shard_map/pallas_call | solution.py:806
  245.3 39.0 %all-reduce.1 = (f32[768]{0:T(1024)}, f32[32,12]{0,1:T(8,128)}, f32[768]{0:T(1024)}) all-reduce(f32[768]{0:T(1024)S(1)} %reduce, f32[32,12]{0,1:T(8,128)S(1)} %dynamic_update_slice.3, f32[768]{0:T(1024)S(1)} %multiply_reduce_fusion), channel_id=1, replica_groups=mesh['dp'=16,'mp'=2] {'dp','mp'}, use_global_device_ids=true, to_apply=%region_0.1 | all-reduce | flops 1920 | bytes 15360 | tf_op jit(solution)/shard_map/psum | solution.py:852
  285.2 3.5 shard_map.226
  288.7 95.9 %reduce-scatter.2.cloned.1.call-done = bf16[48,4608]{1,0:T(8,128)(2,1)} async-done(((bf16[768,4608]{1,0:T(8,128)(2,1)}), bf16[48,4608]{1,0:T(8,128)(2,1)}) %reduce-scatter.2.cloned.1.call-update) | async-done | bytes 442384 | tf_op jit(solution)/shard_map/reduce_scatter | solution.py:828
  387.1 1.5 fusion.9
  (92 shorter events, 30.1 us)
Async XLA Ops:
  7.2 9.8 %copy-start = (f32[32,12]{0,1:T(8,128)S(1)}, f32[32,12]{0,1:T(8,128)}, u32[]{:S(2)}) copy-start(f32[32,12]{0,1:T(8,128)} %param.20) | copy-start | bytes 4612
  7.2 11.9 %copy-start.15 = (bf16[512,768]{1,0:T(8,128)(2,1)S(1)}, bf16[512,768]{1,0:T(8,128)(2,1)}, u32[]{:S(2)}) copy-start(bf16[512,768]{1,0:T(8,128)(2,1)} %param.14) | copy-start | bytes 2359300
  7.2 11.9 %copy-start.2 = (bf16[512,768]{1,0:T(8,128)(2,1)S(1)}, bf16[512,768]{1,0:T(8,128)(2,1)}, u32[]{:S(2)}) copy-start(bf16[512,768]{1,0:T(8,128)(2,1)} %x_ref.1) | copy-start | bytes 2359300
  7.2 110.9 %all-gather.2.cloned.1.call-start = ((), (), s32[]{:S(2)}) async-start(), calls=%async_computation.1 | async-start | bytes 7520256 | tf_op jit(solution)/shard_map/all_gather | solution.py:681
  14.0 370.6 %reduce-scatter.2.cloned.1.call-start = ((), (), s32[]{:S(2)}) async-start(), calls=%async_computation.2 | async-start | bytes 7520256 | tf_op jit(solution)/shard_map/reduce_scatter | solution.py:828
  14.0 4.2 %collective-permute-start.2 = (bf16[512,768]{1,0:T(8,128)(2,1)}, bf16[512,768]{1,0:T(8,128)(2,1)S(1)}, u32[]{:S(2)}, u32[]{:S(2)}) collective-permute-start(bf16[512,768]{1,0:T(8,128)(2,1)} %param.14), channel_id=1, source_target_pairs={{0,1},{1,0},{2,3},{3,2},{4,5},{5,4},{6,7},{7,6},{8,9},{9,8},{10,11... | collective-permute-start | bytes 2359304 | tf_op jit(solution)/shard_map/ppermute | solution.py:672
  14.5 4.6 %collective-permute-start = (bf16[512,768]{1,0:T(8,128)(2,1)}, bf16[512,768]{1,0:T(8,128)(2,1)}, u32[]{:S(2)}, u32[]{:S(2)}) collective-permute-start(bf16[512,768]{1,0:T(8,128)(2,1)} %x_ref.1), channel_id=1, source_target_pairs={{0,1},{1,0},{2,3},{3,2},{4,5},{5,4},{6,7},{7,6},{8,9},{9,8},{10,11... | collective-permute-start | bytes 2359304 | tf_op jit(solution)/shard_map/ppermute | solution.py:672
  124.2 22.0 %copy-start.20 = (f32[768]{0:T(1024)S(1)}, f32[768]{0:T(1024)}, u32[]{:S(2)}) copy-start(f32[768]{0:T(1024)} %param.22) | copy-start | bytes 9220
  146.1 3.7 collective-permute-start.1
  150.9 18.3 %copy-start.11 = (f32[1024,384]{1,0:T(8,128)S(1)}, f32[1024,384]{1,0:T(8,128)}, u32[]{:S(2)}) copy-start(f32[1024,384]{1,0:T(8,128)} %get-tuple-element.47.mixed_ref) | copy-start | bytes 4718596
  168.9 22.1 %collective-permute-start.4 = (bf16[1024,768]{1,0:T(8,128)(2,1)}, bf16[1024,768]{1,0:T(8,128)(2,1)S(1)}, u32[]{:S(2)}, u32[]{:S(2)}) collective-permute-start(bf16[1024,768]{1,0:T(8,128)(2,1)} %get-tuple-element.45.a_ref), channel_id=1, source_target_pairs={{0,1},{1,0},{2,3},{3,2},{4,5},{5,4},{6,7},{7,6},{8,9},{9,8},{10,11... | collective-permute-start | bytes 4718600 | tf_op jit(solution)/shard_map/ppermute | solution.py:672
  180.5 5.3 %copy-start.12 = (bf16[768,1024]{1,0:T(8,128)(2,1)S(1)}, bf16[768,1024]{1,0:T(8,128)(2,1)}, u32[]{:S(2)}) copy-start(bf16[768,1024]{1,0:T(8,128)(2,1)} %shard_map.227) | copy-start | bytes 4718596
  185.7 2.0 copy-start.13
  187.7 2.0 copy-start.14
  227.2 3.6 copy-start.7
  227.2 4.5 %copy-start.6 = (bf16[768,384]{1,0:T(8,128)(2,1)S(1)}, bf16[768,384]{1,0:T(8,128)(2,1)}, u32[]{:S(2)}) copy-start(bf16[768,384]{1,0:T(8,128)(2,1)} %shard_map.231) | copy-start | bytes 1769476
  227.2 5.5 %copy-start.5 = (bf16[768,384]{1,0:T(8,128)(2,1)S(1)}, bf16[768,384]{1,0:T(8,128)(2,1)}, u32[]{:S(2)}) copy-start(bf16[768,384]{1,0:T(8,128)(2,1)} %shard_map.232) | copy-start | bytes 1769476
  230.8 2.9 copy-start.4
  235.7 7.8 %copy-start.10 = (f32[512,768]{1,0:T(8,128)S(1)}, f32[512,768]{1,0:T(8,128)}, u32[]{:S(2)}) copy-start(f32[512,768]{1,0:T(8,128)} %get-tuple-element.42) | copy-start | bytes 4718596
  235.7 7.8 %collective-permute-start.3 = (bf16[512,768]{1,0:T(8,128)(2,1)S(1)}, bf16[512,768]{1,0:T(8,128)(2,1)S(1)}, u32[]{:S(2)}, u32[]{:S(2)}) collective-permute-start(bf16[512,768]{1,0:T(8,128)(2,1)S(1)} %copy-done.23), channel_id=1, source_target_pairs={{0,1},{1,0},{2,3},{3,2},{4,5},{5,4},{6,7},{7,6},{8,9},{9,8},{10,11... | collective-permute-start | bytes 2359304 | tf_op jit(solution)/shard_map/ppermute | solution.py:672
  243.2 2.0 copy-start.21
  243.2 41.1 %collective-permute-start.5 = (bf16[512,768]{1,0:T(8,128)(2,1)}, bf16[512,768]{1,0:T(8,128)(2,1)S(1)}, u32[]{:S(2)}, u32[]{:S(2)}) collective-permute-start(bf16[512,768]{1,0:T(8,128)(2,1)} %get-tuple-element.53), channel_id=1, source_target_pairs={{0,1},{1,0},{2,3},{3,2},{4,5},{5,4},{6,7},{7,6},{8,9},{9,8},{10,11... | collective-permute-start | bytes 2359304 | tf_op jit(solution)/shard_map/ppermute | solution.py:672
  285.2 104.2 %copy-start.1 = (f32[32,12]{0,1:T(8,128)S(1)}, f32[32,12]{0,1:T(8,128)}, u32[]{:S(2)}) copy-start(f32[32,12]{0,1:T(8,128)} %param.20) | copy-start | bytes 4612
  384.6 4.0 %copy-start.3 = (bf16[48,4608]{1,0:T(8,128)(2,1)S(1)}, bf16[48,4608]{1,0:T(8,128)(2,1)}, u32[]{:S(2)}) copy-start(bf16[48,4608]{1,0:T(8,128)(2,1)} %reduce-scatter.2.cloned.1.call-done) | copy-start | bytes 1327108
  (8 other events, 8.7 us)
Sparse Core Ops, SparseCore 0:
  14.1 104.0 all-gather.1
  234.7 149.8 reduce-scatter.1

commit v2 on v0

--- a/solution.py
+++ b/solution.py
@@ -1,6 +1,10 @@
+import functools
+
 import jax
 import jax.numpy as jnp
 from jax import lax
+from jax.experimental import pallas as pl
+from jax.experimental.pallas import tpu as pltpu
 from jax.sharding import PartitionSpec as P
 
 epsilon = 1e-06
@@ -321,6 +325,776 @@
     )
 
 
+MXU_ROWS = 256
+LANES = 128
+VMEM_LIMIT = 56 * 2**20
+PEAK_PER_MICRO = 1_153_500_000
+LOW = jnp.bfloat16
+HIGH = jnp.float32
+
+
+def call(
+    body, grid, in_specs, out_specs, out_shape, scratch=(), prefetch=0, micros=5, aliases=None
+):
+    return pl.pallas_call(
+        body,
+        grid_spec=pltpu.PrefetchScalarGridSpec(
+            num_scalar_prefetch=prefetch,
+            grid=grid,
+            in_specs=in_specs,
+            out_specs=out_specs,
+            scratch_shapes=list(scratch),
+        ),
+        out_shape=out_shape,
+        input_output_aliases=aliases or {},
+        compiler_params=pltpu.CompilerParams(vmem_limit_bytes=VMEM_LIMIT),
+        cost_estimate=pl.CostEstimate(
+            flops=int(micros * PEAK_PER_MICRO), bytes_accessed=0, transcendentals=0
+        ),
+    )
+
+
+def shaped(shape, dtype):
+    return jax.ShapeDtypeStruct(shape, dtype)
+
+
+def whole(shape):
+    return pl.BlockSpec(shape, lambda *_: (0,) * len(shape), pipeline_mode=pl.Buffered(1))
+
+
+def result(shape):
+    return pl.BlockSpec(shape, lambda *_: (0,) * len(shape))
+
+
+def together(*arrays):
+    return lax.optimization_barrier(arrays)
+
+
+def ring_shift(steps, count):
+    return [(i, (i + steps) % count) for i in range(count)]
+
+
+def flip(bit, count):
+    return [(i, i ^ bit) for i in range(count)]
+
+
+def over_x(array):
+    return lax.ppermute(array, "dp", flip(1, lax.axis_size("dp")))
+
+
+def over_y(array):
+    return lax.ppermute(array, "dp", flip(2, lax.axis_size("dp")))
+
+
+def over_far(array, steps):
+    return lax.ppermute(array, "dp", ring_shift(4 * steps, lax.axis_size("dp")))
+
+
+def dp_place():
+    index = lax.axis_index("dp")
+    return (index // 4, (index // 2) % 2, index % 2)
+
+
+def in_bit_order(own, other, bit, axis):
+    return jnp.stack([jnp.where(bit == 0, own, other), jnp.where(bit == 0, other, own)], axis=axis)
+
+
+def far_pieces(shard):
+    return [over_far(shard, k) for k in range(1, lax.axis_size("dp") // 4)]
+
+
+def far_stack(shard, pieces):
+    far = len(pieces) + 1
+    place = dp_place()[0]
+    stacked = jnp.zeros((far,) + shard.shape, shard.dtype)
+    for k, piece in enumerate([shard] + pieces):
+        stacked = lax.dynamic_update_slice(stacked, piece[None], ((place - k) % far, 0, 0))
+    return stacked
+
+
+def at_bit(array, bit, axis):
+    return lax.dynamic_index_in_dim(array, bit, axis, False)
+
+
+def add_low(left, right):
+    return (left.astype(HIGH) + right.astype(HIGH)).astype(LOW)
+
+
+def sum_all(vector):
+    count = lax.axis_size("dp")
+    vector = vector + lax.ppermute(vector, "mp", [(0, 1), (1, 0)])
+    vector = sum(far_pieces(vector), vector)
+    return sum((lax.ppermute(vector, "dp", flip(k, count)) for k in range(1, 4)), vector)
+
+
+def head_masks(dtype):
+    lane = lax.broadcasted_iota(jnp.int32, (1, LANES), 1)
+    first = (lane < LANES // 2).astype(HIGH)
+    return (first.astype(dtype), (1.0 - first).astype(dtype))
+
+
+def put_weights(full_ref, own_ref, other_ref, axis, bit):
+    if axis == 1:
+        full_ref[:, bit] = own_ref[...]
+        full_ref[:, 1 - bit] = other_ref[...]
+    else:
+        full_ref[:, :, bit] = own_ref[...]
+        full_ref[:, :, 1 - bit] = other_ref[...]
+
+
+def matrix(full_ref, start, columns):
+    part = full_ref[:, :, :, :, start : start + columns]
+    return part.reshape(-1, columns)
+
+
+def project_body(
+    place_ref,
+    x_ref,
+    gain_ref,
+    qk_own_ref,
+    qk_other_ref,
+    vo_own_ref,
+    vo_other_ref,
+    turned_ref,
+    q_ref,
+    k_ref,
+    v_ref,
+    qkv_ref,
+    wo_ref,
+    qk_ref,
+    vo_ref,
+):
+    width = q_ref.shape[1]
+
+    @pl.when(pl.program_id(0) == 0)
+    def _():
+        put_weights(qk_ref, qk_own_ref, qk_other_ref, 2, place_ref[1])
+        put_weights(vo_ref, vo_own_ref, vo_other_ref, 1, place_ref[0])
+        qkv_ref[:, : 2 * width] = matrix(qk_ref, 0, 2 * width)
+        qkv_ref[:, 2 * width :] = matrix(vo_ref, 0, width)
+        wo_ref[...] = matrix(vo_ref, width, width)
+
+    unit, _ = rms_parts(x_ref[...].astype(HIGH))
+    normed = (unit * gain_ref[...]).astype(LOW)
+    turned_ref[...] = normed.T
+    q_ref[...] = matmul_nn(normed, qkv_ref[:, :width]).astype(LOW)
+    k_ref[...] = matmul_nn(normed, qkv_ref[:, width : 2 * width]).astype(LOW)
+    v_ref[...] = matmul_nn(normed, qkv_ref[:, 2 * width :]).astype(LOW)
+
+
+def attend_body(
+    q_ref, k_ref, v_ref, strip_ref, wo_ref, e_ref, mixed_ref, low_ref, inv_ref, part_ref, table_ref, acc_ref
+):
+    pair = pl.program_id(0)
+    seq_len = k_ref.shape[0]
+    rows = table_ref.shape[1]
+    low_masks = head_masks(LOW)
+    masks = head_masks(HIGH)
+    own_lanes = tuple(mask > 0.5 for mask in masks)
+    for head in range(2):
+        row = jnp.broadcast_to(strip_ref[0, head : head + 1, :], (rows, 2 * seq_len))
+        table_ref[head] = pltpu.roll(row, 0, 1, stride=1, stride_axis=0)
+    keys = k_ref[...]
+    values = v_ref[...]
+    values_h = tuple(values * low_masks[h] + low_masks[1 - h] for h in range(2))
+
+    @pl.when(pair == 0)
+    def _():
+        acc_ref[...] = jnp.zeros_like(acc_ref)
+
+    for block in range(seq_len // rows):
+        at = slice(block * rows, (block + 1) * rows)
+        queries = q_ref[at, :]
+        mixed = jnp.zeros((rows, LANES), HIGH)
+        inverse = jnp.zeros((rows, LANES), HIGH)
+        for head in range(2):
+            scores = matmul_nt(queries * low_masks[head], keys)
+            scores = scores + table_ref[head, :, seq_len - block * rows : 2 * seq_len - block * rows]
+            top = jnp.max(scores, axis=-1, keepdims=True)
+            weights = jnp.exp(scores - top).astype(LOW)
+            e_ref[head, at, :] = weights
+            summed = matmul_nn(weights, values_h[head])
+            total = jnp.where(own_lanes[head], pltpu.roll(summed, LANES // 2, 1), 1.0)
+            inv = masks[head] / total
+            mixed = mixed + summed * inv
+            inverse = inverse + inv
+        mixed_ref[at, :] = mixed
+        low = mixed.astype(LOW)
+        low_ref[at, :] = low
+        inv_ref[at, :] = inverse
+        acc_ref[at, :] += matmul_nt(low, wo_ref[...])
+
+    @pl.when(pair == pl.num_programs(0) - 1)
+    def _():
+        part_ref[...] = acc_ref[...].astype(LOW)
+
+
+def feed_body(
+    place_ref,
+    x_ref,
+    p_ref,
+    r_ref,
+    g_ref,
+    gain_ref,
+    gu_own_ref,
+    gu_other_ref,
+    ud_own_ref,
+    ud_other_ref,
+    turned_ref,
+    g_turned_ref,
+    hidden_ref,
+    dgu_ref,
+    dn_ref,
+    send_ref,
+    own_ref,
+    gu_ref,
+    ud_ref,
+):
+    step = pl.program_id(0)
+
+    @pl.when(step == 0)
+    def _():
+        put_weights(gu_ref, gu_own_ref, gu_other_ref, 2, place_ref[1])
+        put_weights(ud_ref, ud_own_ref, ud_other_ref, 1, place_ref[0])
+
+    attended = x_ref[...].astype(HIGH) + (p_ref[...].astype(HIGH) + r_ref[...].astype(HIGH))
+    unit, _ = rms_parts(attended)
+    normed = (unit * gain_ref[...]).astype(LOW)
+    turned_ref[...] = normed.T
+    cotangent = g_ref[...]
+    g_turned_ref[...] = cotangent.T
+    root = 0.7978845608028654
+    columns = hidden_ref.shape[1] // 2
+    out = 0.0
+    d_normed = 0.0
+    for part in range(2):
+        w_gate = matrix(gu_ref, part * columns, columns)
+        w_up = matrix(ud_ref, 0, columns) if part else matrix(gu_ref, 2 * columns, columns)
+        w_down = matrix(ud_ref, (1 + part) * columns, columns)
+        gate = matmul_nn(normed, w_gate)
+        up = matmul_nn(normed, w_up)
+        d_hidden = matmul_nn(cotangent, w_down)
+        square = gate * gate
+        bend = jnp.tanh(gate * (root + (root * 0.044715) * square))
+        half = 0.5 + 0.5 * bend
+        gelu = gate * half
+        slope = half + (0.5 * gate) * (1.0 - bend * bend) * (root + (3 * root * 0.044715) * square)
+        hidden = (gelu * up).astype(LOW)
+        d_gate = (d_hidden * up * slope).astype(LOW)
+        d_up = (d_hidden * gelu).astype(LOW)
+        hidden_ref[:, part * columns : (part + 1) * columns] = hidden
+        dgu_ref[:, part * columns : (part + 1) * columns] = d_gate
+        dgu_ref[:, (2 + part) * columns : (3 + part) * columns] = d_up
+        d_normed = d_normed + matmul_nt(d_gate, w_gate) + matmul_nt(d_up, w_up)
+        out = out + matmul_nt(hidden, w_down)
+    dn_ref[...] = d_normed.astype(LOW)
+
+    @pl.when(step < pl.num_programs(0) // 2)
+    def _():
+        send_ref[...] = out.astype(LOW)
+
+    @pl.when(step >= pl.num_programs(0) // 2)
+    def _():
+        own_ref[...] = attended + out
+
+
+def grads_body(
+    first_count, axis, place_ref, left0_ref, left1_ref, right0_ref, right1_ref, own_ref, other_ref, all_ref
+):
+    step = pl.program_id(0)
+
+    def product(left_ref, right_ref):
+        grads = matmul_nn(left_ref[...], right_ref[...]).astype(LOW)
+        all_ref[...] = grads.reshape(all_ref.shape)
+
+    pl.when(step < first_count)(functools.partial(product, left0_ref, right0_ref))
+    pl.when(step >= first_count)(functools.partial(product, left1_ref, right1_ref))
+    bit = place_ref[axis - 1]
+    if axis == 1:
+        own_ref[...] = all_ref[:, bit]
+        other_ref[...] = all_ref[:, 1 - bit]
+    else:
+        own_ref[...] = all_ref[:, :, bit]
+        other_ref[...] = all_ref[:, :, 1 - bit]
+
+
+def turn_body(
+    place_ref,
+    x_ref,
+    p_ref,
+    r_ref,
+    g_ref,
+    a_ref,
+    b_ref,
+    gain_ref,
+    wo_ref,
+    datt_ref,
+    turned_ref,
+    dmix_ref,
+    dgain_ref,
+):
+    step = pl.program_id(0)
+    attended = x_ref[...].astype(HIGH) + (p_ref[...].astype(HIGH) + r_ref[...].astype(HIGH))
+    unit, scale = rms_parts(attended)
+    d_normed = a_ref[...].astype(HIGH) + b_ref[...].astype(HIGH)
+    d_gain = jnp.sum(d_normed * unit, axis=0, keepdims=True)
+    d_attended = g_ref[...].astype(HIGH) + rms_back(d_normed, unit, scale, gain_ref[...])
+    d_low = d_attended.astype(LOW)
+    turned_ref[...] = d_low.T
+    dmix_ref[...] = matmul_nn(d_low, wo_ref[...]).astype(LOW)
+
+    @pl.when(step == 0)
+    def _():
+        dgain_ref[...] = d_gain
+
+    @pl.when(step != 0)
+    def _():
+        dgain_ref[...] += d_gain
+
+    @pl.when(step >= pl.num_programs(0) // 2)
+    def _():
+        datt_ref[...] = d_attended
+
+
+def backward_body(
+    q_ref,
+    k_ref,
+    v_ref,
+    e_ref,
+    dmix_ref,
+    mixed_ref,
+    inv_ref,
+    dq_ref,
+    dk_ref,
+    dv_ref,
+    strip_ref,
+    table_ref,
+    dkt_ref,
+    dvt_ref,
+):
+    seq_len = k_ref.shape[0]
+    rows = table_ref.shape[1]
+    low_masks = head_masks(LOW)
+    masks = head_masks(HIGH)
+    keys = k_ref[...]
+    values = v_ref[...]
+    keys_h = tuple(keys * low_masks[h] for h in range(2))
+    table_ref[...] = jnp.zeros_like(table_ref)
+    for block in range(seq_len // rows):
+        at = slice(block * rows, (block + 1) * rows)
+        queries = q_ref[at, :]
+        scaled = (dmix_ref[at, :].astype(HIGH) * inv_ref[at, :]).astype(LOW)
+        product = scaled.astype(HIGH) * mixed_ref[at, :]
+        d_query = jnp.zeros((rows, LANES), HIGH)
+        d_key = jnp.zeros((LANES, seq_len), HIGH)
+        d_value = jnp.zeros((LANES, seq_len), HIGH)
+        for head in range(2):
+            scaled_h = scaled * low_masks[head]
+            delta = jnp.sum(product * masks[head], axis=-1, keepdims=True)
+            weights = e_ref[head, at, :]
+            d_scores = weights.astype(HIGH) * (matmul_nt(scaled_h, values) - delta)
+            d_low = d_scores.astype(LOW)
+            window = slice(seq_len - block * rows, 2 * seq_len - block * rows)
+            table_ref[head, :, window] += d_scores
+            d_query = d_query + matmul_nn(d_low, keys_h[head])
+            d_key = d_key + matmul_tn(queries * low_masks[head], d_low)
+            d_value = d_value + matmul_tn(scaled_h, weights)
+        dq_ref[at, :] = d_query.astype(LOW)
+        if block == 0:
+            dkt_ref[...] = d_key
+            dvt_ref[...] = d_value
+        else:
+            dkt_ref[...] += d_key
+            dvt_ref[...] += d_value
+    dk_ref[...] = dkt_ref[...].T.astype(LOW)
+    dv_ref[...] = dvt_ref[...].T.astype(LOW)
+    width = 2 * seq_len
+    sub = lax.broadcasted_iota(jnp.int32, (8, 1), 0)
+    for head in range(2):
+        total = table_ref[head, 0:8, :]
+        for group in range(1, rows // 8):
+            part = table_ref[head, 8 * group : 8 * group + 8, :]
+            total = total + pltpu.roll(part, width - 8 * group, 1)
+        for bit in (1, 2, 4):
+            total = jnp.where((sub & bit) != 0, pltpu.roll(total, width - bit, 1), total)
+        strip_ref[0, head : head + 1, :] = jnp.sum(total, axis=0, keepdims=True)
+
+
+def spread_body(
+    place_ref, x_ref, dq_ref, dk_ref, dv_ref, qkv_ref, send_ref, own_ref, dgain_ref
+):
+    step = pl.program_id(0)
+    width = dq_ref.shape[1]
+    unit, _ = rms_parts(x_ref[...].astype(HIGH))
+    d_normed = (
+        matmul_nt(dq_ref[...], qkv_ref[:, :width])
+        + matmul_nt(dk_ref[...], qkv_ref[:, width : 2 * width])
+        + matmul_nt(dv_ref[...], qkv_ref[:, 2 * width :])
+    )
+    d_gain = jnp.sum(d_normed * unit, axis=0, keepdims=True)
+
+    @pl.when(step == 0)
+    def _():
+        dgain_ref[...] = d_gain
+
+    @pl.when(step != 0)
+    def _():
+        dgain_ref[...] += d_gain
+
+    @pl.when(step < pl.num_programs(0) // 2)
+    def _():
+        send_ref[...] = d_normed.astype(LOW)
+
+    @pl.when(step >= pl.num_programs(0) // 2)
+    def _():
+        own_ref[...] = d_normed
+
+
+def finish_body(x_ref, own_ref, other_ref, datt_ref, gain_ref, out_ref):
+    unit, scale = rms_parts(x_ref[...].astype(HIGH))
+    d_normed = own_ref[...] + other_ref[...].astype(HIGH)
+    out_ref[...] = (datt_ref[...] + rms_back(d_normed, unit, scale, gain_ref[...])).astype(LOW)
+
+
+def weight_grads(place, first, second, columns, axis, micros):
+    left0, right0, at0, count0 = first
+    left1, right1, at1, count1 = second
+    height, depth = left0.shape
+    steps = count0 + count1
+    count = lax.axis_size("dp")
+    block = (count // 4, 2, 2, height // count, columns)
+    half = (block[0],) + block[2:]
+    total = half[:-1] + (steps * columns,)
+    half_spec = pl.BlockSpec(half, lambda i, *_: (0, 0, 0, i))
+    return call(
+        functools.partial(grads_body, count0, axis),
+        (steps,),
+        [
+            whole((height, depth)),
+            whole((height, depth)),
+            pl.BlockSpec((depth, columns), lambda i, *_: (0, at0 + jnp.minimum(i, count0 - 1))),
+            pl.BlockSpec((depth, columns), lambda i, *_: (0, at1 + jnp.maximum(i - count0, 0))),
+        ],
+        [half_spec, half_spec],
+        [shaped(total, LOW), shaped(total, LOW)],
+        [pltpu.VMEM(block, LOW)],
+        prefetch=1,
+        micros=micros,
+    )(place, left0, left1, right0, right1)
+
+
+def on_core_pair(
+    tokens,
+    cotangent,
+    gain_attn,
+    w_query,
+    w_key,
+    w_value,
+    w_out,
+    rel_table,
+    buckets,
+    gain_ffn,
+    w_gate,
+    w_up,
+    w_down,
+):
+    own_rows, features = tokens.shape
+    seq_len = 2 * own_rows
+    width = w_query.shape[1]
+    units = w_gate.shape[1]
+    chunk = units // 2
+    pairs = width // LANES
+    bucket_count, head_count = rel_table.shape
+    local_heads = head_count // 2
+    count = lax.axis_size("dp")
+    far_bit, y_bit, x_bit = dp_place()
+    me = lax.axis_index("mp")
+    place = jnp.stack([y_bit, x_bit, me, far_bit]).astype(jnp.int32)
+    rows = MXU_ROWS
+    steps = seq_len // rows
+    half_steps = steps // 2
+    block_rows = w_query.shape[0]
+
+    def swapped(array):
+        return lax.ppermute(array, "mp", [(0, 1), (1, 0)])
+
+    def in_order(array, other):
+        first = jnp.where(me == 0, array, other)
+        second = jnp.where(me == 0, other, array)
+        return jnp.concatenate([first, second], axis=0)
+
+    early = jnp.concatenate([w_query, w_key, w_value, w_out.T], axis=1)
+    late = jnp.concatenate([w_gate, w_up, w_down.T], axis=1)
+    early_pieces = far_pieces(early)
+    x_other, g_other = swapped(tokens), swapped(cotangent)
+    *early_pieces, late = together(*early_pieces, late)
+    near = far_stack(early, early_pieces)
+    late_pieces = far_pieces(late)
+    qk = near[:, :, : 2 * width]
+    vo = near[:, :, 2 * width :]
+    qk_next, vo_next = together(over_y(qk), over_x(vo))
+    qk_own = in_bit_order(qk, qk_next, y_bit, 1)
+    vo_own = in_bit_order(vo, vo_next, x_bit, 1)
+    qk_other = over_x(qk_own)
+    vo_other = over_y(vo_own)
+    x_all = in_order(tokens, x_other)
+    g_all = in_order(cotangent, g_other)
+    qk_other, vo_other, x_all, g_all, *late_pieces = together(
+        qk_other, vo_other, x_all, g_all, *late_pieces
+    )
+    near = far_stack(late, late_pieces)
+    gu = near[:, :, : 3 * chunk]
+    ud = near[:, :, 3 * chunk :]
+    gu_next = over_y(gu)
+    ud_next = over_x(ud)
+
+    gain_a = gain_attn.reshape(1, features)
+    gain_f = gain_ffn.reshape(1, features)
+
+    one_hot = (buckets[:, None] == jnp.arange(bucket_count, dtype=jnp.int32)[None, :]).astype(HIGH)
+    one_hot = jnp.pad(one_hot, ((1, 0), (0, 0)))
+    my_table = lax.dynamic_slice_in_dim(rel_table, me * local_heads, local_heads, 1)
+    strip = lax.dot_general(my_table, one_hot, (((0,), (1,)), ((), ())), precision=precise)
+    strip = strip.reshape(pairs, 2, 2 * seq_len)
+
+    def row_block(columns):
+        return pl.BlockSpec((rows, columns), lambda i, *_: (i, 0))
+
+    turned_block = pl.BlockSpec((features, rows), lambda i, *_: (0, i))
+    full_block = (count // 4, 2, 2, block_rows, 2 * width)
+    half_block = (count // 4, 2, block_rows, 2 * width)
+    normed_turned, queries, keys, values, w_qkv, w_o = call(
+        project_body,
+        (steps,),
+        [row_block(features), whole((1, features))] + [whole(half_block)] * 4,
+        [turned_block]
+        + [row_block(width)] * 3
+        + [result((features, 3 * width)), result((features, width))],
+        [shaped((features, seq_len), LOW)]
+        + [shaped((seq_len, width), LOW)] * 3
+        + [shaped((features, 3 * width), LOW), shaped((features, width), LOW)],
+        [pltpu.VMEM(full_block, LOW), pltpu.VMEM(full_block, LOW)],
+        prefetch=1,
+        micros=7,
+    )(place, x_all, gain_a, qk_own, qk_other, vo_own, vo_other)
+
+    gu_next, ud_next, queries = together(gu_next, ud_next, queries)
+    gu_own = in_bit_order(gu, gu_next, y_bit, 1)
+    ud_own = in_bit_order(ud, ud_next, x_bit, 1)
+    gu_other = over_x(gu_own)
+    ud_other = over_y(ud_own)
+
+    pair_block = pl.BlockSpec((seq_len, LANES), lambda p: (0, p))
+    e_block = pl.BlockSpec((2, seq_len, seq_len), lambda p: (p, 0, 0))
+    strip_block = pl.BlockSpec((1, 2, 2 * seq_len), lambda p: (p, 0, 0))
+    table_scratch = pltpu.VMEM((2, rows, 2 * seq_len), HIGH)
+    weights_e, mixed, mixed_low, inverse, part = call(
+        attend_body,
+        (pairs,),
+        [
+            pair_block,
+            pair_block,
+            pair_block,
+            strip_block,
+            pl.BlockSpec((features, LANES), lambda p: (0, p)),
+        ],
+        [e_block, pair_block, pair_block, pair_block, result((seq_len, features))],
+        [
+            shaped((2 * pairs, seq_len, seq_len), LOW),
+            shaped((seq_len, width), HIGH),
+            shaped((seq_len, width), LOW),
+            shaped((seq_len, width), HIGH),
+            shaped((seq_len, features), LOW),
+        ],
+        [table_scratch, pltpu.VMEM((seq_len, features), HIGH)],
+        micros=20,
+    )(queries, keys, values, strip, w_o)
+    gu_other, ud_other, part = together(gu_other, ud_other, part)
+    part_other = swapped(part)
+
+    def moved(i, m):
+        return (i + half_steps * (1 - m[2])) % steps
+
+    def turned_row(columns):
+        return pl.BlockSpec((rows, columns), lambda i, m: (moved(i, m), 0))
+
+    moved_block = pl.BlockSpec((features, rows), lambda i, m: (0, moved(i, m)))
+    send_row = pl.BlockSpec((rows, features), lambda i, m: (jnp.minimum(i, half_steps - 1), 0))
+    keep_row = pl.BlockSpec((rows, features), lambda i, m: (jnp.maximum(i - half_steps, 0), 0))
+    full_block = (count // 4, 2, 2, block_rows, 3 * chunk)
+    half_block = (count // 4, 2, block_rows, 3 * chunk)
+    normed_f_turned, g_turned, hidden, d_gate_up, dn_part, out_send, out_own = call(
+        feed_body,
+        (steps,),
+        [turned_row(features)] * 4 + [whole((1, features))] + [whole(half_block)] * 4,
+        [
+            moved_block,
+            moved_block,
+            turned_row(units),
+            turned_row(2 * units),
+            turned_row(features),
+            send_row,
+            keep_row,
+        ],
+        [
+            shaped((features, seq_len), LOW),
+            shaped((features, seq_len), LOW),
+            shaped((seq_len, units), LOW),
+            shaped((seq_len, 2 * units), LOW),
+            shaped((seq_len, features), LOW),
+            shaped((own_rows, features), LOW),
+            shaped((own_rows, features), HIGH),
+        ],
+        [pltpu.VMEM(full_block, LOW), pltpu.VMEM(full_block, LOW)],
+        prefetch=1,
+        micros=19,
+    )(place, x_all, part, part_other, g_all, gain_f, gu_own, gu_other, ud_own, ud_other)
+    dn_other = swapped(dn_part)
+
+    gu_own, gu_send = weight_grads(
+        place, (normed_f_turned, d_gate_up, 0, 2), (normed_f_turned, d_gate_up, 2, 1), chunk, 2, 6
+    )
+    gu_send, hidden, dn_other = together(gu_send, hidden, dn_other)
+    gu_came = over_x(gu_send)
+    ud_own, ud_send = weight_grads(
+        place, (normed_f_turned, d_gate_up, 3, 1), (g_turned, hidden, 0, 2), chunk, 1, 6
+    )
+    ud_send, dn_other = together(ud_send, dn_other)
+    ud_came = over_y(ud_send)
+
+    d_attended, d_low_turned, d_mixed, d_gain_f = call(
+        turn_body,
+        (steps,),
+        [turned_row(features)] * 6 + [whole((1, features)), whole((features, width))],
+        [keep_row, moved_block, turned_row(width), result((1, features))],
+        [
+            shaped((own_rows, features), HIGH),
+            shaped((features, seq_len), LOW),
+            shaped((seq_len, width), LOW),
+            shaped((1, features), HIGH),
+        ],
+        prefetch=1,
+        micros=8,
+    )(place, x_all, part, part_other, g_all, dn_part, dn_other, gain_f, w_o)
+    out_other = swapped(out_send)
+
+    d_query, d_key, d_value, d_strip = call(
+        backward_body,
+        (pairs,),
+        [pair_block, pair_block, pair_block, e_block, pair_block, pair_block, pair_block],
+        [pair_block, pair_block, pair_block, strip_block],
+        [shaped((seq_len, width), LOW)] * 3 + [shaped((pairs, 2, 2 * seq_len), HIGH)],
+        [table_scratch, pltpu.VMEM((LANES, seq_len), HIGH), pltpu.VMEM((LANES, seq_len), HIGH)],
+        micros=16,
+    )(queries, keys, values, weights_e, d_mixed, mixed, inverse)
+
+    gu_came, ud_came, out_other, d_query, d_key, d_value, d_strip = together(
+        gu_came, ud_came, out_other, d_query, d_key, d_value, d_strip
+    )
+
+    def next_half(own, came, bit):
+        return (
+            add_low(at_bit(own, bit, 1), at_bit(came, bit, 1)),
+            add_low(at_bit(own, 1 - bit, 1), at_bit(came, 1 - bit, 1)),
+        )
+
+    gu_own, gu_send = next_half(gu_own, gu_came, y_bit)
+    ud_own, ud_send = next_half(ud_own, ud_came, x_bit)
+    gu_came = over_y(gu_send)
+    ud_came = over_x(ud_send)
+
+    qk_own, qk_send = weight_grads(
+        place, (normed_turned, d_query, 0, 1), (normed_turned, d_key, 0, 1), width, 2, 5
+    )
+    qk_send, d_value = together(qk_send, d_value)
+    vo_own, vo_send = weight_grads(
+        place, (normed_turned, d_value, 0, 1), (d_low_turned, mixed_low, 0, 1), width, 1, 5
+    )
+    output = (out_own + out_other.astype(HIGH)).astype(LOW)
+
+    def far_sums(own, came):
+        total = add_low(own, came)
+        pieces = [over_far(at_bit(total, (far_bit + k) % (count // 4), 0), k) for k in range(1, count // 4)]
+        return (at_bit(total, far_bit, 0), pieces)
+
+    gu_came, ud_came, qk_send, vo_send, d_query = together(
+        gu_came, ud_came, qk_send, vo_send, d_query
+    )
+    qk_came = over_x(qk_send)
+    vo_came = over_y(vo_send)
+    gu_kept, gu_pieces = far_sums(gu_own, gu_came)
+    ud_kept, ud_pieces = far_sums(ud_own, ud_came)
+
+    dna_send, dna_own, d_gain_a = call(
+        spread_body,
+        (steps,),
+        [turned_row(features)] + [turned_row(width)] * 3 + [whole((features, 3 * width))],
+        [send_row, keep_row, result((1, features))],
+        [
+            shaped((own_rows, features), LOW),
+            shaped((own_rows, features), HIGH),
+            shaped((1, features), HIGH),
+        ],
+        prefetch=1,
+        micros=7,
+    )(place, x_all, d_query, d_key, d_value, w_qkv)
+    qk_came, vo_came, dna_send, d_gain_a, d_strip = together(
+        qk_came, vo_came, dna_send, d_gain_a, d_strip
+    )
+    dna_other = swapped(dna_send)
+    qk_own, qk_send = next_half(qk_own, qk_came, y_bit)
+    vo_own, vo_send = next_half(vo_own, vo_came, x_bit)
+    qk_came = over_y(qk_send)
+    vo_came = over_x(vo_send)
+
+    d_bias = d_strip.reshape(local_heads, 2 * seq_len)
+    my_d_table = lax.dot_general(one_hot, d_bias, (((0,), (1,)), ((), ())), precision=precise)
+    d_table = lax.dynamic_update_slice_in_dim(
+        jnp.zeros_like(rel_table), my_d_table, me * local_heads, 1
+    )
+    small = jnp.concatenate(
+        [d_gain_a.reshape(features), 0.5 * d_gain_f.reshape(features), d_table.reshape(-1)]
+    )
+    small = jnp.pad(small, (0, -small.shape[0] % 1024)).reshape(-1, LANES)
+    small = sum_all(small).reshape(-1)
+
+    d_tokens = call(
+        finish_body,
+        (half_steps,),
+        [row_block(features)] * 4 + [whole((1, features))],
+        row_block(features),
+        shaped((own_rows, features), LOW),
+        micros=3.5,
+    )(tokens, dna_own, dna_other, d_attended, gain_a)
+
+    qk_came, vo_came, d_tokens, *far_came = together(
+        qk_came, vo_came, d_tokens, *gu_pieces, *ud_pieces
+    )
+    gu_pieces, ud_pieces = far_came[: len(gu_pieces)], far_came[len(gu_pieces) :]
+    qk_kept, qk_pieces = far_sums(qk_own, qk_came)
+    vo_kept, vo_pieces = far_sums(vo_own, vo_came)
+
+    def summed(kept, pieces):
+        return sum((piece.astype(HIGH) for piece in pieces), kept.astype(HIGH))
+
+    grads_gu, grads_ud = summed(gu_kept, gu_pieces), summed(ud_kept, ud_pieces)
+    grads_qk, grads_vo = summed(qk_kept, qk_pieces), summed(vo_kept, vo_pieces)
+    return (
+        output,
+        d_tokens,
+        small[:features],
+        grads_qk[:, :width],
+        grads_qk[:, width:],
+        grads_vo[:, :width],
+        grads_vo[:, width:].T,
+        small[2 * features : 2 * features + rel_table.size].reshape(rel_table.shape),
+        small[features : 2 * features],
+        grads_gu[:, :units],
+        jnp.concatenate([grads_gu[:, units:], grads_ud[:, :chunk]], axis=1),
+        grads_ud[:, chunk:].T,
+    )
+
+
 def solution(mesh):
     placed = (
         P(("dp", "mp"), None),
@@ -337,8 +1111,10 @@
         P("dp", "mp"),
         P("mp", "dp"),
     )
+    paired = mesh.shape["mp"] == 2 and mesh.shape["dp"] % 4 == 0
+    body = on_core_pair if paired else on_device
     return jax.shard_map(
-        on_device,
+        body,
         mesh=mesh,
         in_specs=placed,
         out_specs=(

time: 2540 us -> 255 us (0.10)
  local copies, waits for them, and re-layouts: 1120 us -> 15 us
  waiting for transfers between devices: 1070 us -> 40.7 us
  matrix products: 158 us -> 1.26 us
  Pallas kernels: 0 us -> 114 us
  loops' own time: 68.7 us -> 0 us
  starting transfers between devices: 1.49 us -> 67.4 us
  blocking collectives: 52.9 us -> 0 us
  other arithmetic: 42.6 us -> 14.6 us
    reduce_scatter x10 -> x0, waiting for transfers between devices: 629 us -> none  [the longest x1 127 us: on_device(): lax.psum_scatter(d_gate_w.astype(jnp.bfloat16), 'dp', scatter_dimension=0...]
    reshape x13 -> x6, local copies, waits for them, and re-layouts: 368 us -> 2.05 us  [the longest x1 0.65 us: on_core_pair(): strip = strip.reshape(pairs, 2, 2 * seq_len)]
    another operation x12 -> x2, local copies, waits for them, and re-layouts: 301 us -> 1.99 us  [in_bit_order(): jnp.stack([jnp.where(bit == 0, own, other), jnp.where(bit == 0, other, ow...]
    all_gather x11 -> x0, waiting for transfers between devices: 297 us -> none  [the longest x7 274 us: on_device(): lax.all_gather(as_sent(tuple(col_parts) + ffn_parts), 'dp', axis=0, tiled...]
    slice x12 -> x9, local copies, waits for them, and re-layouts: 217 us -> 2.12 us  [the longest x1 0.69 us: on_core_pair(): grads_gu[:, :units]]
    dot_general x37 -> x2, matrix products: 158 us -> 1.26 us  [the longest x1 0.64 us: on_core_pair(): lax.dot_general(my_table, one_hot, (((0,), (1,)), ((), ())), precision=pr...]
    while x36 -> x0, local copies, waits for them, and re-layouts: 148 us -> none
    unnamed x31 -> x0, waiting for transfers between devices: 143 us -> none
  transfers between devices with their start and end apart: 26 -> 47, of which waited for: 20 -> 19; matrix products, arithmetic and copies ran while one was open for 51% -> 8% of each run, Pallas kernels for 0% -> 37%
where the time goes in v2:
time: 255 us; the launch traced here: 254 us
  Pallas kernels  114 us (45%)
  starting transfers between devices  67.4 us (26%)
  waiting for transfers between devices  40.7 us (16%)
  local copies, waits for them, and re-layouts  15 us (6%)
  other arithmetic  14.6 us (6%)
    ppermute x21, starting transfers between devices, over_far(): return lax.ppermute(array, 'dp', ring_shift(4 * steps, lax.axis_size('dp')))  42.1 us
    pallas_call x4, Pallas kernels, weight_grads(): call(functools.partial(grads_body, count0, axis), (steps,), [whole((heigh...  28.2 us
    pallas_call x1, Pallas kernels, on_core_pair(): call(attend_body, (pairs,), [pair_block, pair_block, pair_block, strip_bl...  21.9 us
    ppermute x21, waiting for transfers between devices, over_far(): return lax.ppermute(array, 'dp', ring_shift(4 * steps, lax.axis_size('dp')))  21.1 us
    pallas_call x1, Pallas kernels, on_core_pair(): call(feed_body, (steps,), [turned_row(features)] * 4 + [whole((1, feature...  19.4 us
    pallas_call x1, Pallas kernels, on_core_pair(): call(backward_body, (pairs,), [pair_block, pair_block, pair_block, e_bloc...  16.5 us
    ppermute x8, starting transfers between devices, over_x(): return lax.ppermute(array, 'dp', flip(1, lax.axis_size('dp')))  12.8 us
    ppermute x8, waiting for transfers between devices, over_y(): return lax.ppermute(array, 'dp', flip(2, lax.axis_size('dp')))  12.3 us
  transfers between devices with their start and end apart: 47, of which 19 were waited for; matrix products, arithmetic and copies ran while one was open for 8% of the time, Pallas kernels for 37%

profile of v2, /device:TPU:0, one launch (start us, length us, event | category | flops | bytes accessed | tf_op | source)
XLA Modules:
  0.0 254.4 jit_solution(13646675572729457650)
XLA Ops:
  1.7 3.1 %collective-permute-start = (bf16[48,1536]{1,0:T(8,128)(2,1)S(1)}, bf16[48,1536]{1,0:T(8,128)(2,1)S(1)}, u32[]{:S(2)}, u32[]{:S(2)}) collective-permute-start(bf16[48,1536]{1,0:T(8,128)(2,1)S(1)} %pad_maximum_fusion.8), channel_id=1, source_target_pairs={{0,8},{2,10},{4,12},{6,14},{8,16},{10,18},{12,20},{14,22},{16,24},... | collective-permute-start | bytes 442376 | tf_op jit(solution)/shard_map/ppermute | solution.py:390
  13.0 4.1 %collective-permute-done.1 = bf16[48,1536]{1,0:T(8,128)(2,1)S(1)} collective-permute-done((bf16[48,1536]{1,0:T(8,128)(2,1)S(1)}, bf16[48,1536]{1,0:T(8,128)(2,1)S(1)}, u32[]{:S(2)}, u32[]{:S(2)}) %collective-permute-start.1) | collective-permute-done | bytes 147488 | tf_op jit(solution)/shard_map/ppermute | solution.py:390
  20.2 2.6 %collective-permute-start.10 = (bf16[48,3072]{1,0:T(8,128)(2,1)S(1)}, bf16[48,3072]{1,0:T(8,128)(2,1)S(1)}, u32[]{:S(2)}, u32[]{:S(2)}) collective-permute-start(bf16[48,3072]{1,0:T(8,128)(2,1)S(1)} %pad_maximum_fusion.6), channel_id=1, source_target_pairs={{0,16},{2,18},{4,20},{6,22},{8,24},{10,26},{12,28},{14,30},{16,0},... | collective-permute-start | bytes 884744 | tf_op jit(solution)/shard_map/ppermute | solution.py:390
  23.0 3.1 %collective-permute-done.3 = bf16[4,48,768]{2,1,0:T(8,128)(2,1)S(1)} collective-permute-done((bf16[4,48,768]{2,1,0:T(8,128)(2,1)S(1)}, bf16[4,48,768]{2,1,0:T(8,128)(2,1)S(1)}, u32[]{:S(2)}, u32[]{:S(2)}) %collective-permute-start.3) | collective-permute-done | bytes 294944 | tf_op jit(solution)/shard_map/ppermute | solution.py:386
  26.1 3.7 %collective-permute-start.11 = (bf16[48,3072]{1,0:T(8,128)(2,1)S(1)}, bf16[48,3072]{1,0:T(8,128)(2,1)S(1)}, u32[]{:S(2)}, u32[]{:S(2)}) collective-permute-start(bf16[48,3072]{1,0:T(8,128)(2,1)S(1)} %pad_maximum_fusion.6), channel_id=1, source_target_pairs={{0,24},{2,26},{4,28},{6,30},{8,0},{10,2},{12,4},{14,6},{16,8},{18,... | collective-permute-start | bytes 884744 | tf_op jit(solution)/shard_map/ppermute | solution.py:390
  38.2 7.4 %collective-permute-done.11 = bf16[48,3072]{1,0:T(8,128)(2,1)S(1)} collective-permute-done((bf16[48,3072]{1,0:T(8,128)(2,1)S(1)}, bf16[48,3072]{1,0:T(8,128)(2,1)S(1)}, u32[]{:S(2)}, u32[]{:S(2)}) %collective-permute-start.11) | collective-permute-done | bytes 294944 | tf_op jit(solution)/shard_map/ppermute | solution.py:390
  49.8 8.1 %shard_map.220 = (bf16[768,1024]{1,0:T(8,128)(2,1)}, bf16[1024,384]{1,0:T(8,128)(2,1)}, bf16[1024,384]{1,0:T(8,128)(2,1)}, bf16[1024,384]{1,0:T(8,128)(2,1)}, bf...) custom-call(s32[4]{0:T(128)} %pad_add_fusion.place_ref, bf16[1024,768]{1,0:T(8,128)(2,1)} %pad_maximum_fusion.x_ref, ...), custom_call_target="tpu_custom_call" | custom-call | flops 8074500096 | tf_op jit(solution)/shard_map/pallas_call | solution.py:866
  58.0 3.1 %collective-permute-done.12 = bf16[4,48,1536]{2,1,0:T(8,128)(2,1)S(1)} collective-permute-done((bf16[4,48,1536]{2,1,0:T(8,128)(2,1)S(1)}, bf16[4,48,1536]{2,1,0:T(8,128)(2,1)S(1)}, u32[]{:S(2)}, u32[]{:S(2)}) %collective-permute-start.12) | collective-permute-done | bytes 589856 | tf_op jit(solution)/shard_map/ppermute | solution.py:386
  65.2 21.9 %shard_map.221 = (bf16[6,1024,1024]{2,1,0:T(8,128)(2,1)}, f32[1024,384]{1,0:T(8,128)}, bf16[1024,384]{1,0:T(8,128)(2,1)}, f32[1024,384]{1,0:T(8,128)}, bf16[1024,768]{1,0:T(8,128)(2,1)}) custom-call(bf16[1024,384]{1,0:T(8,128)(2,1)} %get-tuple-element.116.q_ref, bf16[1024,384]{1,0:T(8,128)(2,1)} %get-tuple-element.117.k_ref, ...), custom_call_target="tpu_custom_call" | custom-call | flops 23069999104 | tf_op jit(solution)/shard_map/pallas_call | solution.py:891
  94.0 19.4 %shard_map.222 = (bf16[768,1024]{1,0:T(8,128)(2,1)}, bf16[768,1024]{1,0:T(8,128)(2,1)}, bf16[1024,1024]{1,0:T(8,128)(2,1)}, bf16[1024,2048]{1,0:T(8,128)(2,1)}, ...) custom-call(s32[4]{0:T(128)} %pad_add_fusion.place_ref, ...), custom_call_target="tpu_custom_call" | custom-call | flops 21916499968 | tf_op jit(solution)/shard_map/pallas_call | solution.py:926
  114.0 7.9 %shard_map.223 = (bf16[4,2,48,1536]{3,2,1,0:T(8,128)(2,1)}, bf16[4,2,48,1536]{3,2,1,0:T(8,128)(2,1)}) custom-call(s32[4]{0:T(128)} %pad_add_fusion.place_ref, bf16[768,1024]{1,0:T(8,128)(2,1)} %get-tuple-element.126.left0_ref.left1_ref, bf16[768,1024]{1,0:T(8,128)(2,1)} %get-tuple-element.126.left0_ref.left1_ref, ...), custom_call_target="tpu_custom_call" | custom-call | flops 6920999936 | tf_op jit(solution)/shard_map/pallas_call | solution.py:769
  121.9 8.0 %shard_map.224 = (bf16[4,2,48,1536]{3,2,1,0:T(8,128)(2,1)}, bf16[4,2,48,1536]{3,2,1,0:T(8,128)(2,1)}) custom-call(s32[4]{0:T(128)} %pad_add_fusion.place_ref, bf16[768,1024]{1,0:T(8,128)(2,1)} %get-tuple-element.126.left0_ref.left1_ref, bf16[768,1024]{1,0:T(8,128)(2,1)} %get-tuple-element.132.left1_ref, ...), custom_call_target="tpu_custom_call" | custom-call | flops 6920999936 | tf_op jit(solution)/shard_map/pallas_call | solution.py:769
  132.7 8.5 %shard_map.225 = (f32[512,768]{1,0:T(8,128)}, bf16[768,1024]{1,0:T(8,128)(2,1)}, bf16[1024,384]{1,0:T(8,128)(2,1)}, f32[1,768]{1,0:T(1,128)}) custom-call(s32[4]{0:T(128)} %pad_add_fusion.place_ref, bf16[1024,768]{1,0:T(8,128)(2,1)} %pad_maximum_fusion.x_ref, bf16[1024,768]{1,0:T(8,128)(2,1)} %get-tuple-element.121.p_ref, bf16[1024,768]{1,0:T(8,128)(2,1)} %copy-done.29, ...), custom_call_target="tpu_custom_call" | custom-call | flops 9228000256 | tf_op jit(solution)/shard_map/pallas_call | solution.py:965
  141.2 16.5 %shard_map.226 = (bf16[1024,384]{1,0:T(8,128)(2,1)}, bf16[1024,384]{1,0:T(8,128)(2,1)}, bf16[1024,384]{1,0:T(8,128)(2,1)}, f32[3,2,2048]{2,1,0:T(2,128)}) custom-call(bf16[1024,384]{1,0:T(8,128)(2,1)} %get-tuple-element.116.q_ref, bf16[1024,384]{1,0:T(8,128)(2,1)} %get-tuple-element.117.k_ref, bf16[1024,384]{1,0:T(8,128)(2,1)} %get-tuple-element.118.v_ref, ...), custom_call_target="tpu_custom_call" | custom-call | flops 18456000512 | tf_op jit(solution)/shard_map/pallas_call | solution.py:981
  162.7 6.2 %shard_map.227 = (bf16[4,2,48,768]{3,2,1,0:T(8,128)(2,1)}, bf16[4,2,48,768]{3,2,1,0:T(8,128)(2,1)}) custom-call(s32[4]{0:T(128)} %pad_add_fusion.place_ref, bf16[768,1024]{1,0:T(8,128)(2,1)} %get-tuple-element.148.left0_ref.left1_ref, bf16[768,1024]{1,0:T(8,128)(2,1)} %get-tuple-element.148.left0_ref.left1_ref, ...), custom_call_target="tpu_custom_call" | custom-call | flops 5767499776 | tf_op jit(solution)/shard_map/pallas_call | solution.py:769
  170.0 6.2 %shard_map.228 = (bf16[4,2,48,768]{3,2,1,0:T(8,128)(2,1)}, bf16[4,2,48,768]{3,2,1,0:T(8,128)(2,1)}) custom-call(s32[4]{0:T(128)} %pad_add_fusion.place_ref, bf16[768,1024]{1,0:T(8,128)(2,1)} %get-tuple-element.148.left0_ref.left1_ref, bf16[768,1024]{1,0:T(8,128)(2,1)} %get-tuple-element.159.left1_ref, ...), custom_call_target="tpu_custom_call" | custom-call | flops 5767499776 | tf_op jit(solution)/shard_map/pallas_call | solution.py:769
  177.2 4.0 %collective-permute-start.31 = (bf16[48,1536]{1,0:T(8,128)(2,1)}, bf16[48,1536]{1,0:T(8,128)(2,1)}, u32[]{:S(2)}, u32[]{:S(2)}) collective-permute-start(bf16[48,1536]{1,0:T(8,128)(2,1)} %get-tuple-element.220), channel_id=1, source_target_pairs={{0,8},{2,10},{4,12},{6,14},{8,16},{10,18},{12,20},{14,22},{16,24},... | collective-permute-start | bytes 442376 | tf_op jit(solution)/shard_map/ppermute | solution.py:390
  183.7 8.0 %shard_map.229 = (bf16[512,768]{1,0:T(8,128)(2,1)}, f32[512,768]{1,0:T(8,128)}, f32[1,768]{1,0:T(1,128)}) custom-call(s32[4]{0:T(128)} %pad_add_fusion.place_ref, bf16[1024,768]{1,0:T(8,128)(2,1)} %pad_maximum_fusion.x_ref, bf16[1024,384]{1,0:T(8,128)(2,1)} %get-tuple-element.165.right0_ref.dq_ref, bf16[1024,384]{1,0:T(8,128)(2,1)} %get-tuple-element.150.right1_ref.dk_ref, ...), custom_call_target="tpu_custom_call" | custom-call | flops 8074500096 | tf_op jit(solution)/shard_map/pallas_call | solution.py:1028
  191.9 2.9 %collective-permute-done.23 = bf16[4,2,48,768]{3,2,1,0:T(8,128)(2,1)S(1)} collective-permute-done((bf16[4,2,48,768]{3,2,1,0:T(8,128)(2,1)}, bf16[4,2,48,768]{3,2,1,0:T(8,128)(2,1)S(1)}, u32[]{:S(2)}, u32[]{:S(2)}) %collective-permute-start.23) | collective-permute-done | bytes 589856 | tf_op jit(solution)/shard_map/ppermute | solution.py:382
  202.5 2.6 %collective-permute-start.37 = (f32[16,128]{1,0:T(8,128)S(1)}, f32[16,128]{1,0:T(8,128)S(1)}, u32[]{:S(2)}, u32[]{:S(2)}) collective-permute-start(f32[16,128]{1,0:T(8,128)S(1)} %fusion.30), channel_id=1, source_target_pairs={{0,24},{2,26},{4,28},{6,30},{8,0},{10,2},{12,4},{14,6},{16,8},{18,... | collective-permute-start | bytes 24584 | tf_op jit(solution)/shard_map/ppermute | solution.py:390
  219.1 7.5 %collective-permute-done.32 = bf16[48,1536]{1,0:T(8,128)(2,1)S(1)} collective-permute-done((bf16[48,1536]{1,0:T(8,128)(2,1)}, bf16[48,1536]{1,0:T(8,128)(2,1)S(1)}, u32[]{:S(2)}, u32[]{:S(2)}) %collective-permute-start.32) | collective-permute-done | bytes 147488 | tf_op jit(solution)/shard_map/ppermute | solution.py:390
  231.9 3.4 %shard_map.230 = bf16[512,768]{1,0:T(8,128)(2,1)} custom-call(bf16[512,768]{1,0:T(8,128)(2,1)} %x_ref.1, f32[512,768]{1,0:T(8,128)} %get-tuple-element.173.own_ref, bf16[512,768]{1,0:T(8,128)(2,1)} %collective-permute-done.27.other_ref, f32[512,768]{1,0:T(8,128)} %get-tuple-element.175.datt_ref, f32[1,768]{1,0:T(1,128)} %reshape.105.gain_ref), custom_call_target="tpu_custom_call" | custom-call | flops 4037250048 | tf_op jit(solution)/shard_map/pallas_call | solution.py:1061
  242.1 3.2 %collective-permute-start.46 = (bf16[48,768]{1,0:T(8,128)(2,1)S(1)}, bf16[48,768]{1,0:T(8,128)(2,1)S(1)}, u32[]{:S(2)}, u32[]{:S(2)}) collective-permute-start(bf16[48,768]{1,0:T(8,128)(2,1)S(1)} %get-tuple-element.229), channel_id=1, source_target_pairs={{0,24},{2,26},{4,28},{6,30},{8,0},{10,2},{12,4},{14,6},{16,8},{18,... | collective-permute-start | bytes 221192 | tf_op jit(solution)/shard_map/ppermute | solution.py:390
  248.3 2.8 %collective-permute-start.43 = (bf16[48,768]{1,0:T(8,128)(2,1)S(1)}, bf16[48,768]{1,0:T(8,128)(2,1)S(1)}, u32[]{:S(2)}, u32[]{:S(2)}) collective-permute-start(bf16[48,768]{1,0:T(8,128)(2,1)S(1)} %get-tuple-element.232), channel_id=1, source_target_pairs={{0,24},{2,26},{4,28},{6,30},{8,0},{10,2},{12,4},{14,6},{16,8},{18,... | collective-permute-start | bytes 221192 | tf_op jit(solution)/shard_map/ppermute | solution.py:390
  (221 shorter events, 89.0 us)
Async XLA Ops:
  8.7 23.5 %collective-permute-start.7 = (bf16[512,768]{1,0:T(8,128)(2,1)}, bf16[512,768]{1,0:T(8,128)(2,1)S(1)}, u32[]{:S(2)}, u32[]{:S(2)}) collective-permute-start(bf16[512,768]{1,0:T(8,128)(2,1)} %x_ref.1), channel_id=1, source_target_pairs={{0,1},{1,0},{2,3},{3,2},{4,5},{5,4},{6,7},{7,6},{8,9},{9,8},{10,11... | collective-permute-start | bytes 2359304 | tf_op jit(solution)/shard_map/ppermute | solution.py:819
  8.7 25.0 %collective-permute-start.8 = (bf16[512,768]{1,0:T(8,128)(2,1)}, bf16[512,768]{1,0:T(8,128)(2,1)}, u32[]{:S(2)}, u32[]{:S(2)}) collective-permute-start(bf16[512,768]{1,0:T(8,128)(2,1)} %param.14), channel_id=1, source_target_pairs={{0,1},{1,0},{2,3},{3,2},{4,5},{5,4},{6,7},{7,6},{8,9},{9,8},{10,11... | collective-permute-start | bytes 2359304 | tf_op jit(solution)/shard_map/ppermute | solution.py:819
  20.2 18.0 %collective-permute-start.10 = (bf16[48,3072]{1,0:T(8,128)(2,1)S(1)}, bf16[48,3072]{1,0:T(8,128)(2,1)S(1)}, u32[]{:S(2)}, u32[]{:S(2)}) collective-permute-start(bf16[48,3072]{1,0:T(8,128)(2,1)S(1)} %pad_maximum_fusion.6), channel_id=1, source_target_pairs={{0,16},{2,18},{4,20},{6,22},{8,24},{10,26},{12,28},{14,30},{16,0},... | collective-permute-start | bytes 884744 | tf_op jit(solution)/shard_map/ppermute | solution.py:390
  26.1 19.5 %collective-permute-start.11 = (bf16[48,3072]{1,0:T(8,128)(2,1)S(1)}, bf16[48,3072]{1,0:T(8,128)(2,1)S(1)}, u32[]{:S(2)}, u32[]{:S(2)}) collective-permute-start(bf16[48,3072]{1,0:T(8,128)(2,1)S(1)} %pad_maximum_fusion.6), channel_id=1, source_target_pairs={{0,24},{2,26},{4,28},{6,30},{8,0},{10,2},{12,4},{14,6},{16,8},{18,... | collective-permute-start | bytes 884744 | tf_op jit(solution)/shard_map/ppermute | solution.py:390
  29.8 15.8 %collective-permute-start.9 = (bf16[48,3072]{1,0:T(8,128)(2,1)S(1)}, bf16[48,3072]{1,0:T(8,128)(2,1)S(1)}, u32[]{:S(2)}, u32[]{:S(2)}) collective-permute-start(bf16[48,3072]{1,0:T(8,128)(2,1)S(1)} %pad_maximum_fusion.6), channel_id=1, source_target_pairs={{0,8},{2,10},{4,12},{6,14},{8,16},{10,18},{12,20},{14,22},{16,24},... | collective-permute-start | bytes 884744 | tf_op jit(solution)/shard_map/ppermute | solution.py:390
  32.2 15.1 %collective-permute-start.5 = (bf16[4,2,48,768]{3,2,0,1:T(8,128)(2,1)S(1)}, bf16[4,2,48,768]{3,2,0,1:T(8,128)(2,1)S(1)}, u32[]{:S(2)}, u32[]{:S(2)}) collective-permute-start(bf16[4,2,48,768]{3,2,0,1:T(8,128)(2,1)S(1)} %pad_maximum_fusion.4), channel_id=1, source_target_pairs={{0,2},{2,0},{4,6},{6,4},{8,10},{10,8},{12,14},{14,12},{16,18},{18,... | collective-permute-start | bytes 1769480 | tf_op jit(solution)/shard_map/ppermute | solution.py:382
  33.7 13.5 %collective-permute-start.6 = (bf16[4,2,48,768]{3,2,1,0:T(8,128)(2,1)S(1)}, bf16[4,2,48,768]{3,2,1,0:T(8,128)(2,1)S(1)}, u32[]{:S(2)}, u32[]{:S(2)}) collective-permute-start(bf16[4,2,48,768]{3,2,1,0:T(8,128)(2,1)S(1)} %pad_maximum_fusion.5.vo_own_ref), channel_id=1, source_target_pairs={{0,4},{2,6},{4,0},{6,2},{8,12},{10,14},{12,8},{14,10},{16,20},{18,... | collective-permute-start | bytes 1769480 | tf_op jit(solution)/shard_map/ppermute | solution.py:386
  48.4 12.7 %collective-permute-start.12 = (bf16[4,48,1536]{2,1,0:T(8,128)(2,1)S(1)}, bf16[4,48,1536]{2,1,0:T(8,128)(2,1)S(1)}, u32[]{:S(2)}, u32[]{:S(2)}) collective-permute-start(bf16[4,48,1536]{2,1,0:T(8,128)(2,1)S(1)} %get-tuple-element.213), channel_id=1, source_target_pairs={{0,4},{2,6},{4,0},{6,2},{8,12},{10,14},{12,8},{14,10},{16,20},{18,... | collective-permute-start | bytes 1769480 | tf_op jit(solution)/shard_map/ppermute | solution.py:386
  49.1 13.3 %collective-permute-start.13 = (bf16[4,48,1536]{2,1,0:T(8,128)(2,1)S(1)}, bf16[4,48,1536]{2,1,0:T(8,128)(2,1)S(1)}, u32[]{:S(2)}, u32[]{:S(2)}) collective-permute-start(bf16[4,48,1536]{2,1,0:T(8,128)(2,1)S(1)} %get-tuple-element.212), channel_id=1, source_target_pairs={{0,2},{2,0},{4,6},{6,4},{8,10},{10,8},{12,14},{14,12},{16,18},{18,... | collective-permute-start | bytes 1769480 | tf_op jit(solution)/shard_map/ppermute | solution.py:382
  62.7 25.1 %collective-permute-start.15 = (bf16[4,2,48,1536]{3,2,1,0:T(8,128)(2,1)S(1)}, bf16[4,2,48,1536]{3,2,1,0:T(8,128)(2,1)S(1)}, u32[]{:S(2)}, u32[]{:S(2)}) collective-permute-start(bf16[4,2,48,1536]{3,2,1,0:T(8,128)(2,1)S(1)} %pad_maximum_fusion.3.ud_own_ref), channel_id=1, source_target_pairs={{0,4},{2,6},{4,0},{6,2},{8,12},{10,14},{12,8},{14,10},{16,20},{18,... | collective-permute-start | bytes 3538952 | tf_op jit(solution)/shard_map/ppermute | solution.py:386
  63.7 25.5 %collective-permute-start.14 = (bf16[4,2,48,1536]{3,2,0,1:T(8,128)(2,1)S(1)}, bf16[4,2,48,1536]{3,2,0,1:T(8,128)(2,1)S(1)}, u32[]{:S(2)}, u32[]{:S(2)}) collective-permute-start(bf16[4,2,48,1536]{3,2,0,1:T(8,128)(2,1)S(1)} %pad_maximum_fusion.2), channel_id=1, source_target_pairs={{0,2},{2,0},{4,6},{6,4},{8,10},{10,8},{12,14},{14,12},{16,18},{18,... | collective-permute-start | bytes 3538952 | tf_op jit(solution)/shard_map/ppermute | solution.py:382
  113.6 44.1 %collective-permute-start.20 = (bf16[512,768]{1,0:T(8,128)(2,1)}, bf16[512,768]{1,0:T(8,128)(2,1)S(1)}, u32[]{:S(2)}, u32[]{:S(2)}) collective-permute-start(bf16[512,768]{1,0:T(8,128)(2,1)} %get-tuple-element.137), channel_id=1, source_target_pairs={{0,1},{1,0},{2,3},{3,2},{4,5},{5,4},{6,7},{7,6},{8,9},{9,8},{10,11... | collective-permute-start | bytes 2359304 | tf_op jit(solution)/shard_map/ppermute | solution.py:819
  129.8 28.3 %collective-permute-start.19 = (bf16[4,2,48,1536]{3,2,1,0:T(8,128)(2,1)}, bf16[4,2,48,1536]{3,2,1,0:T(8,128)(2,1)S(1)}, u32[]{:S(2)}, u32[]{:S(2)}) collective-permute-start(bf16[4,2,48,1536]{3,2,1,0:T(8,128)(2,1)} %get-tuple-element.136), channel_id=1, source_target_pairs={{0,4},{2,6},{4,0},{6,2},{8,12},{10,14},{12,8},{14,10},{16,20},{18,... | collective-permute-start | bytes 3538952 | tf_op jit(solution)/shard_map/ppermute | solution.py:386
  130.9 27.9 %collective-permute-start.18 = (bf16[4,2,48,1536]{3,2,0,1:T(8,128)(2,1)S(1)}, bf16[4,2,48,1536]{3,2,0,1:T(8,128)(2,1)S(1)}, u32[]{:S(2)}, u32[]{:S(2)}) collective-permute-start(bf16[4,2,48,1536]{3,2,0,1:T(8,128)(2,1)S(1)} %copy.46), channel_id=1, source_target_pairs={{0,2},{2,0},{4,6},{6,4},{8,10},{10,8},{12,14},{14,12},{16,18},{18,... | collective-permute-start | bytes 3538952 | tf_op jit(solution)/shard_map/ppermute | solution.py:382
  158.9 17.2 %collective-permute-start.22 = (bf16[4,48,1536]{2,1,0:T(8,128)(2,1)S(1)}, bf16[4,48,1536]{2,1,0:T(8,128)(2,1)S(1)}, u32[]{:S(2)}, u32[]{:S(2)}) collective-permute-start(bf16[4,48,1536]{2,1,0:T(8,128)(2,1)S(1)} %fusion.5), channel_id=1, source_target_pairs={{0,2},{2,0},{4,6},{6,4},{8,10},{10,8},{12,14},{14,12},{16,18},{18,... | collective-permute-start | bytes 1769480 | tf_op jit(solution)/shard_map/ppermute | solution.py:382
  161.7 14.5 %collective-permute-start.21 = (bf16[4,48,1536]{2,1,0:T(8,128)(2,1)}, bf16[4,48,1536]{2,1,0:T(8,128)(2,1)S(1)}, u32[]{:S(2)}, u32[]{:S(2)}) collective-permute-start(bf16[4,48,1536]{2,1,0:T(8,128)(2,1)} %fusion.4), channel_id=1, source_target_pairs={{0,4},{2,6},{4,0},{6,2},{8,12},{10,14},{12,8},{14,10},{16,20},{18,... | collective-permute-start | bytes 1769480 | tf_op jit(solution)/shard_map/ppermute | solution.py:386
  177.2 39.7 %collective-permute-start.31 = (bf16[48,1536]{1,0:T(8,128)(2,1)}, bf16[48,1536]{1,0:T(8,128)(2,1)}, u32[]{:S(2)}, u32[]{:S(2)}) collective-permute-start(bf16[48,1536]{1,0:T(8,128)(2,1)} %get-tuple-element.220), channel_id=1, source_target_pairs={{0,8},{2,10},{4,12},{6,14},{8,16},{10,18},{12,20},{14,22},{16,24},... | collective-permute-start | bytes 442376 | tf_op jit(solution)/shard_map/ppermute | solution.py:390
  181.1 13.6 %collective-permute-start.23 = (bf16[4,2,48,768]{3,2,1,0:T(8,128)(2,1)}, bf16[4,2,48,768]{3,2,1,0:T(8,128)(2,1)S(1)}, u32[]{:S(2)}, u32[]{:S(2)}) collective-permute-start(bf16[4,2,48,768]{3,2,1,0:T(8,128)(2,1)} %get-tuple-element.163), channel_id=1, source_target_pairs={{0,2},{2,0},{4,6},{6,4},{8,10},{10,8},{12,14},{14,12},{16,18},{18,... | collective-permute-start | bytes 1769480 | tf_op jit(solution)/shard_map/ppermute | solution.py:382
  182.6 13.4 %collective-permute-start.24 = (bf16[4,2,48,768]{3,2,1,0:T(8,128)(2,1)}, bf16[4,2,48,768]{3,2,1,0:T(8,128)(2,1)S(1)}, u32[]{:S(2)}, u32[]{:S(2)}) collective-permute-start(bf16[4,2,48,768]{3,2,1,0:T(8,128)(2,1)} %get-tuple-element.164), channel_id=1, source_target_pairs={{0,4},{2,6},{4,0},{6,2},{8,12},{10,14},{12,8},{14,10},{16,20},{18,... | collective-permute-start | bytes 1769480 | tf_op jit(solution)/shard_map/ppermute | solution.py:386
  198.8 32.1 %collective-permute-start.27 = (bf16[512,768]{1,0:T(8,128)(2,1)}, bf16[512,768]{1,0:T(8,128)(2,1)}, u32[]{:S(2)}, u32[]{:S(2)}) collective-permute-start(bf16[512,768]{1,0:T(8,128)(2,1)} %get-tuple-element.174), channel_id=1, source_target_pairs={{0,1},{1,0},{2,3},{3,2},{4,5},{5,4},{6,7},{7,6},{8,9},{9,8},{10,11... | collective-permute-start | bytes 2359304 | tf_op jit(solution)/shard_map/ppermute | solution.py:819
  210.8 15.8 %collective-permute-start.32 = (bf16[48,1536]{1,0:T(8,128)(2,1)}, bf16[48,1536]{1,0:T(8,128)(2,1)S(1)}, u32[]{:S(2)}, u32[]{:S(2)}) collective-permute-start(bf16[48,1536]{1,0:T(8,128)(2,1)} %get-tuple-element.219), channel_id=1, source_target_pairs={{0,16},{2,18},{4,20},{6,22},{8,24},{10,26},{12,28},{14,30},{16,0},... | collective-permute-start | bytes 442376 | tf_op jit(solution)/shard_map/ppermute | solution.py:390
  212.7 15.8 %collective-permute-start.33 = (bf16[48,1536]{1,0:T(8,128)(2,1)}, bf16[48,1536]{1,0:T(8,128)(2,1)}, u32[]{:S(2)}, u32[]{:S(2)}) collective-permute-start(bf16[48,1536]{1,0:T(8,128)(2,1)} %get-tuple-element.218), channel_id=1, source_target_pairs={{0,24},{2,26},{4,28},{6,30},{8,0},{10,2},{12,4},{14,6},{16,8},{18,... | collective-permute-start | bytes 442376 | tf_op jit(solution)/shard_map/ppermute | solution.py:390
  215.2 20.1 %collective-permute-start.28 = (bf16[48,1536]{1,0:T(8,128)(2,1)}, bf16[48,1536]{1,0:T(8,128)(2,1)}, u32[]{:S(2)}, u32[]{:S(2)}) collective-permute-start(bf16[48,1536]{1,0:T(8,128)(2,1)} %get-tuple-element.223), channel_id=1, source_target_pairs={{0,8},{2,10},{4,12},{6,14},{8,16},{10,18},{12,20},{14,22},{16,24},... | collective-permute-start | bytes 442376 | tf_op jit(solution)/shard_map/ppermute | solution.py:390
  216.9 18.4 %collective-permute-start.29 = (bf16[48,1536]{1,0:T(8,128)(2,1)}, bf16[48,1536]{1,0:T(8,128)(2,1)S(1)}, u32[]{:S(2)}, u32[]{:S(2)}) collective-permute-start(bf16[48,1536]{1,0:T(8,128)(2,1)} %get-tuple-element.222), channel_id=1, source_target_pairs={{0,16},{2,18},{4,20},{6,22},{8,24},{10,26},{12,28},{14,30},{16,0},... | collective-permute-start | bytes 442376 | tf_op jit(solution)/shard_map/ppermute | solution.py:390
  (57 other events, 420.9 us)

commit v3 on v2

--- a/solution.py
+++ b/solution.py
@@ -395,8 +395,10 @@
     return (index // 4, (index // 2) % 2, index % 2)
 
 
-def in_bit_order(own, other, bit, axis):
-    return jnp.stack([jnp.where(bit == 0, own, other), jnp.where(bit == 0, other, own)], axis=axis)
+def in_bit_order(own, other, bit):
+    first = jnp.where(bit == 0, own, other)
+    second = jnp.where(bit == 0, other, own)
+    return jnp.concatenate([first, second], axis=0)
 
 
 def far_pieces(shard):
@@ -409,22 +411,20 @@
     stacked = jnp.zeros((far,) + shard.shape, shard.dtype)
     for k, piece in enumerate([shard] + pieces):
         stacked = lax.dynamic_update_slice(stacked, piece[None], ((place - k) % far, 0, 0))
-    return stacked
-
-
-def at_bit(array, bit, axis):
-    return lax.dynamic_index_in_dim(array, bit, axis, False)
+    return stacked.reshape(-1, shard.shape[1])
+
+
+def over_far_bit(array, bit):
+    return lax.ppermute(array, "dp", flip(4 << bit, lax.axis_size("dp")))
+
+
+def part_of(array, index, parts):
+    size = array.shape[0] // parts
+    return lax.dynamic_slice_in_dim(array, index * size, size, 0)
 
 
 def add_low(left, right):
     return (left.astype(HIGH) + right.astype(HIGH)).astype(LOW)
-
-
-def sum_all(vector):
-    count = lax.axis_size("dp")
-    vector = vector + lax.ppermute(vector, "mp", [(0, 1), (1, 0)])
-    vector = sum(far_pieces(vector), vector)
-    return sum((lax.ppermute(vector, "dp", flip(k, count)) for k in range(1, 4)), vector)
 
 
 def head_masks(dtype):
@@ -433,13 +433,27 @@
     return (first.astype(dtype), (1.0 - first).astype(dtype))
 
 
-def put_weights(full_ref, own_ref, other_ref, axis, bit):
-    if axis == 1:
-        full_ref[:, bit] = own_ref[...]
-        full_ref[:, 1 - bit] = other_ref[...]
-    else:
-        full_ref[:, :, bit] = own_ref[...]
-        full_ref[:, :, 1 - bit] = other_ref[...]
+def put_weights(full_ref, own_ref, other_ref, y_first, bit):
+    far, rows = full_ref.shape[0], full_ref.shape[3]
+    for half_ref, at in ((own_ref, bit), (other_ref, 1 - bit)):
+        for near in range(2):
+            for place in range(far):
+                start = (near * far + place) * rows
+                block = half_ref[start : start + rows, :]
+                if y_first:
+                    full_ref[place, near, at] = block
+                else:
+                    full_ref[place, at, near] = block
+
+
+def put_turned(turned_ref, array, x_first, bit):
+    rows = turned_ref.shape[4]
+    turned = array.T
+    for block in range(turned.shape[0] // rows):
+        far, y_bit, x_bit = block // 4, (block // 2) % 2, block % 2
+        first, second = (x_bit, y_bit) if x_first else (y_bit, x_bit)
+        other = 1 - bit if first else bit
+        turned_ref[other, second, far % 2, far // 2] = turned[block * rows : (block + 1) * rows]
 
 
 def matrix(full_ref, start, columns):
@@ -455,7 +469,8 @@
     qk_other_ref,
     vo_own_ref,
     vo_other_ref,
-    turned_ref,
+    turned_x_ref,
+    turned_y_ref,
     q_ref,
     k_ref,
     v_ref,
@@ -468,15 +483,16 @@
 
     @pl.when(pl.program_id(0) == 0)
     def _():
-        put_weights(qk_ref, qk_own_ref, qk_other_ref, 2, place_ref[1])
-        put_weights(vo_ref, vo_own_ref, vo_other_ref, 1, place_ref[0])
+        put_weights(qk_ref, qk_own_ref, qk_other_ref, True, place_ref[1])
+        put_weights(vo_ref, vo_own_ref, vo_other_ref, False, place_ref[0])
         qkv_ref[:, : 2 * width] = matrix(qk_ref, 0, 2 * width)
         qkv_ref[:, 2 * width :] = matrix(vo_ref, 0, width)
         wo_ref[...] = matrix(vo_ref, width, width)
 
     unit, _ = rms_parts(x_ref[...].astype(HIGH))
     normed = (unit * gain_ref[...]).astype(LOW)
-    turned_ref[...] = normed.T
+    put_turned(turned_x_ref, normed, True, place_ref[1])
+    put_turned(turned_y_ref, normed, False, place_ref[0])
     q_ref[...] = matmul_nn(normed, qkv_ref[:, :width]).astype(LOW)
     k_ref[...] = matmul_nn(normed, qkv_ref[:, width : 2 * width]).astype(LOW)
     v_ref[...] = matmul_nn(normed, qkv_ref[:, 2 * width :]).astype(LOW)
@@ -489,8 +505,7 @@
     seq_len = k_ref.shape[0]
     rows = table_ref.shape[1]
     low_masks = head_masks(LOW)
-    masks = head_masks(HIGH)
-    own_lanes = tuple(mask > 0.5 for mask in masks)
+    own_lanes = tuple(mask > 0.5 for mask in head_masks(HIGH))
     for head in range(2):
         row = jnp.broadcast_to(strip_ref[0, head : head + 1, :], (rows, 2 * seq_len))
         table_ref[head] = pltpu.roll(row, 0, 1, stride=1, stride_axis=0)
@@ -502,27 +517,31 @@
     def _():
         acc_ref[...] = jnp.zeros_like(acc_ref)
 
-    for block in range(seq_len // rows):
+    def scored(block, head):
         at = slice(block * rows, (block + 1) * rows)
-        queries = q_ref[at, :]
-        mixed = jnp.zeros((rows, LANES), HIGH)
-        inverse = jnp.zeros((rows, LANES), HIGH)
-        for head in range(2):
-            scores = matmul_nt(queries * low_masks[head], keys)
-            scores = scores + table_ref[head, :, seq_len - block * rows : 2 * seq_len - block * rows]
-            top = jnp.max(scores, axis=-1, keepdims=True)
-            weights = jnp.exp(scores - top).astype(LOW)
-            e_ref[head, at, :] = weights
-            summed = matmul_nn(weights, values_h[head])
-            total = jnp.where(own_lanes[head], pltpu.roll(summed, LANES // 2, 1), 1.0)
-            inv = masks[head] / total
-            mixed = mixed + summed * inv
-            inverse = inverse + inv
-        mixed_ref[at, :] = mixed
-        low = mixed.astype(LOW)
-        low_ref[at, :] = low
-        inv_ref[at, :] = inverse
-        acc_ref[at, :] += matmul_nt(low, wo_ref[...])
+        raw = matmul_nt(q_ref[at, :] * low_masks[head], keys)
+        return raw + table_ref[head, :, seq_len - block * rows : 2 * seq_len - block * rows]
+
+    units = [(block, head) for block in range(seq_len // rows) for head in range(2)]
+    ahead = scored(*units[0])
+    summed = [None, None]
+    for number, (block, head) in enumerate(units):
+        at = slice(block * rows, (block + 1) * rows)
+        scores = ahead
+        if number + 1 < len(units):
+            ahead = scored(*units[number + 1])
+        top = jnp.max(scores, axis=-1, keepdims=True)
+        weights = jnp.exp(scores - top).astype(LOW)
+        e_ref[head, at, :] = weights
+        summed[head] = matmul_nn(weights, values_h[head])
+        if head == 1:
+            totals = jnp.where(own_lanes[0], summed[1], summed[0])
+            inverse = 1.0 / pltpu.roll(totals, LANES // 2, 1)
+            mixed = jnp.where(own_lanes[0], summed[0], summed[1]) * inverse
+            mixed_ref[at, :] = mixed
+            low_ref[at, :] = mixed.astype(LOW)
+            inv_ref[at, :] = inverse
+    acc_ref[...] += matmul_nt(low_ref[...], wo_ref[...])
 
     @pl.when(pair == pl.num_programs(0) - 1)
     def _():
@@ -540,7 +559,8 @@
     gu_other_ref,
     ud_own_ref,
     ud_other_ref,
-    turned_ref,
+    turned_x_ref,
+    turned_y_ref,
     g_turned_ref,
     hidden_ref,
     dgu_ref,
@@ -554,15 +574,16 @@
 
     @pl.when(step == 0)
     def _():
-        put_weights(gu_ref, gu_own_ref, gu_other_ref, 2, place_ref[1])
-        put_weights(ud_ref, ud_own_ref, ud_other_ref, 1, place_ref[0])
+        put_weights(gu_ref, gu_own_ref, gu_other_ref, True, place_ref[1])
+        put_weights(ud_ref, ud_own_ref, ud_other_ref, False, place_ref[0])
 
     attended = x_ref[...].astype(HIGH) + (p_ref[...].astype(HIGH) + r_ref[...].astype(HIGH))
     unit, _ = rms_parts(attended)
     normed = (unit * gain_ref[...]).astype(LOW)
-    turned_ref[...] = normed.T
+    put_turned(turned_x_ref, normed, True, place_ref[1])
+    put_turned(turned_y_ref, normed, False, place_ref[0])
     cotangent = g_ref[...]
-    g_turned_ref[...] = cotangent.T
+    put_turned(g_turned_ref, cotangent, False, place_ref[0])
     root = 0.7978845608028654
     columns = hidden_ref.shape[1] // 2
     out = 0.0
@@ -598,24 +619,24 @@
         own_ref[...] = attended + out
 
 
-def grads_body(
-    first_count, axis, place_ref, left0_ref, left1_ref, right0_ref, right1_ref, own_ref, other_ref, all_ref
-):
+def grads_body(first_count, left0_ref, left1_ref, right0_ref, right1_ref, own_ref, other_ref):
     step = pl.program_id(0)
+    half = own_ref.shape[0]
 
     def product(left_ref, right_ref):
-        grads = matmul_nn(left_ref[...], right_ref[...]).astype(LOW)
-        all_ref[...] = grads.reshape(all_ref.shape)
+        right = right_ref[...]
+        own_ref[...] = matmul_nn(left_ref[:half, :], right).astype(LOW)
+        other_ref[...] = matmul_nn(left_ref[half:, :], right).astype(LOW)
 
     pl.when(step < first_count)(functools.partial(product, left0_ref, right0_ref))
     pl.when(step >= first_count)(functools.partial(product, left1_ref, right1_ref))
-    bit = place_ref[axis - 1]
-    if axis == 1:
-        own_ref[...] = all_ref[:, bit]
-        other_ref[...] = all_ref[:, 1 - bit]
-    else:
-        own_ref[...] = all_ref[:, :, bit]
-        other_ref[...] = all_ref[:, :, 1 - bit]
+
+
+def grads_one_body(left_ref, right_ref, own_ref, other_ref):
+    half = own_ref.shape[0]
+    right = right_ref[...]
+    own_ref[...] = matmul_nn(left_ref[:half, :], right).astype(LOW)
+    other_ref[...] = matmul_nn(left_ref[half:, :], right).astype(LOW)
 
 
 def turn_body(
@@ -640,7 +661,7 @@
     d_gain = jnp.sum(d_normed * unit, axis=0, keepdims=True)
     d_attended = g_ref[...].astype(HIGH) + rms_back(d_normed, unit, scale, gain_ref[...])
     d_low = d_attended.astype(LOW)
-    turned_ref[...] = d_low.T
+    put_turned(turned_ref, d_low, False, place_ref[0])
     dmix_ref[...] = matmul_nn(d_low, wo_ref[...]).astype(LOW)
 
     @pl.when(step == 0)
@@ -756,31 +777,44 @@
     out_ref[...] = (datt_ref[...] + rms_back(d_normed, unit, scale, gain_ref[...])).astype(LOW)
 
 
-def weight_grads(place, first, second, columns, axis, micros):
+def flat_left(left):
+    return left.reshape(-1, left.shape[-1])
+
+
+def weight_grads(first, second, columns, micros):
     left0, right0, at0, count0 = first
     left1, right1, at1, count1 = second
+    left0, left1 = flat_left(left0), flat_left(left1)
     height, depth = left0.shape
     steps = count0 + count1
-    count = lax.axis_size("dp")
-    block = (count // 4, 2, 2, height // count, columns)
-    half = (block[0],) + block[2:]
-    total = half[:-1] + (steps * columns,)
-    half_spec = pl.BlockSpec(half, lambda i, *_: (0, 0, 0, i))
+    half_spec = pl.BlockSpec((height // 2, columns), lambda i: (0, i))
     return call(
-        functools.partial(grads_body, count0, axis),
+        functools.partial(grads_body, count0),
         (steps,),
         [
             whole((height, depth)),
             whole((height, depth)),
-            pl.BlockSpec((depth, columns), lambda i, *_: (0, at0 + jnp.minimum(i, count0 - 1))),
-            pl.BlockSpec((depth, columns), lambda i, *_: (0, at1 + jnp.maximum(i - count0, 0))),
+            pl.BlockSpec((depth, columns), lambda i: (0, at0 + jnp.minimum(i, count0 - 1))),
+            pl.BlockSpec((depth, columns), lambda i: (0, at1 + jnp.maximum(i - count0, 0))),
         ],
         [half_spec, half_spec],
-        [shaped(total, LOW), shaped(total, LOW)],
-        [pltpu.VMEM(block, LOW)],
-        prefetch=1,
+        [shaped((height // 2, steps * columns), LOW)] * 2,
         micros=micros,
-    )(place, left0, left1, right0, right1)
+    )(left0, left1, right0, right1)
+
+
+def weight_grads_one(left, right, columns, steps, micros):
+    left = flat_left(left)
+    height, depth = left.shape
+    half_spec = pl.BlockSpec((height // 2, columns), lambda i: (0, i))
+    return call(
+        grads_one_body,
+        (steps,),
+        [whole((height, depth)), pl.BlockSpec((depth, columns), lambda i: (0, i))],
+        [half_spec, half_spec],
+        [shaped((height // 2, steps * columns), LOW)] * 2,
+        micros=micros,
+    )(left, right)
 
 
 def on_core_pair(
@@ -827,14 +861,14 @@
     late = jnp.concatenate([w_gate, w_up, w_down.T], axis=1)
     early_pieces = far_pieces(early)
     x_other, g_other = swapped(tokens), swapped(cotangent)
-    *early_pieces, late = together(*early_pieces, late)
-    near = far_stack(early, early_pieces)
     late_pieces = far_pieces(late)
-    qk = near[:, :, : 2 * width]
-    vo = near[:, :, 2 * width :]
+    early_pieces = together(*early_pieces)
+    near = far_stack(early, list(early_pieces))
+    qk = near[:, : 2 * width]
+    vo = near[:, 2 * width :]
     qk_next, vo_next = together(over_y(qk), over_x(vo))
-    qk_own = in_bit_order(qk, qk_next, y_bit, 1)
-    vo_own = in_bit_order(vo, vo_next, x_bit, 1)
+    qk_own = in_bit_order(qk, qk_next, y_bit)
+    vo_own = in_bit_order(vo, vo_next, x_bit)
     qk_other = over_x(qk_own)
     vo_other = over_y(vo_own)
     x_all = in_order(tokens, x_other)
@@ -843,8 +877,8 @@
         qk_other, vo_other, x_all, g_all, *late_pieces
     )
     near = far_stack(late, late_pieces)
-    gu = near[:, :, : 3 * chunk]
-    ud = near[:, :, 3 * chunk :]
+    gu = near[:, : 3 * chunk]
+    ud = near[:, 3 * chunk :]
     gu_next = over_y(gu)
     ud_next = over_x(ud)
 
@@ -860,17 +894,19 @@
     def row_block(columns):
         return pl.BlockSpec((rows, columns), lambda i, *_: (i, 0))
 
-    turned_block = pl.BlockSpec((features, rows), lambda i, *_: (0, i))
+    turned_shape = (2, 2, 2, 2, block_rows)
+    turned_block = pl.BlockSpec(turned_shape + (rows,), lambda i, *_: (0, 0, 0, 0, 0, i))
+    turned = shaped(turned_shape + (seq_len,), LOW)
     full_block = (count // 4, 2, 2, block_rows, 2 * width)
-    half_block = (count // 4, 2, block_rows, 2 * width)
-    normed_turned, queries, keys, values, w_qkv, w_o = call(
+    half_block = (features // 2, 2 * width)
+    normed_x_turned, normed_y_turned, queries, keys, values, w_qkv, w_o = call(
         project_body,
         (steps,),
         [row_block(features), whole((1, features))] + [whole(half_block)] * 4,
-        [turned_block]
+        [turned_block, turned_block]
         + [row_block(width)] * 3
         + [result((features, 3 * width)), result((features, width))],
-        [shaped((features, seq_len), LOW)]
+        [turned, turned]
         + [shaped((seq_len, width), LOW)] * 3
         + [shaped((features, 3 * width), LOW), shaped((features, width), LOW)],
         [pltpu.VMEM(full_block, LOW), pltpu.VMEM(full_block, LOW)],
@@ -879,8 +915,8 @@
     )(place, x_all, gain_a, qk_own, qk_other, vo_own, vo_other)
 
     gu_next, ud_next, queries = together(gu_next, ud_next, queries)
-    gu_own = in_bit_order(gu, gu_next, y_bit, 1)
-    ud_own = in_bit_order(ud, ud_next, x_bit, 1)
+    gu_own = in_bit_order(gu, gu_next, y_bit)
+    ud_own = in_bit_order(ud, ud_next, x_bit)
     gu_other = over_x(gu_own)
     ud_other = over_y(ud_own)
 
@@ -918,16 +954,19 @@
     def turned_row(columns):
         return pl.BlockSpec((rows, columns), lambda i, m: (moved(i, m), 0))
 
-    moved_block = pl.BlockSpec((features, rows), lambda i, m: (0, moved(i, m)))
+    moved_block = pl.BlockSpec(
+        turned_shape + (rows,), lambda i, m: (0, 0, 0, 0, 0, moved(i, m))
+    )
     send_row = pl.BlockSpec((rows, features), lambda i, m: (jnp.minimum(i, half_steps - 1), 0))
     keep_row = pl.BlockSpec((rows, features), lambda i, m: (jnp.maximum(i - half_steps, 0), 0))
     full_block = (count // 4, 2, 2, block_rows, 3 * chunk)
-    half_block = (count // 4, 2, block_rows, 3 * chunk)
-    normed_f_turned, g_turned, hidden, d_gate_up, dn_part, out_send, out_own = call(
+    half_block = (features // 2, 3 * chunk)
+    feed_x_turned, feed_y_turned, g_turned, hidden, d_gate_up, dn_part, out_send, out_own = call(
         feed_body,
         (steps,),
         [turned_row(features)] * 4 + [whole((1, features))] + [whole(half_block)] * 4,
         [
+            moved_block,
             moved_block,
             moved_block,
             turned_row(units),
@@ -937,8 +976,9 @@
             keep_row,
         ],
         [
-            shaped((features, seq_len), LOW),
-            shaped((features, seq_len), LOW),
+            turned,
+            turned,
+            turned,
             shaped((seq_len, units), LOW),
             shaped((seq_len, 2 * units), LOW),
             shaped((seq_len, features), LOW),
@@ -951,13 +991,11 @@
     )(place, x_all, part, part_other, g_all, gain_f, gu_own, gu_other, ud_own, ud_other)
     dn_other = swapped(dn_part)
 
-    gu_own, gu_send = weight_grads(
-        place, (normed_f_turned, d_gate_up, 0, 2), (normed_f_turned, d_gate_up, 2, 1), chunk, 2, 6
-    )
+    gu_own, gu_send = weight_grads_one(feed_x_turned, d_gate_up, 3 * chunk // 2, 2, 5.5)
     gu_send, hidden, dn_other = together(gu_send, hidden, dn_other)
     gu_came = over_x(gu_send)
     ud_own, ud_send = weight_grads(
-        place, (normed_f_turned, d_gate_up, 3, 1), (g_turned, hidden, 0, 2), chunk, 1, 6
+        (feed_y_turned, d_gate_up, 3, 1), (g_turned, hidden, 0, 2), chunk, 6.5
     )
     ud_send, dn_other = together(ud_send, dn_other)
     ud_came = over_y(ud_send)
@@ -969,7 +1007,7 @@
         [keep_row, moved_block, turned_row(width), result((1, features))],
         [
             shaped((own_rows, features), HIGH),
-            shaped((features, seq_len), LOW),
+            turned,
             shaped((seq_len, width), LOW),
             shaped((1, features), HIGH),
         ],
@@ -994,8 +1032,8 @@
 
     def next_half(own, came, bit):
         return (
-            add_low(at_bit(own, bit, 1), at_bit(came, bit, 1)),
-            add_low(at_bit(own, 1 - bit, 1), at_bit(came, 1 - bit, 1)),
+            add_low(part_of(own, bit, 2), part_of(came, bit, 2)),
+            add_low(part_of(own, 1 - bit, 2), part_of(came, 1 - bit, 2)),
         )
 
     gu_own, gu_send = next_half(gu_own, gu_came, y_bit)
@@ -1004,26 +1042,24 @@
     ud_came = over_x(ud_send)
 
     qk_own, qk_send = weight_grads(
-        place, (normed_turned, d_query, 0, 1), (normed_turned, d_key, 0, 1), width, 2, 5
+        (normed_x_turned, d_query, 0, 1), (normed_x_turned, d_key, 0, 1), width, 5
     )
     qk_send, d_value = together(qk_send, d_value)
     vo_own, vo_send = weight_grads(
-        place, (normed_turned, d_value, 0, 1), (d_low_turned, mixed_low, 0, 1), width, 1, 5
+        (normed_y_turned, d_value, 0, 1), (d_low_turned, mixed_low, 0, 1), width, 5
     )
     output = (out_own + out_other.astype(HIGH)).astype(LOW)
-
-    def far_sums(own, came):
-        total = add_low(own, came)
-        pieces = [over_far(at_bit(total, (far_bit + k) % (count // 4), 0), k) for k in range(1, count // 4)]
-        return (at_bit(total, far_bit, 0), pieces)
 
     gu_came, ud_came, qk_send, vo_send, d_query = together(
         gu_came, ud_came, qk_send, vo_send, d_query
     )
     qk_came = over_x(qk_send)
     vo_came = over_y(vo_send)
-    gu_kept, gu_pieces = far_sums(gu_own, gu_came)
-    ud_kept, ud_pieces = far_sums(ud_own, ud_came)
+    gu_own, gu_send = next_half(gu_own, gu_came, far_bit % 2)
+    ud_own, ud_send = next_half(ud_own, ud_came, far_bit % 2)
+    unit_own = jnp.concatenate([gu_own, ud_own], axis=1)
+    unit_send = jnp.concatenate([gu_send, ud_send], axis=1)
+    unit_came = over_far_bit(unit_send, 0)
 
     dna_send, dna_own, d_gain_a = call(
         spread_body,
@@ -1038,9 +1074,11 @@
         prefetch=1,
         micros=7,
     )(place, x_all, d_query, d_key, d_value, w_qkv)
-    qk_came, vo_came, dna_send, d_gain_a, d_strip = together(
-        qk_came, vo_came, dna_send, d_gain_a, d_strip
-    )
+    qk_came, vo_came, unit_came, dna_send, d_gain_a, d_strip = together(
+        qk_came, vo_came, unit_came, dna_send, d_gain_a, d_strip
+    )
+    unit_own, unit_send = next_half(unit_own, unit_came, far_bit // 2)
+    unit_came = over_far_bit(unit_send, 1)
     dna_other = swapped(dna_send)
     qk_own, qk_send = next_half(qk_own, qk_came, y_bit)
     vo_own, vo_send = next_half(vo_own, vo_came, x_bit)
@@ -1056,7 +1094,9 @@
         [d_gain_a.reshape(features), 0.5 * d_gain_f.reshape(features), d_table.reshape(-1)]
     )
     small = jnp.pad(small, (0, -small.shape[0] % 1024)).reshape(-1, LANES)
-    small = sum_all(small).reshape(-1)
+    small = small + swapped(small)
+    small = small + over_x(small)
+    small = small + over_y(small)
 
     d_tokens = call(
         finish_body,
@@ -1067,18 +1107,22 @@
         micros=3.5,
     )(tokens, dna_own, dna_other, d_attended, gain_a)
 
-    qk_came, vo_came, d_tokens, *far_came = together(
-        qk_came, vo_came, d_tokens, *gu_pieces, *ud_pieces
-    )
-    gu_pieces, ud_pieces = far_came[: len(gu_pieces)], far_came[len(gu_pieces) :]
-    qk_kept, qk_pieces = far_sums(qk_own, qk_came)
-    vo_kept, vo_pieces = far_sums(vo_own, vo_came)
-
-    def summed(kept, pieces):
-        return sum((piece.astype(HIGH) for piece in pieces), kept.astype(HIGH))
-
-    grads_gu, grads_ud = summed(gu_kept, gu_pieces), summed(ud_kept, ud_pieces)
-    grads_qk, grads_vo = summed(qk_kept, qk_pieces), summed(vo_kept, vo_pieces)
+    qk_came, vo_came, unit_came, d_tokens, small = together(
+        qk_came, vo_came, unit_came, d_tokens, small
+    )
+    head_own = jnp.concatenate([qk_own, vo_own], axis=-1)
+    head_came = jnp.concatenate([qk_came, vo_came], axis=-1)
+    total = add_low(head_own, head_came)
+
+    def far_part(far):
+        return part_of(total, 2 * (far % 2) + far // 2, 4)
+
+    pieces = [over_far(far_part((far_bit + k) % 4), k) for k in range(1, 4)]
+    small = small + over_far_bit(small, 0)
+    small = (small + over_far_bit(small, 1)).reshape(-1)
+    grads_head = sum((piece.astype(HIGH) for piece in pieces), far_part(far_bit).astype(HIGH))
+    grads_qk, grads_vo = grads_head[:, : 2 * width], grads_head[:, 2 * width :]
+    grads_unit = unit_own.astype(HIGH) + unit_came.astype(HIGH)
     return (
         output,
         d_tokens,
@@ -1089,9 +1133,9 @@
         grads_vo[:, width:].T,
         small[2 * features : 2 * features + rel_table.size].reshape(rel_table.shape),
         small[features : 2 * features],
-        grads_gu[:, :units],
-        jnp.concatenate([grads_gu[:, units:], grads_ud[:, :chunk]], axis=1),
-        grads_ud[:, chunk:].T,
+        grads_unit[:, :units],
+        grads_unit[:, units : 2 * units],
+        grads_unit[:, 2 * units :].T,
     )
 
 
@@ -1111,7 +1155,7 @@
         P("dp", "mp"),
         P("mp", "dp"),
     )
-    paired = mesh.shape["mp"] == 2 and mesh.shape["dp"] % 4 == 0
+    paired = mesh.shape["mp"] == 2 and mesh.shape["dp"] == 16
     body = on_core_pair if paired else on_device
     return jax.shard_map(
         body,

time: 255 us -> 226 us (0.89)
  starting transfers between devices: 67.4 us -> 53.9 us
  Pallas kernels: 114 us -> 106 us
  local copies, waits for them, and re-layouts: 15 us -> 8.78 us
  other arithmetic: 14.6 us -> 10.5 us
  waiting for transfers between devices: 40.7 us -> 43.7 us
    ppermute x21 -> x9, starting transfers between devices: 42.1 us -> 26.6 us  [over_far(): return lax.ppermute(array, 'dp', ring_shift(4 * steps, lax.axis_size('dp')))]
    ppermute x21 -> x9, waiting for transfers between devices: 21.1 us -> 9.24 us  [over_far(): return lax.ppermute(array, 'dp', ring_shift(4 * steps, lax.axis_size('dp')))]
    ppermute x4, waiting for transfers between devices: 0.01 us -> 9.95 us  [over_far_bit(): return lax.ppermute(array, 'dp', flip(4 << bit, lax.axis_size('dp')))]
    pallas_call x4, Pallas kernels: 28.2 us -> 23.4 us  [the longest x3 17.9 us: weight_grads(): call(functools.partial(grads_body, count0), (steps,), [whole((height, dep...]
    pallas_call x1, Pallas kernels: 21.9 us -> 17.6 us  [on_core_pair(): call(attend_body, (pairs,), [pair_block, pair_block, pair_block, strip_bl...]
    ppermute x8 -> x9, waiting for transfers between devices: 12.3 us -> 16.1 us  [over_y(): return lax.ppermute(array, 'dp', flip(2, lax.axis_size('dp')))]
    ppermute x8 -> x9, starting transfers between devices: 7.44 us -> 9.55 us  [over_y(): return lax.ppermute(array, 'dp', flip(2, lax.axis_size('dp')))]
    ppermute x8 -> x9, waiting for transfers between devices: 6.47 us -> 5.4 us  [over_x(): return lax.ppermute(array, 'dp', flip(1, lax.axis_size('dp')))]
  transfers between devices with their start and end apart: 47 -> 38, of which waited for: 19 -> 22; matrix products, arithmetic and copies ran while one was open for 8% -> 5% of each run, Pallas kernels for 37% -> 38%
where the time goes in v3:
time: 226 us; the launch traced here: 225 us
  Pallas kernels  106 us (47%)
  starting transfers between devices  53.9 us (24%)
  waiting for transfers between devices  43.7 us (19%)
  other arithmetic  10.5 us (5%)
  local copies, waits for them, and re-layouts  8.78 us (4%)
    ppermute x9, starting transfers between devices, over_far(): return lax.ppermute(array, 'dp', ring_shift(4 * steps, lax.axis_size('dp')))  26.6 us
    pallas_call x1, Pallas kernels, on_core_pair(): call(feed_body, (steps,), [turned_row(features)] * 4 + [whole((1, feature...  19.6 us
    pallas_call x3, Pallas kernels, weight_grads(): call(functools.partial(grads_body, count0), (steps,), [whole((height, dep...  17.9 us
    pallas_call x1, Pallas kernels, on_core_pair(): call(attend_body, (pairs,), [pair_block, pair_block, pair_block, strip_bl...  17.6 us
    pallas_call x1, Pallas kernels, on_core_pair(): call(backward_body, (pairs,), [pair_block, pair_block, pair_block, e_bloc...  16.4 us
    ppermute x9, waiting for transfers between devices, over_y(): return lax.ppermute(array, 'dp', flip(2, lax.axis_size('dp')))  16.1 us
    ppermute x9, starting transfers between devices, over_x(): return lax.ppermute(array, 'dp', flip(1, lax.axis_size('dp')))  12.4 us
    ppermute x4, waiting for transfers between devices, over_far_bit(): return lax.ppermute(array, 'dp', flip(4 << bit, lax.axis_size('dp')))  9.95 us
  transfers between devices with their start and end apart: 38, of which 22 were waited for; matrix products, arithmetic and copies ran while one was open for 5% of the time, Pallas kernels for 38%

profile of v3, /device:TPU:0, one launch (start us, length us, event | category | flops | bytes accessed | tf_op | source)
XLA Modules:
  0.0 225.1 jit_solution(14917291625108279442)
XLA Ops:
  1.7 3.1 %collective-permute-start = (bf16[48,1536]{1,0:T(8,128)(2,1)S(1)}, bf16[48,1536]{1,0:T(8,128)(2,1)S(1)}, u32[]{:S(2)}, u32[]{:S(2)}) collective-permute-start(bf16[48,1536]{1,0:T(8,128)(2,1)S(1)} %pad_maximum_fusion.8), channel_id=1, source_target_pairs={{0,8},{2,10},{4,12},{6,14},{8,16},{10,18},{12,20},{14,22},{16,24},... | collective-permute-start | bytes 442376 | tf_op jit(solution)/shard_map/ppermute | solution.py:390
  4.7 2.6 %collective-permute-start.1 = (bf16[48,1536]{1,0:T(8,128)(2,1)S(1)}, bf16[48,1536]{1,0:T(8,128)(2,1)S(1)}, u32[]{:S(2)}, u32[]{:S(2)}) collective-permute-start(bf16[48,1536]{1,0:T(8,128)(2,1)S(1)} %pad_maximum_fusion.8), channel_id=1, source_target_pairs={{0,16},{2,18},{4,20},{6,22},{8,24},{10,26},{12,28},{14,30},{16,0},... | collective-permute-start | bytes 442376 | tf_op jit(solution)/shard_map/ppermute | solution.py:390
  13.0 9.0 %collective-permute-start.10 = (bf16[48,3072]{1,0:T(8,128)(2,1)S(1)}, bf16[48,3072]{1,0:T(8,128)(2,1)S(1)}, u32[]{:S(2)}, u32[]{:S(2)}) collective-permute-start(bf16[48,3072]{1,0:T(8,128)(2,1)S(1)} %pad_maximum_fusion.7), channel_id=1, source_target_pairs={{0,16},{2,18},{4,20},{6,22},{8,24},{10,26},{12,28},{14,30},{16,0},... | collective-permute-start | bytes 884744 | tf_op jit(solution)/shard_map/ppermute | solution.py:390
  25.3 3.6 %collective-permute-done.3 = bf16[192,768]{1,0:T(8,128)(2,1)S(1)} collective-permute-done((bf16[192,768]{1,0:T(8,128)(2,1)S(1)}, bf16[192,768]{1,0:T(8,128)(2,1)S(1)}, u32[]{:S(2)}, u32[]{:S(2)}) %collective-permute-start.3) | collective-permute-done | bytes 294944 | tf_op jit(solution)/shard_map/ppermute | solution.py:386
  28.9 4.1 %collective-permute-start.11 = (bf16[48,3072]{1,0:T(8,128)(2,1)S(1)}, bf16[48,3072]{1,0:T(8,128)(2,1)S(1)}, u32[]{:S(2)}, u32[]{:S(2)}) collective-permute-start(bf16[48,3072]{1,0:T(8,128)(2,1)S(1)} %pad_maximum_fusion.7), channel_id=1, source_target_pairs={{0,24},{2,26},{4,28},{6,30},{8,0},{10,2},{12,4},{14,6},{16,8},{18,... | collective-permute-start | bytes 884744 | tf_op jit(solution)/shard_map/ppermute | solution.py:390
  41.0 4.8 %collective-permute-done.9 = bf16[48,3072]{1,0:T(8,128)(2,1)S(1)} collective-permute-done((bf16[48,3072]{1,0:T(8,128)(2,1)S(1)}, bf16[48,3072]{1,0:T(8,128)(2,1)S(1)}, u32[]{:S(2)}, u32[]{:S(2)}) %collective-permute-start.9) | collective-permute-done | bytes 294944 | tf_op jit(solution)/shard_map/ppermute | solution.py:390
  45.8 2.4 %collective-permute-done.6.vo_other_ref = bf16[384,768]{1,0:T(8,128)(2,1)S(1)} collective-permute-done((bf16[384,768]{1,0:T(8,128)(2,1)S(1)}, bf16[384,768]{1,0:T(8,128)(2,1)S(1)}, u32[]{:S(2)}, u32[]{:S(2)}) %collective-permute-start.6) | collective-permute-done | bytes 589856 | tf_op jit(solution)/shard_map/ppermute | solution.py:386
  52.3 8.7 %shard_map.220 = (bf16[2,2,2,2,48,1024]{5,4,3,2,1,0:T(8,128)(2,1)}, bf16[2,2,2,2,48,1024]{5,4,3,2,1,0:T(8,128)(2,1)}, bf16[1024,384]{1,0:T(8,128)(2,1)}, bf16[10...) custom-call(s32[4]{0:T(128)} %pad_add_fusion.place_ref, ...), custom_call_target="tpu_custom_call" | custom-call | flops 8074500096 | tf_op jit(solution)/shard_map/pallas_call | solution.py:902
  65.8 17.6 %shard_map.221 = (bf16[6,1024,1024]{2,1,0:T(8,128)(2,1)}, f32[1024,384]{1,0:T(8,128)}, bf16[1024,384]{1,0:T(8,128)(2,1)}, f32[1024,384]{1,0:T(8,128)}, bf16[1024,768]{1,0:T(8,128)(2,1)}) custom-call(bf16[1024,384]{1,0:T(8,128)(2,1)} %get-tuple-element.113.q_ref, bf16[1024,384]{1,0:T(8,128)(2,1)} %get-tuple-element.114.k_ref, ...), custom_call_target="tpu_custom_call" | custom-call | flops 23069999104 | tf_op jit(solution)/shard_map/pallas_call | solution.py:927
  83.4 3.9 %collective-permute-done.15.ud_other_ref = bf16[384,1536]{1,0:T(8,128)(2,1)S(1)} collective-permute-done((bf16[384,1536]{1,0:T(8,128)(2,1)S(1)}, bf16[384,1536]{1,0:T(8,128)(2,1)S(1)}, u32[]{:S(2)}, u32[]{:S(2)}) %collective-permute-start.15) | collective-permute-done | bytes 1179680 | tf_op jit(solution)/shard_map/ppermute | solution.py:386
  88.9 3.0 %collective-permute-done.16.r_ref = bf16[1024,768]{1,0:T(8,128)(2,1)S(1)} collective-permute-done((bf16[1024,768]{1,0:T(8,128)(2,1)}, bf16[1024,768]{1,0:T(8,128)(2,1)S(1)}, u32[]{:S(2)}, u32[]{:S(2)}) %collective-permute-start.16) | collective-permute-done | bytes 1572896 | tf_op jit(solution)/shard_map/ppermute | solution.py:853
  93.1 19.6 %shard_map.222 = (bf16[2,2,2,2,48,1024]{5,4,3,2,1,0:T(8,128)(2,1)}, bf16[2,2,2,2,48,1024]{5,4,3,2,1,0:T(8,128)(2,1)}, bf16[2,2,2,2,48,1024]{5,4,3,2,1,0:T(8,128)...) custom-call(s32[4]{0:T(128)} %pad_add_fusion.place_ref, ...), custom_call_target="tpu_custom_call" | custom-call | flops 21916499968 | tf_op jit(solution)/shard_map/pallas_call | solution.py:964
  113.3 5.6 %shard_map.223 = (bf16[384,1536]{1,0:T(8,128)(2,1)}, bf16[384,1536]{1,0:T(8,128)(2,1)}) custom-call(bf16[768,1024]{1,0:T(8,128)(2,1)} %bitcast.58, bf16[1024,2048]{1,0:T(8,128)(2,1)} %get-tuple-element.124.right_ref.right0_ref), custom_call_target="tpu_custom_call" | custom-call | flops 6344249856 | tf_op jit(solution)/shard_map/pallas_call | solution.py:810
  118.8 7.3 %shard_map.224 = (bf16[384,1536]{1,0:T(8,128)(2,1)}, bf16[384,1536]{1,0:T(8,128)(2,1)}) custom-call(bf16[768,1024]{1,0:T(8,128)(2,1)} %bitcast.56, bf16[768,1024]{1,0:T(8,128)(2,1)} %bitcast.57, bf16[1024,2048]{1,0:T(8,128)(2,1)} %get-tuple-element.124.right_ref.right0_ref, bf16[1024,1024]{1,0:T(8,128)(2,1)} %get-tuple-element.131.right1_ref), custom_call_target="tpu_custom_call" | custom-call | flops 7497750016 | tf_op jit(solution)/shard_map/pallas_call | solution.py:791
  128.5 8.5 %shard_map.225 = (f32[512,768]{1,0:T(8,128)}, bf16[2,2,2,2,48,1024]{5,4,3,2,1,0:T(8,128)(2,1)}, bf16[1024,384]{1,0:T(8,128)(2,1)}, f32[1,768]{1,0:T(1,128)}) custom-call(s32[4]{0:T(128)} %pad_add_fusion.place_ref, bf16[1024,768]{1,0:T(8,128)(2,1)} %pad_maximum_fusion.x_ref, bf16[1024,768]{1,0:T(8,128)(2,1)} %get-tuple-element.118.p_ref, ...), custom_call_target="tpu_custom_call" | custom-call | flops 9228000256 | tf_op jit(solution)/shard_map/pallas_call | solution.py:1003
  137.0 16.4 %shard_map.226 = (bf16[1024,384]{1,0:T(8,128)(2,1)}, bf16[1024,384]{1,0:T(8,128)(2,1)}, bf16[1024,384]{1,0:T(8,128)(2,1)}, f32[3,2,2048]{2,1,0:T(2,128)}) custom-call(bf16[1024,384]{1,0:T(8,128)(2,1)} %get-tuple-element.113.q_ref, bf16[1024,384]{1,0:T(8,128)(2,1)} %get-tuple-element.114.k_ref, bf16[1024,384]{1,0:T(8,128)(2,1)} %get-tuple-element.115.v_ref, ...), custom_call_target="tpu_custom_call" | custom-call | flops 18456000512 | tf_op jit(solution)/shard_map/pallas_call | solution.py:1019
  158.3 5.4 %shard_map.227 = (bf16[384,768]{1,0:T(8,128)(2,1)}, bf16[384,768]{1,0:T(8,128)(2,1)}) custom-call(bf16[768,1024]{1,0:T(8,128)(2,1)} %bitcast.54, bf16[768,1024]{1,0:T(8,128)(2,1)} %bitcast.55, bf16[1024,384]{1,0:T(8,128)(2,1)} %get-tuple-element.166.right0_ref.dq_ref, bf16[1024,384]{1,0:T(8,128)(2,1)} %get-tuple-element.148.right1_ref.dk_ref), custom_call_target="tpu_custom_call" | custom-call | flops 5767499776 | tf_op jit(solution)/shard_map/pallas_call | solution.py:791
  164.7 5.2 %shard_map.228 = (bf16[384,768]{1,0:T(8,128)(2,1)}, bf16[384,768]{1,0:T(8,128)(2,1)}) custom-call(bf16[768,1024]{1,0:T(8,128)(2,1)} %bitcast.53, bf16[768,1024]{1,0:T(8,128)(2,1)} %bitcast.59, bf16[1024,384]{1,0:T(8,128)(2,1)} %get-tuple-element.159.right0_ref.dv_ref, bf16[1024,384]{1,0:T(8,128)(2,1)} %get-tuple-element.160.right1_ref), custom_call_target="tpu_custom_call" | custom-call | flops 5767499776 | tf_op jit(solution)/shard_map/pallas_call | solution.py:791
  175.4 7.8 %shard_map.229 = (bf16[512,768]{1,0:T(8,128)(2,1)}, f32[512,768]{1,0:T(8,128)}, f32[1,768]{1,0:T(1,128)}) custom-call(s32[4]{0:T(128)} %pad_add_fusion.place_ref, bf16[1024,768]{1,0:T(8,128)(2,1)} %pad_maximum_fusion.x_ref, bf16[1024,384]{1,0:T(8,128)(2,1)} %get-tuple-element.166.right0_ref.dq_ref, bf16[1024,384]{1,0:T(8,128)(2,1)} %get-tuple-element.148.right1_ref.dk_ref, ...), custom_call_target="tpu_custom_call" | custom-call | flops 8074500096 | tf_op jit(solution)/shard_map/pallas_call | solution.py:1064
  200.2 3.4 %shard_map.230 = bf16[512,768]{1,0:T(8,128)(2,1)} custom-call(bf16[512,768]{1,0:T(8,128)(2,1)} %x_ref.1, f32[512,768]{1,0:T(8,128)} %get-tuple-element.175.own_ref, bf16[512,768]{1,0:T(8,128)(2,1)} %copy-done.28, f32[512,768]{1,0:T(8,128)} %get-tuple-element.177.datt_ref, f32[1,768]{1,0:T(1,128)} %reshape.84.gain_ref), custom_call_target="tpu_custom_call" | custom-call | flops 4037250048 | tf_op jit(solution)/shard_map/pallas_call | solution.py:1101
  203.7 2.6 %collective-permute-done.28 = bf16[48,3072]{1,0:T(8,128)(2,1)S(1)} collective-permute-done((bf16[48,3072]{1,0:T(8,128)(2,1)S(1)}, bf16[48,3072]{1,0:T(8,128)(2,1)S(1)}, u32[]{:S(2)}, u32[]{:S(2)}) %collective-permute-start.28) | collective-permute-done | bytes 294944 | tf_op jit(solution)/shard_map/ppermute | solution.py:418
  207.4 3.5 %collective-permute-done.33 = f32[16,128]{1,0:T(8,128)S(1)} collective-permute-done((f32[16,128]{1,0:T(8,128)S(1)}, f32[16,128]{1,0:T(8,128)S(1)}, u32[]{:S(2)}, u32[]{:S(2)}) %collective-permute-start.33) | collective-permute-done | bytes 8224 | tf_op jit(solution)/shard_map/ppermute | solution.py:418
  214.0 2.8 %collective-permute-start.37 = (bf16[48,1536]{1,0:T(8,128)(2,1)S(1)}, bf16[48,1536]{1,0:T(8,128)(2,1)S(1)}, u32[]{:S(2)}, u32[]{:S(2)}) collective-permute-start(bf16[48,1536]{1,0:T(8,128)(2,1)S(1)} %get-tuple-element.230), channel_id=1, source_target_pairs={{0,24},{2,26},{4,28},{6,30},{8,0},{10,2},{12,4},{14,6},{16,8},{18,... | collective-permute-start | bytes 442376 | tf_op jit(solution)/shard_map/ppermute | solution.py:390
  220.3 4.0 %collective-permute-done.36 = bf16[48,1536]{1,0:T(8,128)(2,1)S(1)} collective-permute-done((bf16[48,1536]{1,0:T(8,128)(2,1)S(1)}, bf16[48,1536]{1,0:T(8,128)(2,1)S(1)}, u32[]{:S(2)}, u32[]{:S(2)}) %collective-permute-start.36) | collective-permute-done | bytes 147488 | tf_op jit(solution)/shard_map/ppermute | solution.py:390
  (190 shorter events, 68.8 us)
Async XLA Ops:
  1.7 11.3 %collective-permute-start = (bf16[48,1536]{1,0:T(8,128)(2,1)S(1)}, bf16[48,1536]{1,0:T(8,128)(2,1)S(1)}, u32[]{:S(2)}, u32[]{:S(2)}) collective-permute-start(bf16[48,1536]{1,0:T(8,128)(2,1)S(1)} %pad_maximum_fusion.8), channel_id=1, source_target_pairs={{0,8},{2,10},{4,12},{6,14},{8,16},{10,18},{12,20},{14,22},{16,24},... | collective-permute-start | bytes 442376 | tf_op jit(solution)/shard_map/ppermute | solution.py:390
  4.7 17.2 %collective-permute-start.1 = (bf16[48,1536]{1,0:T(8,128)(2,1)S(1)}, bf16[48,1536]{1,0:T(8,128)(2,1)S(1)}, u32[]{:S(2)}, u32[]{:S(2)}) collective-permute-start(bf16[48,1536]{1,0:T(8,128)(2,1)S(1)} %pad_maximum_fusion.8), channel_id=1, source_target_pairs={{0,16},{2,18},{4,20},{6,22},{8,24},{10,26},{12,28},{14,30},{16,0},... | collective-permute-start | bytes 442376 | tf_op jit(solution)/shard_map/ppermute | solution.py:390
  7.3 14.6 %collective-permute-start.2 = (bf16[48,1536]{1,0:T(8,128)(2,1)S(1)}, bf16[48,1536]{1,0:T(8,128)(2,1)S(1)}, u32[]{:S(2)}, u32[]{:S(2)}) collective-permute-start(bf16[48,1536]{1,0:T(8,128)(2,1)S(1)} %pad_maximum_fusion.8), channel_id=1, source_target_pairs={{0,24},{2,26},{4,28},{6,30},{8,0},{10,2},{12,4},{14,6},{16,8},{18,... | collective-permute-start | bytes 442376 | tf_op jit(solution)/shard_map/ppermute | solution.py:390
  8.7 25.7 %collective-permute-start.7 = (bf16[512,768]{1,0:T(8,128)(2,1)}, bf16[512,768]{1,0:T(8,128)(2,1)S(1)}, u32[]{:S(2)}, u32[]{:S(2)}) collective-permute-start(bf16[512,768]{1,0:T(8,128)(2,1)} %x_ref.1), channel_id=1, source_target_pairs={{0,1},{1,0},{2,3},{3,2},{4,5},{5,4},{6,7},{7,6},{8,9},{9,8},{10,11... | collective-permute-start | bytes 2359304 | tf_op jit(solution)/shard_map/ppermute | solution.py:853
  8.7 26.3 %collective-permute-start.8 = (bf16[512,768]{1,0:T(8,128)(2,1)}, bf16[512,768]{1,0:T(8,128)(2,1)}, u32[]{:S(2)}, u32[]{:S(2)}) collective-permute-start(bf16[512,768]{1,0:T(8,128)(2,1)} %param.14), channel_id=1, source_target_pairs={{0,1},{1,0},{2,3},{3,2},{4,5},{5,4},{6,7},{7,6},{8,9},{9,8},{10,11... | collective-permute-start | bytes 2359304 | tf_op jit(solution)/shard_map/ppermute | solution.py:853
  13.0 27.5 %collective-permute-start.10 = (bf16[48,3072]{1,0:T(8,128)(2,1)S(1)}, bf16[48,3072]{1,0:T(8,128)(2,1)S(1)}, u32[]{:S(2)}, u32[]{:S(2)}) collective-permute-start(bf16[48,3072]{1,0:T(8,128)(2,1)S(1)} %pad_maximum_fusion.7), channel_id=1, source_target_pairs={{0,16},{2,18},{4,20},{6,22},{8,24},{10,26},{12,28},{14,30},{16,0},... | collective-permute-start | bytes 884744 | tf_op jit(solution)/shard_map/ppermute | solution.py:390
  28.9 12.1 %collective-permute-start.11 = (bf16[48,3072]{1,0:T(8,128)(2,1)S(1)}, bf16[48,3072]{1,0:T(8,128)(2,1)S(1)}, u32[]{:S(2)}, u32[]{:S(2)}) collective-permute-start(bf16[48,3072]{1,0:T(8,128)(2,1)S(1)} %pad_maximum_fusion.7), channel_id=1, source_target_pairs={{0,24},{2,26},{4,28},{6,30},{8,0},{10,2},{12,4},{14,6},{16,8},{18,... | collective-permute-start | bytes 884744 | tf_op jit(solution)/shard_map/ppermute | solution.py:390
  32.9 12.8 %collective-permute-start.9 = (bf16[48,3072]{1,0:T(8,128)(2,1)S(1)}, bf16[48,3072]{1,0:T(8,128)(2,1)S(1)}, u32[]{:S(2)}, u32[]{:S(2)}) collective-permute-start(bf16[48,3072]{1,0:T(8,128)(2,1)S(1)} %pad_maximum_fusion.7), channel_id=1, source_target_pairs={{0,8},{2,10},{4,12},{6,14},{8,16},{10,18},{12,20},{14,22},{16,24},... | collective-permute-start | bytes 884744 | tf_op jit(solution)/shard_map/ppermute | solution.py:390
  34.4 13.8 %collective-permute-start.6 = (bf16[384,768]{1,0:T(8,128)(2,1)S(1)}, bf16[384,768]{1,0:T(8,128)(2,1)S(1)}, u32[]{:S(2)}, u32[]{:S(2)}) collective-permute-start(bf16[384,768]{1,0:T(8,128)(2,1)S(1)} %pad_maximum_fusion.5.vo_own_ref), channel_id=1, source_target_pairs={{0,4},{2,6},{4,0},{6,2},{8,12},{10,14},{12,8},{14,10},{16,20},{18,... | collective-permute-start | bytes 1769480 | tf_op jit(solution)/shard_map/ppermute | solution.py:386
  35.0 13.5 %collective-permute-start.5 = (bf16[384,768]{1,0:T(8,128)(2,1)S(1)}, bf16[384,768]{1,0:T(8,128)(2,1)S(1)}, u32[]{:S(2)}, u32[]{:S(2)}) collective-permute-start(bf16[384,768]{1,0:T(8,128)(2,1)S(1)} %pad_maximum_fusion.4.qk_own_ref), channel_id=1, source_target_pairs={{0,2},{2,0},{4,6},{6,4},{8,10},{10,8},{12,14},{14,12},{16,18},{18,... | collective-permute-start | bytes 1769480 | tf_op jit(solution)/shard_map/ppermute | solution.py:382
  49.4 12.6 %collective-permute-start.12 = (bf16[192,1536]{1,0:T(8,128)(2,1)S(1)}, bf16[192,1536]{1,0:T(8,128)(2,1)S(1)}, u32[]{:S(2)}, u32[]{:S(2)}) collective-permute-start(bf16[192,1536]{1,0:T(8,128)(2,1)S(1)} %get-tuple-element.221), channel_id=1, source_target_pairs={{0,4},{2,6},{4,0},{6,2},{8,12},{10,14},{12,8},{14,10},{16,20},{18,... | collective-permute-start | bytes 1769480 | tf_op jit(solution)/shard_map/ppermute | solution.py:386
  50.8 12.2 %collective-permute-start.13 = (bf16[192,1536]{1,0:T(8,128)(2,1)S(1)}, bf16[192,1536]{1,0:T(8,128)(2,1)S(1)}, u32[]{:S(2)}, u32[]{:S(2)}) collective-permute-start(bf16[192,1536]{1,0:T(8,128)(2,1)S(1)} %get-tuple-element.220), channel_id=1, source_target_pairs={{0,2},{2,0},{4,6},{6,4},{8,10},{10,8},{12,14},{14,12},{16,18},{18,... | collective-permute-start | bytes 1769480 | tf_op jit(solution)/shard_map/ppermute | solution.py:382
  63.3 24.0 %collective-permute-start.15 = (bf16[384,1536]{1,0:T(8,128)(2,1)S(1)}, bf16[384,1536]{1,0:T(8,128)(2,1)S(1)}, u32[]{:S(2)}, u32[]{:S(2)}) collective-permute-start(bf16[384,1536]{1,0:T(8,128)(2,1)S(1)} %pad_maximum_fusion.3.ud_own_ref), channel_id=1, source_target_pairs={{0,4},{2,6},{4,0},{6,2},{8,12},{10,14},{12,8},{14,10},{16,20},{18,... | collective-permute-start | bytes 3538952 | tf_op jit(solution)/shard_map/ppermute | solution.py:386
  64.3 24.0 %collective-permute-start.14 = (bf16[384,1536]{1,0:T(8,128)(2,1)S(1)}, bf16[384,1536]{1,0:T(8,128)(2,1)S(1)}, u32[]{:S(2)}, u32[]{:S(2)}) collective-permute-start(bf16[384,1536]{1,0:T(8,128)(2,1)S(1)} %pad_maximum_fusion.2.gu_own_ref), channel_id=1, source_target_pairs={{0,2},{2,0},{4,6},{6,4},{8,10},{10,8},{12,14},{14,12},{16,18},{18,... | collective-permute-start | bytes 3538952 | tf_op jit(solution)/shard_map/ppermute | solution.py:382
  113.0 40.4 %collective-permute-start.20 = (bf16[512,768]{1,0:T(8,128)(2,1)}, bf16[512,768]{1,0:T(8,128)(2,1)S(1)}, u32[]{:S(2)}, u32[]{:S(2)}) collective-permute-start(bf16[512,768]{1,0:T(8,128)(2,1)} %get-tuple-element.135), channel_id=1, source_target_pairs={{0,1},{1,0},{2,3},{3,2},{4,5},{5,4},{6,7},{7,6},{8,9},{9,8},{10,11... | collective-permute-start | bytes 2359304 | tf_op jit(solution)/shard_map/ppermute | solution.py:853
  126.1 28.4 %collective-permute-start.19 = (bf16[384,1536]{1,0:T(8,128)(2,1)}, bf16[384,1536]{1,0:T(8,128)(2,1)S(1)}, u32[]{:S(2)}, u32[]{:S(2)}) collective-permute-start(bf16[384,1536]{1,0:T(8,128)(2,1)} %get-tuple-element.134), channel_id=1, source_target_pairs={{0,4},{2,6},{4,0},{6,2},{8,12},{10,14},{12,8},{14,10},{16,20},{18,... | collective-permute-start | bytes 3538952 | tf_op jit(solution)/shard_map/ppermute | solution.py:386
  127.0 27.9 %collective-permute-start.18 = (bf16[384,1536]{1,0:T(8,128)(2,1)S(1)}, bf16[384,1536]{1,0:T(8,128)(2,1)S(1)}, u32[]{:S(2)}, u32[]{:S(2)}) collective-permute-start(bf16[384,1536]{1,0:T(8,128)(2,1)S(1)} %copy-done.25), channel_id=1, source_target_pairs={{0,2},{2,0},{4,6},{6,4},{8,10},{10,8},{12,14},{14,12},{16,18},{18,... | collective-permute-start | bytes 3538952 | tf_op jit(solution)/shard_map/ppermute | solution.py:382
  155.2 14.7 %collective-permute-start.22 = (bf16[192,1536]{1,0:T(8,128)(2,1)S(1)}, bf16[192,1536]{1,0:T(8,128)(2,1)S(1)}, u32[]{:S(2)}, u32[]{:S(2)}) collective-permute-start(bf16[192,1536]{1,0:T(8,128)(2,1)S(1)} %get-tuple-element.201), channel_id=1, source_target_pairs={{0,2},{2,0},{4,6},{6,4},{8,10},{10,8},{12,14},{14,12},{16,18},{18,... | collective-permute-start | bytes 1769480 | tf_op jit(solution)/shard_map/ppermute | solution.py:382
  157.1 14.2 %collective-permute-start.21 = (bf16[192,1536]{1,0:T(8,128)(2,1)S(1)}, bf16[192,1536]{1,0:T(8,128)(2,1)S(1)}, u32[]{:S(2)}, u32[]{:S(2)}) collective-permute-start(bf16[192,1536]{1,0:T(8,128)(2,1)S(1)} %get-tuple-element.199), channel_id=1, source_target_pairs={{0,4},{2,6},{4,0},{6,2},{8,12},{10,14},{12,8},{14,10},{16,20},{18,... | collective-permute-start | bytes 1769480 | tf_op jit(solution)/shard_map/ppermute | solution.py:386
  171.7 13.3 %collective-permute-start.25 = (bf16[96,3072]{1,0:T(8,128)(2,1)S(1)}, bf16[96,3072]{1,0:T(8,128)(2,1)S(1)}, u32[]{:S(2)}, u32[]{:S(2)}) collective-permute-start(bf16[96,3072]{1,0:T(8,128)(2,1)S(1)} %pad_maximum_fusion.6), channel_id=1, source_target_pairs={{0,8},{2,10},{4,12},{6,14},{8,0},{10,2},{12,4},{14,6},{16,24},{18,... | collective-permute-start | bytes 1769480 | tf_op jit(solution)/shard_map/ppermute | solution.py:418
  173.2 13.0 %collective-permute-start.23 = (bf16[384,768]{1,0:T(8,128)(2,1)S(1)}, bf16[384,768]{1,0:T(8,128)(2,1)S(1)}, u32[]{:S(2)}, u32[]{:S(2)}) collective-permute-start(bf16[384,768]{1,0:T(8,128)(2,1)S(1)} %copy-done.31), channel_id=1, source_target_pairs={{0,2},{2,0},{4,6},{6,4},{8,10},{10,8},{12,14},{14,12},{16,18},{18,... | collective-permute-start | bytes 1769480 | tf_op jit(solution)/shard_map/ppermute | solution.py:382
  174.4 13.0 %collective-permute-start.24 = (bf16[384,768]{1,0:T(8,128)(2,1)S(1)}, bf16[384,768]{1,0:T(8,128)(2,1)S(1)}, u32[]{:S(2)}, u32[]{:S(2)}) collective-permute-start(bf16[384,768]{1,0:T(8,128)(2,1)S(1)} %copy-done.32), channel_id=1, source_target_pairs={{0,4},{2,6},{4,0},{6,2},{8,12},{10,14},{12,8},{14,10},{16,20},{18,... | collective-permute-start | bytes 1769480 | tf_op jit(solution)/shard_map/ppermute | solution.py:386
  190.0 16.3 %collective-permute-start.28 = (bf16[48,3072]{1,0:T(8,128)(2,1)S(1)}, bf16[48,3072]{1,0:T(8,128)(2,1)S(1)}, u32[]{:S(2)}, u32[]{:S(2)}) collective-permute-start(bf16[48,3072]{1,0:T(8,128)(2,1)S(1)} %add_convert_fusion.9), channel_id=1, source_target_pairs={{0,16},{2,18},{4,20},{6,22},{8,24},{10,26},{12,28},{14,30},{16,0},... | collective-permute-start | bytes 884744 | tf_op jit(solution)/shard_map/ppermute | solution.py:418
  192.5 13.8 %collective-permute-start.27 = (bf16[192,768]{1,0:T(8,128)(2,1)S(1)}, bf16[192,768]{1,0:T(8,128)(2,1)S(1)}, u32[]{:S(2)}, u32[]{:S(2)}) collective-permute-start(bf16[192,768]{1,0:T(8,128)(2,1)S(1)} %get-tuple-element.213), channel_id=1, source_target_pairs={{0,2},{2,0},{4,6},{6,4},{8,10},{10,8},{12,14},{14,12},{16,18},{18,... | collective-permute-start | bytes 884744 | tf_op jit(solution)/shard_map/ppermute | solution.py:382
  (47 other events, 345.8 us)

commit v4 on v3

--- a/solution.py
+++ b/solution.py
@@ -386,6 +386,10 @@
     return lax.ppermute(array, "dp", flip(2, lax.axis_size("dp")))
 
 
+def over_xy(array):
+    return lax.ppermute(array, "dp", flip(3, lax.axis_size("dp")))
+
+
 def over_far(array, steps):
     return lax.ppermute(array, "dp", ring_shift(4 * steps, lax.axis_size("dp")))
 
@@ -425,6 +429,20 @@
 
 def add_low(left, right):
     return (left.astype(HIGH) + right.astype(HIGH)).astype(LOW)
+
+
+def in_terms(array):
+    terms, rest = [], array
+    for _ in range(3):
+        term = lax.optimization_barrier(rest.astype(LOW))
+        terms.append(term)
+        rest = rest - term.astype(HIGH)
+    rows = jnp.concatenate(terms, axis=0)
+    return jnp.pad(rows, ((0, -rows.shape[0] % 8), (0, 0)))
+
+
+def from_terms(rows, height):
+    return sum(rows[i * height : (i + 1) * height].astype(HIGH) for i in range(3))
 
 
 def head_masks(dtype):
@@ -499,7 +517,7 @@
 
 
 def attend_body(
-    q_ref, k_ref, v_ref, strip_ref, wo_ref, e_ref, mixed_ref, low_ref, inv_ref, part_ref, table_ref, acc_ref
+    q_ref, k_ref, v_ref, strip_ref, wo_ref, e_ref, mixed_ref, low_ref, inv_ref, part0_ref, part1_ref, table_ref, acc_ref
 ):
     pair = pl.program_id(0)
     seq_len = k_ref.shape[0]
@@ -545,14 +563,27 @@
 
     @pl.when(pair == pl.num_programs(0) - 1)
     def _():
-        part_ref[...] = acc_ref[...].astype(LOW)
+        half = part0_ref.shape[0]
+        part0_ref[...] = acc_ref[:half, :].astype(LOW)
+        part1_ref[...] = acc_ref[half:, :].astype(LOW)
+
+
+def late_half(place_ref):
+    partner_first = pl.program_id(0) < pl.num_programs(0) // 2
+    return partner_first == (place_ref[2] == 0)
+
+
+def summed_halves(left_ref, right_ref):
+    return left_ref[...].astype(HIGH) + right_ref[...].astype(HIGH)
 
 
 def feed_body(
     place_ref,
     x_ref,
-    p_ref,
-    r_ref,
+    p0_ref,
+    p1_ref,
+    r0_ref,
+    r1_ref,
     g_ref,
     gain_ref,
     gu_own_ref,
@@ -571,13 +602,16 @@
     ud_ref,
 ):
     step = pl.program_id(0)
+    late = late_half(place_ref)
 
     @pl.when(step == 0)
     def _():
         put_weights(gu_ref, gu_own_ref, gu_other_ref, True, place_ref[1])
         put_weights(ud_ref, ud_own_ref, ud_other_ref, False, place_ref[0])
 
-    attended = x_ref[...].astype(HIGH) + (p_ref[...].astype(HIGH) + r_ref[...].astype(HIGH))
+    attended = x_ref[...].astype(HIGH) + jnp.where(
+        late, summed_halves(p1_ref, r1_ref), summed_halves(p0_ref, r0_ref)
+    )
     unit, _ = rms_parts(attended)
     normed = (unit * gain_ref[...]).astype(LOW)
     put_turned(turned_x_ref, normed, True, place_ref[1])
@@ -586,8 +620,7 @@
     put_turned(g_turned_ref, cotangent, False, place_ref[0])
     root = 0.7978845608028654
     columns = hidden_ref.shape[1] // 2
-    out = 0.0
-    d_normed = 0.0
+    products = []
     for part in range(2):
         w_gate = matrix(gu_ref, part * columns, columns)
         w_up = matrix(ud_ref, 0, columns) if part else matrix(gu_ref, 2 * columns, columns)
@@ -595,6 +628,10 @@
         gate = matmul_nn(normed, w_gate)
         up = matmul_nn(normed, w_up)
         d_hidden = matmul_nn(cotangent, w_down)
+        products.append((gate, up, d_hidden, w_gate, w_up, w_down))
+    out = 0.0
+    d_normed = 0.0
+    for part, (gate, up, d_hidden, w_gate, w_up, w_down) in enumerate(products):
         square = gate * gate
         bend = jnp.tanh(gate * (root + (root * 0.044715) * square))
         half = 0.5 + 0.5 * bend
@@ -642,8 +679,10 @@
 def turn_body(
     place_ref,
     x_ref,
-    p_ref,
-    r_ref,
+    p0_ref,
+    p1_ref,
+    r0_ref,
+    r1_ref,
     g_ref,
     a_ref,
     b_ref,
@@ -655,7 +694,10 @@
     dgain_ref,
 ):
     step = pl.program_id(0)
-    attended = x_ref[...].astype(HIGH) + (p_ref[...].astype(HIGH) + r_ref[...].astype(HIGH))
+    late = late_half(place_ref)
+    attended = x_ref[...].astype(HIGH) + jnp.where(
+        late, summed_halves(p1_ref, r1_ref), summed_halves(p0_ref, r0_ref)
+    )
     unit, scale = rms_parts(attended)
     d_normed = a_ref[...].astype(HIGH) + b_ref[...].astype(HIGH)
     d_gain = jnp.sum(d_normed * unit, axis=0, keepdims=True)
@@ -924,7 +966,7 @@
     e_block = pl.BlockSpec((2, seq_len, seq_len), lambda p: (p, 0, 0))
     strip_block = pl.BlockSpec((1, 2, 2 * seq_len), lambda p: (p, 0, 0))
     table_scratch = pltpu.VMEM((2, rows, 2 * seq_len), HIGH)
-    weights_e, mixed, mixed_low, inverse, part = call(
+    weights_e, mixed, mixed_low, inverse, part0, part1 = call(
         attend_body,
         (pairs,),
         [
@@ -934,19 +976,22 @@
             strip_block,
             pl.BlockSpec((features, LANES), lambda p: (0, p)),
         ],
-        [e_block, pair_block, pair_block, pair_block, result((seq_len, features))],
+        [e_block, pair_block, pair_block, pair_block] + [result((own_rows, features))] * 2,
         [
             shaped((2 * pairs, seq_len, seq_len), LOW),
             shaped((seq_len, width), HIGH),
             shaped((seq_len, width), LOW),
             shaped((seq_len, width), HIGH),
-            shaped((seq_len, features), LOW),
+            shaped((own_rows, features), LOW),
+            shaped((own_rows, features), LOW),
         ],
         [table_scratch, pltpu.VMEM((seq_len, features), HIGH)],
         micros=20,
     )(queries, keys, values, strip, w_o)
-    gu_other, ud_other, part = together(gu_other, ud_other, part)
-    part_other = swapped(part)
+    gu_other, ud_other, came0, came1 = together(
+        gu_other, ud_other, swapped(part0), swapped(part1)
+    )
+    parts = (part0, part1, came0, came1)
 
     def moved(i, m):
         return (i + half_steps * (1 - m[2])) % steps
@@ -954,6 +999,13 @@
     def turned_row(columns):
         return pl.BlockSpec((rows, columns), lambda i, m: (moved(i, m), 0))
 
+    half0_row = pl.BlockSpec(
+        (rows, features), lambda i, m: (jnp.minimum(moved(i, m), half_steps - 1), 0)
+    )
+    half1_row = pl.BlockSpec(
+        (rows, features), lambda i, m: (jnp.maximum(moved(i, m) - half_steps, 0), 0)
+    )
+    attended_rows = [turned_row(features)] + [half0_row, half1_row] * 2
     moved_block = pl.BlockSpec(
         turned_shape + (rows,), lambda i, m: (0, 0, 0, 0, 0, moved(i, m))
     )
@@ -964,7 +1016,9 @@
     feed_x_turned, feed_y_turned, g_turned, hidden, d_gate_up, dn_part, out_send, out_own = call(
         feed_body,
         (steps,),
-        [turned_row(features)] * 4 + [whole((1, features))] + [whole(half_block)] * 4,
+        attended_rows
+        + [turned_row(features), whole((1, features))]
+        + [whole(half_block)] * 4,
         [
             moved_block,
             moved_block,
@@ -988,7 +1042,7 @@
         [pltpu.VMEM(full_block, LOW), pltpu.VMEM(full_block, LOW)],
         prefetch=1,
         micros=19,
-    )(place, x_all, part, part_other, g_all, gain_f, gu_own, gu_other, ud_own, ud_other)
+    )(place, x_all, *parts, g_all, gain_f, gu_own, gu_other, ud_own, ud_other)
     dn_other = swapped(dn_part)
 
     gu_own, gu_send = weight_grads_one(feed_x_turned, d_gate_up, 3 * chunk // 2, 2, 5.5)
@@ -1003,7 +1057,9 @@
     d_attended, d_low_turned, d_mixed, d_gain_f = call(
         turn_body,
         (steps,),
-        [turned_row(features)] * 6 + [whole((1, features)), whole((features, width))],
+        attended_rows
+        + [turned_row(features)] * 3
+        + [whole((1, features)), whole((features, width))],
         [keep_row, moved_block, turned_row(width), result((1, features))],
         [
             shaped((own_rows, features), HIGH),
@@ -1012,8 +1068,8 @@
             shaped((1, features), HIGH),
         ],
         prefetch=1,
-        micros=8,
-    )(place, x_all, part, part_other, g_all, dn_part, dn_other, gain_f, w_o)
+        micros=4,
+    )(place, x_all, *parts, g_all, dn_part, dn_other, gain_f, w_o)
     out_other = swapped(out_send)
 
     d_query, d_key, d_value, d_strip = call(
@@ -1023,7 +1079,7 @@
         [pair_block, pair_block, pair_block, strip_block],
         [shaped((seq_len, width), LOW)] * 3 + [shaped((pairs, 2, 2 * seq_len), HIGH)],
         [table_scratch, pltpu.VMEM((LANES, seq_len), HIGH), pltpu.VMEM((LANES, seq_len), HIGH)],
-        micros=16,
+        micros=4,
     )(queries, keys, values, weights_e, d_mixed, mixed, inverse)
 
     gu_came, ud_came, out_other, d_query, d_key, d_value, d_strip = together(
@@ -1090,13 +1146,12 @@
     d_table = lax.dynamic_update_slice_in_dim(
         jnp.zeros_like(rel_table), my_d_table, me * local_heads, 1
     )
-    small = jnp.concatenate(
-        [d_gain_a.reshape(features), 0.5 * d_gain_f.reshape(features), d_table.reshape(-1)]
-    )
-    small = jnp.pad(small, (0, -small.shape[0] % 1024)).reshape(-1, LANES)
+    small_early = jnp.concatenate([0.5 * d_gain_f, d_table.reshape(1, -1)], axis=1)
+    small_early = jnp.pad(small_early, ((0, 0), (0, -(features + small_early.shape[1]) % (4 * width))))
+    small = jnp.concatenate([d_gain_a, small_early], axis=1)
+    small = small.reshape(-1, 4 * width)
     small = small + swapped(small)
-    small = small + over_x(small)
-    small = small + over_y(small)
+    small = small + over_x(small) + over_y(small) + over_xy(small)
 
     d_tokens = call(
         finish_body,
@@ -1117,9 +1172,14 @@
     def far_part(far):
         return part_of(total, 2 * (far % 2) + far // 2, 4)
 
-    pieces = [over_far(far_part((far_bit + k) % 4), k) for k in range(1, 4)]
-    small = small + over_far_bit(small, 0)
-    small = (small + over_far_bit(small, 1)).reshape(-1)
+    small_rows = in_terms(small)
+    pieces = [
+        over_far(jnp.concatenate([far_part((far_bit + k) % 4), small_rows], axis=0), k)
+        for k in range(1, 4)
+    ]
+    small = sum((from_terms(piece[block_rows:], small.shape[0]) for piece in pieces), small)
+    small = small.reshape(-1)
+    pieces = [piece[:block_rows] for piece in pieces]
     grads_head = sum((piece.astype(HIGH) for piece in pieces), far_part(far_bit).astype(HIGH))
     grads_qk, grads_vo = grads_head[:, : 2 * width], grads_head[:, 2 * width :]
     grads_unit = unit_own.astype(HIGH) + unit_came.astype(HIGH)

time: 226 us -> 223 us (0.987)
  waiting for transfers between devices: 43.7 us -> 40.2 us
    ppermute x9, waiting for transfers between devices: 9.24 us -> 16.8 us  [over_far(): return lax.ppermute(array, 'dp', ring_shift(4 * steps, lax.axis_size('dp')))]
    ppermute x9, waiting for transfers between devices: 16.1 us -> 9.22 us  [over_y(): return lax.ppermute(array, 'dp', flip(2, lax.axis_size('dp')))]
    ppermute x4 -> x2, waiting for transfers between devices: 9.95 us -> 5.89 us  [over_far_bit(): return lax.ppermute(array, 'dp', flip(4 << bit, lax.axis_size('dp')))]
  transfers between devices with their start and end apart: 38 -> 38, of which waited for: 22 -> 21; matrix products, arithmetic and copies ran while one was open for 5% -> 5% of each run, Pallas kernels for 38% -> 36%
where the time goes in v4:
time: 223 us; the launch traced here: 222 us
  Pallas kernels  107 us (48%)
  starting transfers between devices  52.6 us (24%)
  waiting for transfers between devices  40.2 us (18%)
  other arithmetic  10.1 us (5%)
  local copies, waits for them, and re-layouts  9.6 us (4%)
    ppermute x9, starting transfers between devices, over_far(): return lax.ppermute(array, 'dp', ring_shift(4 * steps, lax.axis_size('dp')))  25.3 us
    pallas_call x1, Pallas kernels, on_core_pair(): call(feed_body, (steps,), attended_rows + [turned_row(features), whole((1...  19.9 us
    pallas_call x3, Pallas kernels, weight_grads(): call(functools.partial(grads_body, count0), (steps,), [whole((height, dep...  18.3 us
    pallas_call x1, Pallas kernels, on_core_pair(): call(attend_body, (pairs,), [pair_block, pair_block, pair_block, strip_bl...  17.8 us
    ppermute x9, waiting for transfers between devices, over_far(): return lax.ppermute(array, 'dp', ring_shift(4 * steps, lax.axis_size('dp')))  16.8 us
    pallas_call x1, Pallas kernels, on_core_pair(): call(backward_body, (pairs,), [pair_block, pair_block, pair_block, e_bloc...  16.4 us
    ppermute x9, starting transfers between devices, over_x(): return lax.ppermute(array, 'dp', flip(1, lax.axis_size('dp')))  11.6 us
    ppermute x9, starting transfers between devices, over_y(): return lax.ppermute(array, 'dp', flip(2, lax.axis_size('dp')))  9.92 us
  transfers between devices with their start and end apart: 38, of which 21 were waited for; matrix products, arithmetic and copies ran while one was open for 5% of the time, Pallas kernels for 36%

profile of v4, /device:TPU:0, one launch (start us, length us, event | category | flops | bytes accessed | tf_op | source)
XLA Modules:
  0.0 222.3 jit_solution(9939288545527520566)
XLA Ops:
  1.7 3.1 %collective-permute-start = (bf16[48,1536]{1,0:T(8,128)(2,1)S(1)}, bf16[48,1536]{1,0:T(8,128)(2,1)S(1)}, u32[]{:S(2)}, u32[]{:S(2)}) collective-permute-start(bf16[48,1536]{1,0:T(8,128)(2,1)S(1)} %pad_maximum_fusion.11), channel_id=1, source_target_pairs={{0,8},{2,10},{4,12},{6,14},{8,16},{10,18},{12,20},{14,22},{16,24},... | collective-permute-start | bytes 442376 | tf_op jit(solution)/shard_map/ppermute | solution.py:394
  4.7 2.6 %collective-permute-start.1 = (bf16[48,1536]{1,0:T(8,128)(2,1)S(1)}, bf16[48,1536]{1,0:T(8,128)(2,1)S(1)}, u32[]{:S(2)}, u32[]{:S(2)}) collective-permute-start(bf16[48,1536]{1,0:T(8,128)(2,1)S(1)} %pad_maximum_fusion.11), channel_id=1, source_target_pairs={{0,16},{2,18},{4,20},{6,22},{8,24},{10,26},{12,28},{14,30},{16,0},... | collective-permute-start | bytes 442376 | tf_op jit(solution)/shard_map/ppermute | solution.py:394
  13.0 9.0 %collective-permute-start.10 = (bf16[48,3072]{1,0:T(8,128)(2,1)S(1)}, bf16[48,3072]{1,0:T(8,128)(2,1)S(1)}, u32[]{:S(2)}, u32[]{:S(2)}) collective-permute-start(bf16[48,3072]{1,0:T(8,128)(2,1)S(1)} %pad_maximum_fusion.7), channel_id=1, source_target_pairs={{0,16},{2,18},{4,20},{6,22},{8,24},{10,26},{12,28},{14,30},{16,0},... | collective-permute-start | bytes 884744 | tf_op jit(solution)/shard_map/ppermute | solution.py:394
  26.2 3.6 %collective-permute-done.3 = bf16[192,768]{1,0:T(8,128)(2,1)S(1)} collective-permute-done((bf16[192,768]{1,0:T(8,128)(2,1)S(1)}, bf16[192,768]{1,0:T(8,128)(2,1)S(1)}, u32[]{:S(2)}, u32[]{:S(2)}) %collective-permute-start.3) | collective-permute-done | bytes 294944 | tf_op jit(solution)/shard_map/ppermute | solution.py:386
  29.8 4.1 %collective-permute-start.11 = (bf16[48,3072]{1,0:T(8,128)(2,1)S(1)}, bf16[48,3072]{1,0:T(8,128)(2,1)S(1)}, u32[]{:S(2)}, u32[]{:S(2)}) collective-permute-start(bf16[48,3072]{1,0:T(8,128)(2,1)S(1)} %pad_maximum_fusion.7), channel_id=1, source_target_pairs={{0,24},{2,26},{4,28},{6,30},{8,0},{10,2},{12,4},{14,6},{16,8},{18,... | collective-permute-start | bytes 884744 | tf_op jit(solution)/shard_map/ppermute | solution.py:394
  40.3 1.8 collective-permute-done.11
  42.1 4.6 %collective-permute-done.9 = bf16[48,3072]{1,0:T(8,128)(2,1)S(1)} collective-permute-done((bf16[48,3072]{1,0:T(8,128)(2,1)S(1)}, bf16[48,3072]{1,0:T(8,128)(2,1)S(1)}, u32[]{:S(2)}, u32[]{:S(2)}) %collective-permute-start.9) | collective-permute-done | bytes 294944 | tf_op jit(solution)/shard_map/ppermute | solution.py:394
  46.7 2.5 %collective-permute-done.6.vo_other_ref = bf16[384,768]{1,0:T(8,128)(2,1)S(1)} collective-permute-done((bf16[384,768]{1,0:T(8,128)(2,1)S(1)}, bf16[384,768]{1,0:T(8,128)(2,1)S(1)}, u32[]{:S(2)}, u32[]{:S(2)}) %collective-permute-start.6) | collective-permute-done | bytes 589856 | tf_op jit(solution)/shard_map/ppermute | solution.py:386
  53.3 8.7 %shard_map.220 = (bf16[2,2,2,2,48,1024]{5,4,3,2,1,0:T(8,128)(2,1)}, bf16[2,2,2,2,48,1024]{5,4,3,2,1,0:T(8,128)(2,1)}, bf16[1024,384]{1,0:T(8,128)(2,1)}, bf16[10...) custom-call(s32[4]{0:T(128)} %pad_add_fusion.place_ref, ...), custom_call_target="tpu_custom_call" | custom-call | flops 8074500096 | tf_op jit(solution)/shard_map/pallas_call | solution.py:944
  66.8 17.8 %shard_map.221 = (bf16[6,1024,1024]{2,1,0:T(8,128)(2,1)}, f32[1024,384]{1,0:T(8,128)}, bf16[1024,384]{1,0:T(8,128)(2,1)}, f32[1024,384]{1,0:T(8,128)}, bf16[512,...) custom-call(bf16[1024,384]{1,0:T(8,128)(2,1)} %get-tuple-element.113.q_ref, bf16[1024,384]{1,0:T(8,128)(2,1)} %get-tuple-element.114.k_ref, ...), custom_call_target="tpu_custom_call" | custom-call | flops 23069999104 | tf_op jit(solution)/shard_map/pallas_call | solution.py:969
  90.6 19.9 %shard_map.222 = (bf16[2,2,2,2,48,1024]{5,4,3,2,1,0:T(8,128)(2,1)}, bf16[2,2,2,2,48,1024]{5,4,3,2,1,0:T(8,128)(2,1)}, bf16[2,2,2,2,48,1024]{5,4,3,2,1,0:T(8,128)...) custom-call(s32[4]{0:T(128)} %pad_add_fusion.place_ref, ...), custom_call_target="tpu_custom_call" | custom-call | flops 21916499968 | tf_op jit(solution)/shard_map/pallas_call | solution.py:1016
  110.8 5.5 %shard_map.223 = (bf16[384,1536]{1,0:T(8,128)(2,1)}, bf16[384,1536]{1,0:T(8,128)(2,1)}) custom-call(bf16[768,1024]{1,0:T(8,128)(2,1)} %bitcast.49, bf16[1024,2048]{1,0:T(8,128)(2,1)} %get-tuple-element.128.right_ref.right0_ref), custom_call_target="tpu_custom_call" | custom-call | flops 6344249856 | tf_op jit(solution)/shard_map/pallas_call | solution.py:852
  116.4 7.7 %shard_map.224 = (bf16[384,1536]{1,0:T(8,128)(2,1)}, bf16[384,1536]{1,0:T(8,128)(2,1)}) custom-call(bf16[768,1024]{1,0:T(8,128)(2,1)} %bitcast.47, bf16[768,1024]{1,0:T(8,128)(2,1)} %bitcast.48, bf16[1024,2048]{1,0:T(8,128)(2,1)} %get-tuple-element.128.right_ref.right0_ref, bf16[1024,1024]{1,0:T(8,128)(2,1)} %get-tuple-element.135.right1_ref), custom_call_target="tpu_custom_call" | custom-call | flops 7497750016 | tf_op jit(solution)/shard_map/pallas_call | solution.py:833
  126.5 9.2 %shard_map.225 = (f32[512,768]{1,0:T(8,128)}, bf16[2,2,2,2,48,1024]{5,4,3,2,1,0:T(8,128)(2,1)}, bf16[1024,384]{1,0:T(8,128)(2,1)}, f32[1,768]{1,0:T(1,128)}) custom-call(s32[4]{0:T(128)} %pad_add_fusion.place_ref, bf16[1024,768]{1,0:T(8,128)(2,1)} %pad_maximum_fusion.x_ref, bf16[512,768]{1,0:T(8,128)(2,1)} %get-tuple-element.117.p0_ref, ...), custom_call_target="tpu_custom_call" | custom-call | flops 4614000128 | tf_op jit(solution)/shard_map/pallas_call | solution.py:1057
  136.4 16.4 %shard_map.226 = (bf16[1024,384]{1,0:T(8,128)(2,1)}, bf16[1024,384]{1,0:T(8,128)(2,1)}, bf16[1024,384]{1,0:T(8,128)(2,1)}, f32[3,2,2048]{2,1,0:T(2,128)}) custom-call(bf16[1024,384]{1,0:T(8,128)(2,1)} %get-tuple-element.113.q_ref, bf16[1024,384]{1,0:T(8,128)(2,1)} %get-tuple-element.114.k_ref, bf16[1024,384]{1,0:T(8,128)(2,1)} %get-tuple-element.115.v_ref, ...), custom_call_target="tpu_custom_call" | custom-call | flops 4614000128 | tf_op jit(solution)/shard_map/pallas_call | solution.py:1075
  156.3 5.3 %shard_map.227 = (bf16[384,768]{1,0:T(8,128)(2,1)}, bf16[384,768]{1,0:T(8,128)(2,1)}) custom-call(bf16[768,1024]{1,0:T(8,128)(2,1)} %bitcast.44, bf16[768,1024]{1,0:T(8,128)(2,1)} %bitcast.45, bf16[1024,384]{1,0:T(8,128)(2,1)} %get-tuple-element.170.right0_ref.dq_ref, bf16[1024,384]{1,0:T(8,128)(2,1)} %get-tuple-element.152.right1_ref.dk_ref), custom_call_target="tpu_custom_call" | custom-call | flops 5767499776 | tf_op jit(solution)/shard_map/pallas_call | solution.py:833
  162.7 5.2 %shard_map.228 = (bf16[384,768]{1,0:T(8,128)(2,1)}, bf16[384,768]{1,0:T(8,128)(2,1)}) custom-call(bf16[768,1024]{1,0:T(8,128)(2,1)} %bitcast.43, bf16[768,1024]{1,0:T(8,128)(2,1)} %bitcast.46, bf16[1024,384]{1,0:T(8,128)(2,1)} %get-tuple-element.163.right0_ref.dv_ref, bf16[1024,384]{1,0:T(8,128)(2,1)} %get-tuple-element.164.right1_ref), custom_call_target="tpu_custom_call" | custom-call | flops 5767499776 | tf_op jit(solution)/shard_map/pallas_call | solution.py:833
  173.9 7.8 %shard_map.229 = (bf16[512,768]{1,0:T(8,128)(2,1)}, f32[512,768]{1,0:T(8,128)}, f32[1,768]{1,0:T(1,128)}) custom-call(s32[4]{0:T(128)} %pad_add_fusion.place_ref, bf16[1024,768]{1,0:T(8,128)(2,1)} %pad_maximum_fusion.x_ref, bf16[1024,384]{1,0:T(8,128)(2,1)} %get-tuple-element.170.right0_ref.dq_ref, bf16[1024,384]{1,0:T(8,128)(2,1)} %get-tuple-element.152.right1_ref.dk_ref, ...), custom_call_target="tpu_custom_call" | custom-call | flops 8074500096 | tf_op jit(solution)/shard_map/pallas_call | solution.py:1120
  181.7 2.4 %collective-permute-done.26 = bf16[96,3072]{1,0:T(8,128)(2,1)S(1)} collective-permute-done((bf16[96,3072]{1,0:T(8,128)(2,1)S(1)}, bf16[96,3072]{1,0:T(8,128)(2,1)S(1)}, u32[]{:S(2)}, u32[]{:S(2)}) %collective-permute-start.26) | collective-permute-done | bytes 589856 | tf_op jit(solution)/shard_map/ppermute | solution.py:422
  197.5 3.4 %shard_map.230 = bf16[512,768]{1,0:T(8,128)(2,1)} custom-call(bf16[512,768]{1,0:T(8,128)(2,1)} %x_ref.1, f32[512,768]{1,0:T(8,128)} %get-tuple-element.179.own_ref, bf16[512,768]{1,0:T(8,128)(2,1)} %copy-done.29, f32[512,768]{1,0:T(8,128)} %get-tuple-element.181.datt_ref, f32[1,768]{1,0:T(1,128)} %reshape.76.gain_ref), custom_call_target="tpu_custom_call" | custom-call | flops 4037250048 | tf_op jit(solution)/shard_map/pallas_call | solution.py:1156
  200.9 3.5 %collective-permute-done.29 = bf16[48,3072]{1,0:T(8,128)(2,1)S(1)} collective-permute-done((bf16[48,3072]{1,0:T(8,128)(2,1)S(1)}, bf16[48,3072]{1,0:T(8,128)(2,1)S(1)}, u32[]{:S(2)}, u32[]{:S(2)}) %collective-permute-start.29) | collective-permute-done | bytes 294944 | tf_op jit(solution)/shard_map/ppermute | solution.py:422
  204.8 2.3 %collective-permute-start.36 = (bf16[56,1536]{1,0:T(8,128)(2,1)S(1)}, bf16[56,1536]{1,0:T(8,128)(2,1)S(1)}, u32[]{:S(2)}, u32[]{:S(2)}) collective-permute-start(bf16[56,1536]{1,0:T(8,128)(2,1)S(1)} %get-tuple-element.245), channel_id=1, source_target_pairs={{0,16},{2,18},{4,20},{6,22},{8,24},{10,26},{12,28},{14,30},{16,0},... | collective-permute-start | bytes 516104 | tf_op jit(solution)/shard_map/ppermute | solution.py:394
  209.6 4.4 %collective-permute-done.35 = bf16[56,1536]{1,0:T(8,128)(2,1)S(1)} collective-permute-done((bf16[56,1536]{1,0:T(8,128)(2,1)S(1)}, bf16[56,1536]{1,0:T(8,128)(2,1)S(1)}, u32[]{:S(2)}, u32[]{:S(2)}) %collective-permute-start.35) | collective-permute-done | bytes 172064 | tf_op jit(solution)/shard_map/ppermute | solution.py:394
  214.0 6.0 %collective-permute-done.36 = bf16[56,1536]{1,0:T(8,128)(2,1)S(1)} collective-permute-done((bf16[56,1536]{1,0:T(8,128)(2,1)S(1)}, bf16[56,1536]{1,0:T(8,128)(2,1)S(1)}, u32[]{:S(2)}, u32[]{:S(2)}) %collective-permute-start.36) | collective-permute-done | bytes 172064 | tf_op jit(solution)/shard_map/ppermute | solution.py:394
  (197 shorter events, 64.1 us)
Async XLA Ops:
  4.7 17.2 %collective-permute-start.1 = (bf16[48,1536]{1,0:T(8,128)(2,1)S(1)}, bf16[48,1536]{1,0:T(8,128)(2,1)S(1)}, u32[]{:S(2)}, u32[]{:S(2)}) collective-permute-start(bf16[48,1536]{1,0:T(8,128)(2,1)S(1)} %pad_maximum_fusion.11), channel_id=1, source_target_pairs={{0,16},{2,18},{4,20},{6,22},{8,24},{10,26},{12,28},{14,30},{16,0},... | collective-permute-start | bytes 442376 | tf_op jit(solution)/shard_map/ppermute | solution.py:394
  7.3 14.6 %collective-permute-start.2 = (bf16[48,1536]{1,0:T(8,128)(2,1)S(1)}, bf16[48,1536]{1,0:T(8,128)(2,1)}, u32[]{:S(2)}, u32[]{:S(2)}) collective-permute-start(bf16[48,1536]{1,0:T(8,128)(2,1)S(1)} %pad_maximum_fusion.11), channel_id=1, source_target_pairs={{0,24},{2,26},{4,28},{6,30},{8,0},{10,2},{12,4},{14,6},{16,8},{18,... | collective-permute-start | bytes 442376 | tf_op jit(solution)/shard_map/ppermute | solution.py:394
  8.7 26.8 %collective-permute-start.7 = (bf16[512,768]{1,0:T(8,128)(2,1)}, bf16[512,768]{1,0:T(8,128)(2,1)S(1)}, u32[]{:S(2)}, u32[]{:S(2)}) collective-permute-start(bf16[512,768]{1,0:T(8,128)(2,1)} %x_ref.1), channel_id=1, source_target_pairs={{0,1},{1,0},{2,3},{3,2},{4,5},{5,4},{6,7},{7,6},{8,9},{9,8},{10,11... | collective-permute-start | bytes 2359304 | tf_op jit(solution)/shard_map/ppermute | solution.py:895
  8.7 27.3 %collective-permute-start.8 = (bf16[512,768]{1,0:T(8,128)(2,1)}, bf16[512,768]{1,0:T(8,128)(2,1)S(1)}, u32[]{:S(2)}, u32[]{:S(2)}) collective-permute-start(bf16[512,768]{1,0:T(8,128)(2,1)} %param.14), channel_id=1, source_target_pairs={{0,1},{1,0},{2,3},{3,2},{4,5},{5,4},{6,7},{7,6},{8,9},{9,8},{10,11... | collective-permute-start | bytes 2359304 | tf_op jit(solution)/shard_map/ppermute | solution.py:895
  13.0 27.3 %collective-permute-start.10 = (bf16[48,3072]{1,0:T(8,128)(2,1)S(1)}, bf16[48,3072]{1,0:T(8,128)(2,1)S(1)}, u32[]{:S(2)}, u32[]{:S(2)}) collective-permute-start(bf16[48,3072]{1,0:T(8,128)(2,1)S(1)} %pad_maximum_fusion.7), channel_id=1, source_target_pairs={{0,16},{2,18},{4,20},{6,22},{8,24},{10,26},{12,28},{14,30},{16,0},... | collective-permute-start | bytes 884744 | tf_op jit(solution)/shard_map/ppermute | solution.py:394
  29.8 12.3 %collective-permute-start.11 = (bf16[48,3072]{1,0:T(8,128)(2,1)S(1)}, bf16[48,3072]{1,0:T(8,128)(2,1)S(1)}, u32[]{:S(2)}, u32[]{:S(2)}) collective-permute-start(bf16[48,3072]{1,0:T(8,128)(2,1)S(1)} %pad_maximum_fusion.7), channel_id=1, source_target_pairs={{0,24},{2,26},{4,28},{6,30},{8,0},{10,2},{12,4},{14,6},{16,8},{18,... | collective-permute-start | bytes 884744 | tf_op jit(solution)/shard_map/ppermute | solution.py:394
  33.9 12.8 %collective-permute-start.9 = (bf16[48,3072]{1,0:T(8,128)(2,1)S(1)}, bf16[48,3072]{1,0:T(8,128)(2,1)S(1)}, u32[]{:S(2)}, u32[]{:S(2)}) collective-permute-start(bf16[48,3072]{1,0:T(8,128)(2,1)S(1)} %pad_maximum_fusion.7), channel_id=1, source_target_pairs={{0,8},{2,10},{4,12},{6,14},{8,16},{10,18},{12,20},{14,22},{16,24},... | collective-permute-start | bytes 884744 | tf_op jit(solution)/shard_map/ppermute | solution.py:394
  35.4 13.8 %collective-permute-start.6 = (bf16[384,768]{1,0:T(8,128)(2,1)S(1)}, bf16[384,768]{1,0:T(8,128)(2,1)S(1)}, u32[]{:S(2)}, u32[]{:S(2)}) collective-permute-start(bf16[384,768]{1,0:T(8,128)(2,1)S(1)} %pad_maximum_fusion.5.vo_own_ref), channel_id=1, source_target_pairs={{0,4},{2,6},{4,0},{6,2},{8,12},{10,14},{12,8},{14,10},{16,20},{18,... | collective-permute-start | bytes 1769480 | tf_op jit(solution)/shard_map/ppermute | solution.py:386
  36.0 13.5 %collective-permute-start.5 = (bf16[384,768]{1,0:T(8,128)(2,1)S(1)}, bf16[384,768]{1,0:T(8,128)(2,1)S(1)}, u32[]{:S(2)}, u32[]{:S(2)}) collective-permute-start(bf16[384,768]{1,0:T(8,128)(2,1)S(1)} %pad_maximum_fusion.4.qk_own_ref), channel_id=1, source_target_pairs={{0,2},{2,0},{4,6},{6,4},{8,10},{10,8},{12,14},{14,12},{16,18},{18,... | collective-permute-start | bytes 1769480 | tf_op jit(solution)/shard_map/ppermute | solution.py:382
  50.4 12.6 %collective-permute-start.12 = (bf16[192,1536]{1,0:T(8,128)(2,1)S(1)}, bf16[192,1536]{1,0:T(8,128)(2,1)S(1)}, u32[]{:S(2)}, u32[]{:S(2)}) collective-permute-start(bf16[192,1536]{1,0:T(8,128)(2,1)S(1)} %get-tuple-element.225), channel_id=1, source_target_pairs={{0,4},{2,6},{4,0},{6,2},{8,12},{10,14},{12,8},{14,10},{16,20},{18,... | collective-permute-start | bytes 1769480 | tf_op jit(solution)/shard_map/ppermute | solution.py:386
  51.8 12.2 %collective-permute-start.13 = (bf16[192,1536]{1,0:T(8,128)(2,1)S(1)}, bf16[192,1536]{1,0:T(8,128)(2,1)S(1)}, u32[]{:S(2)}, u32[]{:S(2)}) collective-permute-start(bf16[192,1536]{1,0:T(8,128)(2,1)S(1)} %get-tuple-element.224), channel_id=1, source_target_pairs={{0,2},{2,0},{4,6},{6,4},{8,10},{10,8},{12,14},{14,12},{16,18},{18,... | collective-permute-start | bytes 1769480 | tf_op jit(solution)/shard_map/ppermute | solution.py:382
  64.3 24.0 %collective-permute-start.15 = (bf16[384,1536]{1,0:T(8,128)(2,1)S(1)}, bf16[384,1536]{1,0:T(8,128)(2,1)S(1)}, u32[]{:S(2)}, u32[]{:S(2)}) collective-permute-start(bf16[384,1536]{1,0:T(8,128)(2,1)S(1)} %pad_maximum_fusion.3.ud_own_ref), channel_id=1, source_target_pairs={{0,4},{2,6},{4,0},{6,2},{8,12},{10,14},{12,8},{14,10},{16,20},{18,... | collective-permute-start | bytes 3538952 | tf_op jit(solution)/shard_map/ppermute | solution.py:386
  65.3 24.0 %collective-permute-start.14 = (bf16[384,1536]{1,0:T(8,128)(2,1)S(1)}, bf16[384,1536]{1,0:T(8,128)(2,1)S(1)}, u32[]{:S(2)}, u32[]{:S(2)}) collective-permute-start(bf16[384,1536]{1,0:T(8,128)(2,1)S(1)} %pad_maximum_fusion.2.gu_own_ref), channel_id=1, source_target_pairs={{0,2},{2,0},{4,6},{6,4},{8,10},{10,8},{12,14},{14,12},{16,18},{18,... | collective-permute-start | bytes 3538952 | tf_op jit(solution)/shard_map/ppermute | solution.py:382
  124.1 28.7 %collective-permute-start.20 = (bf16[384,1536]{1,0:T(8,128)(2,1)}, bf16[384,1536]{1,0:T(8,128)(2,1)S(1)}, u32[]{:S(2)}, u32[]{:S(2)}) collective-permute-start(bf16[384,1536]{1,0:T(8,128)(2,1)} %get-tuple-element.138), channel_id=1, source_target_pairs={{0,4},{2,6},{4,0},{6,2},{8,12},{10,14},{12,8},{14,10},{16,20},{18,... | collective-permute-start | bytes 3538952 | tf_op jit(solution)/shard_map/ppermute | solution.py:386
  125.4 28.1 %collective-permute-start.19 = (bf16[384,1536]{1,0:T(8,128)(2,1)}, bf16[384,1536]{1,0:T(8,128)(2,1)S(1)}, u32[]{:S(2)}, u32[]{:S(2)}) collective-permute-start(bf16[384,1536]{1,0:T(8,128)(2,1)} %get-tuple-element.132), channel_id=1, source_target_pairs={{0,2},{2,0},{4,6},{6,4},{8,10},{10,8},{12,14},{14,12},{16,18},{18,... | collective-permute-start | bytes 3538952 | tf_op jit(solution)/shard_map/ppermute | solution.py:382
  126.5 26.3 %collective-permute-start.21 = (bf16[512,768]{1,0:T(8,128)(2,1)S(1)}, bf16[512,768]{1,0:T(8,128)(2,1)S(1)}, u32[]{:S(2)}, u32[]{:S(2)}) collective-permute-start(bf16[512,768]{1,0:T(8,128)(2,1)S(1)} %copy-done.28), channel_id=1, source_target_pairs={{0,1},{1,0},{2,3},{3,2},{4,5},{5,4},{6,7},{7,6},{8,9},{9,8},{10,11... | collective-permute-start | bytes 2359304 | tf_op jit(solution)/shard_map/ppermute | solution.py:895
  153.8 15.0 %collective-permute-start.23 = (bf16[192,1536]{1,0:T(8,128)(2,1)S(1)}, bf16[192,1536]{1,0:T(8,128)(2,1)S(1)}, u32[]{:S(2)}, u32[]{:S(2)}) collective-permute-start(bf16[192,1536]{1,0:T(8,128)(2,1)S(1)} %get-tuple-element.205), channel_id=1, source_target_pairs={{0,2},{2,0},{4,6},{6,4},{8,10},{10,8},{12,14},{14,12},{16,18},{18,... | collective-permute-start | bytes 1769480 | tf_op jit(solution)/shard_map/ppermute | solution.py:382
  155.5 14.6 %collective-permute-start.22 = (bf16[192,1536]{1,0:T(8,128)(2,1)S(1)}, bf16[192,1536]{1,0:T(8,128)(2,1)S(1)}, u32[]{:S(2)}, u32[]{:S(2)}) collective-permute-start(bf16[192,1536]{1,0:T(8,128)(2,1)S(1)} %get-tuple-element.203), channel_id=1, source_target_pairs={{0,4},{2,6},{4,0},{6,2},{8,12},{10,14},{12,8},{14,10},{16,20},{18,... | collective-permute-start | bytes 1769480 | tf_op jit(solution)/shard_map/ppermute | solution.py:386
  170.4 13.7 %collective-permute-start.26 = (bf16[96,3072]{1,0:T(8,128)(2,1)S(1)}, bf16[96,3072]{1,0:T(8,128)(2,1)S(1)}, u32[]{:S(2)}, u32[]{:S(2)}) collective-permute-start(bf16[96,3072]{1,0:T(8,128)(2,1)S(1)} %pad_maximum_fusion.6), channel_id=1, source_target_pairs={{0,8},{2,10},{4,12},{6,14},{8,0},{10,2},{12,4},{14,6},{16,24},{18,... | collective-permute-start | bytes 1769480 | tf_op jit(solution)/shard_map/ppermute | solution.py:422
  171.6 13.3 %collective-permute-start.24 = (bf16[384,768]{1,0:T(8,128)(2,1)S(1)}, bf16[384,768]{1,0:T(8,128)(2,1)S(1)}, u32[]{:S(2)}, u32[]{:S(2)}) collective-permute-start(bf16[384,768]{1,0:T(8,128)(2,1)S(1)} %copy-done.32), channel_id=1, source_target_pairs={{0,2},{2,0},{4,6},{6,4},{8,10},{10,8},{12,14},{14,12},{16,18},{18,... | collective-permute-start | bytes 1769480 | tf_op jit(solution)/shard_map/ppermute | solution.py:382
  172.6 13.1 %collective-permute-start.25 = (bf16[384,768]{1,0:T(8,128)(2,1)S(1)}, bf16[384,768]{1,0:T(8,128)(2,1)S(1)}, u32[]{:S(2)}, u32[]{:S(2)}) collective-permute-start(bf16[384,768]{1,0:T(8,128)(2,1)S(1)} %copy-done.33), channel_id=1, source_target_pairs={{0,4},{2,6},{4,0},{6,2},{8,12},{10,14},{12,8},{14,10},{16,20},{18,... | collective-permute-start | bytes 1769480 | tf_op jit(solution)/shard_map/ppermute | solution.py:386
  188.1 16.3 %collective-permute-start.29 = (bf16[48,3072]{1,0:T(8,128)(2,1)S(1)}, bf16[48,3072]{1,0:T(8,128)(2,1)S(1)}, u32[]{:S(2)}, u32[]{:S(2)}) collective-permute-start(bf16[48,3072]{1,0:T(8,128)(2,1)S(1)} %add_convert_fusion.9), channel_id=1, source_target_pairs={{0,16},{2,18},{4,20},{6,22},{8,24},{10,26},{12,28},{14,30},{16,0},... | collective-permute-start | bytes 884744 | tf_op jit(solution)/shard_map/ppermute | solution.py:422
  204.8 15.2 %collective-permute-start.36 = (bf16[56,1536]{1,0:T(8,128)(2,1)S(1)}, bf16[56,1536]{1,0:T(8,128)(2,1)S(1)}, u32[]{:S(2)}, u32[]{:S(2)}) collective-permute-start(bf16[56,1536]{1,0:T(8,128)(2,1)S(1)} %get-tuple-element.245), channel_id=1, source_target_pairs={{0,16},{2,18},{4,20},{6,22},{8,24},{10,26},{12,28},{14,30},{16,0},... | collective-permute-start | bytes 516104 | tf_op jit(solution)/shard_map/ppermute | solution.py:394
  207.1 12.9 %collective-permute-start.37 = (bf16[56,1536]{1,0:T(8,128)(2,1)S(1)}, bf16[56,1536]{1,0:T(8,128)(2,1)S(1)}, u32[]{:S(2)}, u32[]{:S(2)}) collective-permute-start(bf16[56,1536]{1,0:T(8,128)(2,1)S(1)} %get-tuple-element.246), channel_id=1, source_target_pairs={{0,24},{2,26},{4,28},{6,30},{8,0},{10,2},{12,4},{14,6},{16,8},{18,... | collective-permute-start | bytes 516104 | tf_op jit(solution)/shard_map/ppermute | solution.py:394
  (48 other events, 319.6 us)

commit v5 on v4

--- a/solution.py
+++ b/solution.py
@@ -464,14 +464,16 @@
                     full_ref[place, at, near] = block
 
 
-def put_turned(turned_ref, array, x_first, bit):
+def put_turned(turned_ref, array, x_first, bit, lanes=slice(None)):
     rows = turned_ref.shape[4]
     turned = array.T
     for block in range(turned.shape[0] // rows):
         far, y_bit, x_bit = block // 4, (block // 2) % 2, block % 2
         first, second = (x_bit, y_bit) if x_first else (y_bit, x_bit)
         other = 1 - bit if first else bit
-        turned_ref[other, second, far % 2, far // 2] = turned[block * rows : (block + 1) * rows]
+        turned_ref[other, second, far % 2, far // 2, :, lanes] = turned[
+            block * rows : (block + 1) * rows
+        ]
 
 
 def matrix(full_ref, start, columns):
@@ -568,16 +570,12 @@
         part1_ref[...] = acc_ref[half:, :].astype(LOW)
 
 
-def late_half(place_ref):
-    partner_first = pl.program_id(0) < pl.num_programs(0) // 2
-    return partner_first == (place_ref[2] == 0)
-
-
 def summed_halves(left_ref, right_ref):
     return left_ref[...].astype(HIGH) + right_ref[...].astype(HIGH)
 
 
 def feed_body(
+    row_steps,
     place_ref,
     x_ref,
     p0_ref,
@@ -590,19 +588,67 @@
     gu_other_ref,
     ud_own_ref,
     ud_other_ref,
+    unit_ref,
+    scale_ref,
+    dn_ref,
+    send_ref,
+    own_ref,
+    dgu_own_ref,
+    dgu_other_ref,
+    dud_own_ref,
+    dud_other_ref,
+    gu_ref,
+    ud_ref,
     turned_x_ref,
     turned_y_ref,
     g_turned_ref,
     hidden_ref,
-    dgu_ref,
-    dn_ref,
-    send_ref,
-    own_ref,
-    gu_ref,
-    ud_ref,
+    dgate_up_ref,
 ):
     step = pl.program_id(0)
-    late = late_half(place_ref)
+    columns = hidden_ref.shape[1] // 2
+    pl.when(step < row_steps)(
+        functools.partial(
+            feed_rows,
+            step,
+            row_steps,
+            place_ref,
+            (x_ref, p0_ref, p1_ref, r0_ref, r1_ref, g_ref, gain_ref),
+            (gu_own_ref, gu_other_ref, ud_own_ref, ud_other_ref),
+            (unit_ref, scale_ref, dn_ref, send_ref, own_ref),
+            (gu_ref, ud_ref, turned_x_ref, turned_y_ref, g_turned_ref, hidden_ref, dgate_up_ref),
+        )
+    )
+
+    def product(left_ref, right, own_out_ref, other_out_ref):
+        for half, out_ref in enumerate((own_out_ref, other_out_ref)):
+            left = left_ref[half].reshape(out_ref.shape[0], -1)
+            out_ref[...] = matmul_nn(left, right).astype(LOW)
+
+    for block in range(6):
+
+        @pl.when(step == row_steps + block)
+        def _(block=block):
+            if block < 3:
+                right = dgate_up_ref[:, block * columns : (block + 1) * columns]
+                product(turned_x_ref, right, dgu_own_ref, dgu_other_ref)
+            elif block == 3:
+                right = dgate_up_ref[:, block * columns : (block + 1) * columns]
+                product(turned_y_ref, right, dud_own_ref, dud_other_ref)
+            else:
+                right = hidden_ref[:, (block - 4) * columns : (block - 3) * columns]
+                product(g_turned_ref, right, dud_own_ref, dud_other_ref)
+
+
+def feed_rows(step, row_steps, place_ref, inputs, weights, outputs, scratch):
+    x_ref, p0_ref, p1_ref, r0_ref, r1_ref, g_ref, gain_ref = inputs
+    gu_own_ref, gu_other_ref, ud_own_ref, ud_other_ref = weights
+    unit_ref, scale_ref, dn_ref, send_ref, own_ref = outputs
+    gu_ref, ud_ref, turned_x_ref, turned_y_ref, g_turned_ref, hidden_ref, dgate_up_ref = scratch
+    rows = x_ref.shape[0]
+    late = (step < row_steps // 2) == (place_ref[2] == 0)
+    position = lax.rem(step + (row_steps // 2) * (1 - place_ref[2]), row_steps)
+    at = pl.ds(pl.multiple_of(position * rows, rows), rows)
 
     @pl.when(step == 0)
     def _():
@@ -612,12 +658,14 @@
     attended = x_ref[...].astype(HIGH) + jnp.where(
         late, summed_halves(p1_ref, r1_ref), summed_halves(p0_ref, r0_ref)
     )
-    unit, _ = rms_parts(attended)
+    unit, scale = rms_parts(attended)
     normed = (unit * gain_ref[...]).astype(LOW)
-    put_turned(turned_x_ref, normed, True, place_ref[1])
-    put_turned(turned_y_ref, normed, False, place_ref[0])
+    unit_ref[...] = unit.astype(LOW)
+    scale_ref[...] = jnp.broadcast_to(scale, scale_ref.shape)
+    put_turned(turned_x_ref, normed, True, place_ref[1], at)
+    put_turned(turned_y_ref, normed, False, place_ref[0], at)
     cotangent = g_ref[...]
-    put_turned(g_turned_ref, cotangent, False, place_ref[0])
+    put_turned(g_turned_ref, cotangent, False, place_ref[0], at)
     root = 0.7978845608028654
     columns = hidden_ref.shape[1] // 2
     products = []
@@ -640,18 +688,18 @@
         hidden = (gelu * up).astype(LOW)
         d_gate = (d_hidden * up * slope).astype(LOW)
         d_up = (d_hidden * gelu).astype(LOW)
-        hidden_ref[:, part * columns : (part + 1) * columns] = hidden
-        dgu_ref[:, part * columns : (part + 1) * columns] = d_gate
-        dgu_ref[:, (2 + part) * columns : (3 + part) * columns] = d_up
+        hidden_ref[at, part * columns : (part + 1) * columns] = hidden
+        dgate_up_ref[at, part * columns : (part + 1) * columns] = d_gate
+        dgate_up_ref[at, (2 + part) * columns : (3 + part) * columns] = d_up
         d_normed = d_normed + matmul_nt(d_gate, w_gate) + matmul_nt(d_up, w_up)
         out = out + matmul_nt(hidden, w_down)
     dn_ref[...] = d_normed.astype(LOW)
 
-    @pl.when(step < pl.num_programs(0) // 2)
+    @pl.when(step < row_steps // 2)
     def _():
         send_ref[...] = out.astype(LOW)
 
-    @pl.when(step >= pl.num_programs(0) // 2)
+    @pl.when(step >= row_steps // 2)
     def _():
         own_ref[...] = attended + out
 
@@ -669,20 +717,10 @@
     pl.when(step >= first_count)(functools.partial(product, left1_ref, right1_ref))
 
 
-def grads_one_body(left_ref, right_ref, own_ref, other_ref):
-    half = own_ref.shape[0]
-    right = right_ref[...]
-    own_ref[...] = matmul_nn(left_ref[:half, :], right).astype(LOW)
-    other_ref[...] = matmul_nn(left_ref[half:, :], right).astype(LOW)
-
-
 def turn_body(
     place_ref,
-    x_ref,
-    p0_ref,
-    p1_ref,
-    r0_ref,
-    r1_ref,
+    unit_ref,
+    scale_ref,
     g_ref,
     a_ref,
     b_ref,
@@ -694,11 +732,8 @@
     dgain_ref,
 ):
     step = pl.program_id(0)
-    late = late_half(place_ref)
-    attended = x_ref[...].astype(HIGH) + jnp.where(
-        late, summed_halves(p1_ref, r1_ref), summed_halves(p0_ref, r0_ref)
-    )
-    unit, scale = rms_parts(attended)
+    unit = unit_ref[...].astype(HIGH)
+    scale = scale_ref[:, :1]
     d_normed = a_ref[...].astype(HIGH) + b_ref[...].astype(HIGH)
     d_gain = jnp.sum(d_normed * unit, axis=0, keepdims=True)
     d_attended = g_ref[...].astype(HIGH) + rms_back(d_normed, unit, scale, gain_ref[...])
@@ -845,20 +880,6 @@
     )(left0, left1, right0, right1)
 
 
-def weight_grads_one(left, right, columns, steps, micros):
-    left = flat_left(left)
-    height, depth = left.shape
-    half_spec = pl.BlockSpec((height // 2, columns), lambda i: (0, i))
-    return call(
-        grads_one_body,
-        (steps,),
-        [whole((height, depth)), pl.BlockSpec((depth, columns), lambda i: (0, i))],
-        [half_spec, half_spec],
-        [shaped((height // 2, steps * columns), LOW)] * 2,
-        micros=micros,
-    )(left, right)
-
-
 def on_core_pair(
     tokens,
     cotangent,
@@ -994,7 +1015,7 @@
     parts = (part0, part1, came0, came1)
 
     def moved(i, m):
-        return (i + half_steps * (1 - m[2])) % steps
+        return (jnp.minimum(i, steps - 1) + half_steps * (1 - m[2])) % steps
 
     def turned_row(columns):
         return pl.BlockSpec((rows, columns), lambda i, m: (moved(i, m), 0))
@@ -1005,59 +1026,53 @@
     half1_row = pl.BlockSpec(
         (rows, features), lambda i, m: (jnp.maximum(moved(i, m) - half_steps, 0), 0)
     )
-    attended_rows = [turned_row(features)] + [half0_row, half1_row] * 2
-    moved_block = pl.BlockSpec(
-        turned_shape + (rows,), lambda i, m: (0, 0, 0, 0, 0, moved(i, m))
-    )
+    moved_block = pl.BlockSpec(turned_shape + (rows,), lambda i, m: (0, 0, 0, 0, 0, moved(i, m)))
     send_row = pl.BlockSpec((rows, features), lambda i, m: (jnp.minimum(i, half_steps - 1), 0))
-    keep_row = pl.BlockSpec((rows, features), lambda i, m: (jnp.maximum(i - half_steps, 0), 0))
+    keep_row = pl.BlockSpec(
+        (rows, features),
+        lambda i, m: (jnp.clip(i - half_steps, 0, half_steps - 1), 0),
+    )
+
+    def grads_block(first):
+        return pl.BlockSpec(
+            (features // 2, chunk), lambda i, m: (0, jnp.clip(i - steps - first, 0, 2))
+        )
+
     full_block = (count // 4, 2, 2, block_rows, 3 * chunk)
     half_block = (features // 2, 3 * chunk)
-    feed_x_turned, feed_y_turned, g_turned, hidden, d_gate_up, dn_part, out_send, out_own = call(
-        feed_body,
-        (steps,),
-        attended_rows
+    half_grads = shaped((features // 2, 3 * chunk), LOW)
+    unit_f, scale_f, dn_part, out_send, out_own, gu_own, gu_send, ud_own, ud_send = call(
+        functools.partial(feed_body, steps),
+        (steps + 6,),
+        [turned_row(features)]
+        + [half0_row, half1_row] * 2
         + [turned_row(features), whole((1, features))]
         + [whole(half_block)] * 4,
+        [turned_row(features), turned_row(LANES), turned_row(features), send_row, keep_row]
+        + [grads_block(0)] * 2
+        + [grads_block(3)] * 2,
         [
-            moved_block,
-            moved_block,
-            moved_block,
-            turned_row(units),
-            turned_row(2 * units),
-            turned_row(features),
-            send_row,
-            keep_row,
-        ],
-        [
-            turned,
-            turned,
-            turned,
-            shaped((seq_len, units), LOW),
-            shaped((seq_len, 2 * units), LOW),
+            shaped((seq_len, features), LOW),
+            shaped((seq_len, LANES), HIGH),
             shaped((seq_len, features), LOW),
             shaped((own_rows, features), LOW),
             shaped((own_rows, features), HIGH),
-        ],
-        [pltpu.VMEM(full_block, LOW), pltpu.VMEM(full_block, LOW)],
+        ]
+        + [half_grads] * 4,
+        [pltpu.VMEM(full_block, LOW), pltpu.VMEM(full_block, LOW)]
+        + [pltpu.VMEM(turned_shape + (seq_len,), LOW)] * 3
+        + [pltpu.VMEM((seq_len, units), LOW), pltpu.VMEM((seq_len, 2 * units), LOW)],
         prefetch=1,
-        micros=19,
+        micros=28,
     )(place, x_all, *parts, g_all, gain_f, gu_own, gu_other, ud_own, ud_other)
     dn_other = swapped(dn_part)
-
-    gu_own, gu_send = weight_grads_one(feed_x_turned, d_gate_up, 3 * chunk // 2, 2, 5.5)
-    gu_send, hidden, dn_other = together(gu_send, hidden, dn_other)
     gu_came = over_x(gu_send)
-    ud_own, ud_send = weight_grads(
-        (feed_y_turned, d_gate_up, 3, 1), (g_turned, hidden, 0, 2), chunk, 6.5
-    )
-    ud_send, dn_other = together(ud_send, dn_other)
     ud_came = over_y(ud_send)
 
     d_attended, d_low_turned, d_mixed, d_gain_f = call(
         turn_body,
         (steps,),
-        attended_rows
+        [turned_row(features), turned_row(LANES)]
         + [turned_row(features)] * 3
         + [whole((1, features)), whole((features, width))],
         [keep_row, moved_block, turned_row(width), result((1, features))],
@@ -1069,7 +1084,7 @@
         ],
         prefetch=1,
         micros=4,
-    )(place, x_all, *parts, g_all, dn_part, dn_other, gain_f, w_o)
+    )(place, unit_f, scale_f, g_all, dn_part, dn_other, gain_f, w_o)
     out_other = swapped(out_send)
 
     d_query, d_key, d_value, d_strip = call(

time: 223 us -> 219 us (0.982)
  Pallas kernels: 107 us -> 100 us
  waiting for transfers between devices: 40.2 us -> 43.2 us
    pallas_call x3 -> x2, Pallas kernels: 18.3 us -> 10.5 us  [weight_grads(): call(functools.partial(grads_body, count0), (steps,), [whole((height, dep...]
    pallas_call x3 -> x2, Pallas kernels: 34.7 us -> 35.9 us  [the longest x1 28.3 us: on_core_pair(): call(functools.partial(feed_body, steps), (steps + 6,), [turned_row(featu...]
  transfers between devices with their start and end apart: 38 -> 38, of which waited for: 21 -> 24; matrix products, arithmetic and copies ran while one was open for 5% -> 5% of each run, Pallas kernels for 36% -> 33%
where the time goes in v5:
time: 219 us; the launch traced here: 218 us
  Pallas kernels  100 us (46%)
  starting transfers between devices  52.5 us (24%)
  waiting for transfers between devices  43.2 us (20%)
  other arithmetic  10.2 us (5%)
  local copies, waits for them, and re-layouts  9.46 us (4%)
    pallas_call x1, Pallas kernels, on_core_pair(): call(functools.partial(feed_body, steps), (steps + 6,), [turned_row(featu...  28.3 us
    ppermute x9, starting transfers between devices, over_far(): return lax.ppermute(array, 'dp', ring_shift(4 * steps, lax.axis_size('dp')))  25.3 us
    pallas_call x1, Pallas kernels, on_core_pair(): call(attend_body, (pairs,), [pair_block, pair_block, pair_block, strip_bl...  17.7 us
    ppermute x9, waiting for transfers between devices, over_far(): return lax.ppermute(array, 'dp', ring_shift(4 * steps, lax.axis_size('dp')))  16.8 us
    pallas_call x1, Pallas kernels, on_core_pair(): call(backward_body, (pairs,), [pair_block, pair_block, pair_block, e_bloc...  16.7 us
    ppermute x9, starting transfers between devices, over_x(): return lax.ppermute(array, 'dp', flip(1, lax.axis_size('dp')))  11.8 us
    pallas_call x2, Pallas kernels, weight_grads(): call(functools.partial(grads_body, count0), (steps,), [whole((height, dep...  10.5 us
    ppermute x9, waiting for transfers between devices, over_y(): return lax.ppermute(array, 'dp', flip(2, lax.axis_size('dp')))  10.1 us
  transfers between devices with their start and end apart: 38, of which 24 were waited for; matrix products, arithmetic and copies ran while one was open for 5% of the time, Pallas kernels for 33%

profile of v5, /device:TPU:0, one launch (start us, length us, event | category | flops | bytes accessed | tf_op | source)
XLA Modules:
  0.0 218.4 jit_solution(18094693457837218857)
XLA Ops:
  1.7 3.1 %collective-permute-start = (bf16[48,1536]{1,0:T(8,128)(2,1)S(1)}, bf16[48,1536]{1,0:T(8,128)(2,1)S(1)}, u32[]{:S(2)}, u32[]{:S(2)}) collective-permute-start(bf16[48,1536]{1,0:T(8,128)(2,1)S(1)} %pad_maximum_fusion.11), channel_id=1, source_target_pairs={{0,8},{2,10},{4,12},{6,14},{8,16},{10,18},{12,20},{14,22},{16,24},... | collective-permute-start | bytes 442376 | tf_op jit(solution)/shard_map/ppermute | solution.py:394
  4.7 2.6 %collective-permute-start.1 = (bf16[48,1536]{1,0:T(8,128)(2,1)S(1)}, bf16[48,1536]{1,0:T(8,128)(2,1)S(1)}, u32[]{:S(2)}, u32[]{:S(2)}) collective-permute-start(bf16[48,1536]{1,0:T(8,128)(2,1)S(1)} %pad_maximum_fusion.11), channel_id=1, source_target_pairs={{0,16},{2,18},{4,20},{6,22},{8,24},{10,26},{12,28},{14,30},{16,0},... | collective-permute-start | bytes 442376 | tf_op jit(solution)/shard_map/ppermute | solution.py:394
  13.0 9.0 %collective-permute-start.10 = (bf16[48,3072]{1,0:T(8,128)(2,1)S(1)}, bf16[48,3072]{1,0:T(8,128)(2,1)S(1)}, u32[]{:S(2)}, u32[]{:S(2)}) collective-permute-start(bf16[48,3072]{1,0:T(8,128)(2,1)S(1)} %pad_maximum_fusion.7), channel_id=1, source_target_pairs={{0,16},{2,18},{4,20},{6,22},{8,24},{10,26},{12,28},{14,30},{16,0},... | collective-permute-start | bytes 884744 | tf_op jit(solution)/shard_map/ppermute | solution.py:394
  26.2 3.6 %collective-permute-done.3 = bf16[192,768]{1,0:T(8,128)(2,1)S(1)} collective-permute-done((bf16[192,768]{1,0:T(8,128)(2,1)S(1)}, bf16[192,768]{1,0:T(8,128)(2,1)S(1)}, u32[]{:S(2)}, u32[]{:S(2)}) %collective-permute-start.3) | collective-permute-done | bytes 294944 | tf_op jit(solution)/shard_map/ppermute | solution.py:386
  29.8 4.1 %collective-permute-start.11 = (bf16[48,3072]{1,0:T(8,128)(2,1)S(1)}, bf16[48,3072]{1,0:T(8,128)(2,1)S(1)}, u32[]{:S(2)}, u32[]{:S(2)}) collective-permute-start(bf16[48,3072]{1,0:T(8,128)(2,1)S(1)} %pad_maximum_fusion.7), channel_id=1, source_target_pairs={{0,24},{2,26},{4,28},{6,30},{8,0},{10,2},{12,4},{14,6},{16,8},{18,... | collective-permute-start | bytes 884744 | tf_op jit(solution)/shard_map/ppermute | solution.py:394
  40.3 1.8 collective-permute-done.11
  42.1 4.6 %collective-permute-done.9 = bf16[48,3072]{1,0:T(8,128)(2,1)S(1)} collective-permute-done((bf16[48,3072]{1,0:T(8,128)(2,1)S(1)}, bf16[48,3072]{1,0:T(8,128)(2,1)S(1)}, u32[]{:S(2)}, u32[]{:S(2)}) %collective-permute-start.9) | collective-permute-done | bytes 294944 | tf_op jit(solution)/shard_map/ppermute | solution.py:394
  46.7 2.5 %collective-permute-done.6.vo_other_ref = bf16[384,768]{1,0:T(8,128)(2,1)S(1)} collective-permute-done((bf16[384,768]{1,0:T(8,128)(2,1)S(1)}, bf16[384,768]{1,0:T(8,128)(2,1)S(1)}, u32[]{:S(2)}, u32[]{:S(2)}) %collective-permute-start.6) | collective-permute-done | bytes 589856 | tf_op jit(solution)/shard_map/ppermute | solution.py:386
  53.3 8.5 %shard_map.220 = (bf16[2,2,2,2,48,1024]{5,4,3,2,1,0:T(8,128)(2,1)}, bf16[2,2,2,2,48,1024]{5,4,3,2,1,0:T(8,128)(2,1)}, bf16[1024,384]{1,0:T(8,128)(2,1)}, bf16[10...) custom-call(s32[4]{0:T(128)} %pad_add_fusion.place_ref, ...), custom_call_target="tpu_custom_call" | custom-call | flops 8074500096 | tf_op jit(solution)/shard_map/pallas_call | solution.py:965
  66.8 17.7 %shard_map.221 = (bf16[6,1024,1024]{2,1,0:T(8,128)(2,1)}, f32[1024,384]{1,0:T(8,128)}, bf16[1024,384]{1,0:T(8,128)(2,1)}, f32[1024,384]{1,0:T(8,128)}, bf16[512,...) custom-call(bf16[1024,384]{1,0:T(8,128)(2,1)} %get-tuple-element.105.q_ref, bf16[1024,384]{1,0:T(8,128)(2,1)} %get-tuple-element.106.k_ref, ...), custom_call_target="tpu_custom_call" | custom-call | flops 23069999104 | tf_op jit(solution)/shard_map/pallas_call | solution.py:990
  90.5 28.3 %shard_map.222 = (bf16[1024,768]{1,0:T(8,128)(2,1)}, f32[1024,128]{1,0:T(8,128)}, bf16[1024,768]{1,0:T(8,128)(2,1)}, bf16[512,768]{1,0:T(8,128)(2,1)}, f32[512,7...) custom-call(s32[4]{0:T(128)} %pad_add_fusion.place_ref, ...), custom_call_target="tpu_custom_call" | custom-call | flops 32298000384 | tf_op jit(solution)/shard_map/pallas_call | solution.py:1044
  122.6 7.6 %shard_map.223 = (f32[512,768]{1,0:T(8,128)}, bf16[2,2,2,2,48,1024]{5,4,3,2,1,0:T(8,128)(2,1)}, bf16[1024,384]{1,0:T(8,128)(2,1)}, f32[1,768]{1,0:T(1,128)}) custom-call(s32[4]{0:T(128)} %pad_add_fusion.place_ref, bf16[1024,768]{1,0:T(8,128)(2,1)} %get-tuple-element.123.unit_ref, f32[1024,128]{1,0:T(8,128)} %get-tuple-element.124.scale_ref, ...), custom_call_target="tpu_custom_call" | custom-call | flops 4614000128 | tf_op jit(solution)/shard_map/pallas_call | solution.py:1072
  130.2 16.7 %shard_map.224 = (bf16[1024,384]{1,0:T(8,128)(2,1)}, bf16[1024,384]{1,0:T(8,128)(2,1)}, bf16[1024,384]{1,0:T(8,128)(2,1)}, f32[3,2,2048]{2,1,0:T(2,128)}) custom-call(bf16[1024,384]{1,0:T(8,128)(2,1)} %get-tuple-element.105.q_ref, bf16[1024,384]{1,0:T(8,128)(2,1)} %get-tuple-element.106.k_ref, bf16[1024,384]{1,0:T(8,128)(2,1)} %get-tuple-element.107.v_ref, ...), custom_call_target="tpu_custom_call" | custom-call | flops 4614000128 | tf_op jit(solution)/shard_map/pallas_call | solution.py:1090
  153.0 5.3 %shard_map.225 = (bf16[384,768]{1,0:T(8,128)(2,1)}, bf16[384,768]{1,0:T(8,128)(2,1)}) custom-call(bf16[768,1024]{1,0:T(8,128)(2,1)} %bitcast.41, bf16[768,1024]{1,0:T(8,128)(2,1)} %bitcast.42, bf16[1024,384]{1,0:T(8,128)(2,1)} %get-tuple-element.154.right0_ref.dq_ref, bf16[1024,384]{1,0:T(8,128)(2,1)} %get-tuple-element.136.right1_ref.dk_ref), custom_call_target="tpu_custom_call" | custom-call | flops 5767499776 | tf_op jit(solution)/shard_map/pallas_call | solution.py:868
  158.3 5.2 %shard_map.226 = (bf16[384,768]{1,0:T(8,128)(2,1)}, bf16[384,768]{1,0:T(8,128)(2,1)}) custom-call(bf16[768,1024]{1,0:T(8,128)(2,1)} %bitcast.40, bf16[768,1024]{1,0:T(8,128)(2,1)} %bitcast.43, bf16[1024,384]{1,0:T(8,128)(2,1)} %get-tuple-element.147.right0_ref.dv_ref, bf16[1024,384]{1,0:T(8,128)(2,1)} %get-tuple-element.148.right1_ref), custom_call_target="tpu_custom_call" | custom-call | flops 5767499776 | tf_op jit(solution)/shard_map/pallas_call | solution.py:868
  166.1 1.7 collective-permute-start.26
  169.2 7.8 %shard_map.227 = (bf16[512,768]{1,0:T(8,128)(2,1)}, f32[512,768]{1,0:T(8,128)}, f32[1,768]{1,0:T(1,128)}) custom-call(s32[4]{0:T(128)} %pad_add_fusion.place_ref, bf16[1024,768]{1,0:T(8,128)(2,1)} %pad_maximum_fusion.x_ref, bf16[1024,384]{1,0:T(8,128)(2,1)} %get-tuple-element.154.right0_ref.dq_ref, bf16[1024,384]{1,0:T(8,128)(2,1)} %get-tuple-element.136.right1_ref.dk_ref, ...), custom_call_target="tpu_custom_call" | custom-call | flops 8074500096 | tf_op jit(solution)/shard_map/pallas_call | solution.py:1135
  177.1 3.3 %collective-permute-done.26 = bf16[96,3072]{1,0:T(8,128)(2,1)S(1)} collective-permute-done((bf16[96,3072]{1,0:T(8,128)(2,1)S(1)}, bf16[96,3072]{1,0:T(8,128)(2,1)S(1)}, u32[]{:S(2)}, u32[]{:S(2)}) %collective-permute-start.26) | collective-permute-done | bytes 589856 | tf_op jit(solution)/shard_map/ppermute | solution.py:422
  185.7 1.7 collective-permute-start.32
  194.0 3.4 %shard_map.228 = bf16[512,768]{1,0:T(8,128)(2,1)} custom-call(bf16[512,768]{1,0:T(8,128)(2,1)} %x_ref.1, f32[512,768]{1,0:T(8,128)} %get-tuple-element.163.own_ref, bf16[512,768]{1,0:T(8,128)(2,1)} %copy-done.28, f32[512,768]{1,0:T(8,128)} %get-tuple-element.165.datt_ref, f32[1,768]{1,0:T(1,128)} %reshape.67.gain_ref), custom_call_target="tpu_custom_call" | custom-call | flops 4037250048 | tf_op jit(solution)/shard_map/pallas_call | solution.py:1171
  197.4 3.1 %collective-permute-done.29 = bf16[48,3072]{1,0:T(8,128)(2,1)S(1)} collective-permute-done((bf16[48,3072]{1,0:T(8,128)(2,1)S(1)}, bf16[48,3072]{1,0:T(8,128)(2,1)S(1)}, u32[]{:S(2)}, u32[]{:S(2)}) %collective-permute-start.29) | collective-permute-done | bytes 294944 | tf_op jit(solution)/shard_map/ppermute | solution.py:422
  201.0 2.3 %collective-permute-start.36 = (bf16[56,1536]{1,0:T(8,128)(2,1)S(1)}, bf16[56,1536]{1,0:T(8,128)(2,1)S(1)}, u32[]{:S(2)}, u32[]{:S(2)}) collective-permute-start(bf16[56,1536]{1,0:T(8,128)(2,1)S(1)} %get-tuple-element.229), channel_id=1, source_target_pairs={{0,16},{2,18},{4,20},{6,22},{8,24},{10,26},{12,28},{14,30},{16,0},... | collective-permute-start | bytes 516104 | tf_op jit(solution)/shard_map/ppermute | solution.py:394
  205.7 4.4 %collective-permute-done.35 = bf16[56,1536]{1,0:T(8,128)(2,1)S(1)} collective-permute-done((bf16[56,1536]{1,0:T(8,128)(2,1)S(1)}, bf16[56,1536]{1,0:T(8,128)(2,1)S(1)}, u32[]{:S(2)}, u32[]{:S(2)}) %collective-permute-start.35) | collective-permute-done | bytes 172064 | tf_op jit(solution)/shard_map/ppermute | solution.py:394
  210.2 6.0 %collective-permute-done.36 = bf16[56,1536]{1,0:T(8,128)(2,1)S(1)} collective-permute-done((bf16[56,1536]{1,0:T(8,128)(2,1)S(1)}, bf16[56,1536]{1,0:T(8,128)(2,1)S(1)}, u32[]{:S(2)}, u32[]{:S(2)}) %collective-permute-start.36) | collective-permute-done | bytes 172064 | tf_op jit(solution)/shard_map/ppermute | solution.py:394
  (197 shorter events, 62.9 us)
Async XLA Ops:
  4.7 17.2 %collective-permute-start.1 = (bf16[48,1536]{1,0:T(8,128)(2,1)S(1)}, bf16[48,1536]{1,0:T(8,128)(2,1)S(1)}, u32[]{:S(2)}, u32[]{:S(2)}) collective-permute-start(bf16[48,1536]{1,0:T(8,128)(2,1)S(1)} %pad_maximum_fusion.11), channel_id=1, source_target_pairs={{0,16},{2,18},{4,20},{6,22},{8,24},{10,26},{12,28},{14,30},{16,0},... | collective-permute-start | bytes 442376 | tf_op jit(solution)/shard_map/ppermute | solution.py:394
  7.3 14.6 %collective-permute-start.2 = (bf16[48,1536]{1,0:T(8,128)(2,1)S(1)}, bf16[48,1536]{1,0:T(8,128)(2,1)}, u32[]{:S(2)}, u32[]{:S(2)}) collective-permute-start(bf16[48,1536]{1,0:T(8,128)(2,1)S(1)} %pad_maximum_fusion.11), channel_id=1, source_target_pairs={{0,24},{2,26},{4,28},{6,30},{8,0},{10,2},{12,4},{14,6},{16,8},{18,... | collective-permute-start | bytes 442376 | tf_op jit(solution)/shard_map/ppermute | solution.py:394
  8.7 26.8 %collective-permute-start.7 = (bf16[512,768]{1,0:T(8,128)(2,1)}, bf16[512,768]{1,0:T(8,128)(2,1)S(1)}, u32[]{:S(2)}, u32[]{:S(2)}) collective-permute-start(bf16[512,768]{1,0:T(8,128)(2,1)} %x_ref.1), channel_id=1, source_target_pairs={{0,1},{1,0},{2,3},{3,2},{4,5},{5,4},{6,7},{7,6},{8,9},{9,8},{10,11... | collective-permute-start | bytes 2359304 | tf_op jit(solution)/shard_map/ppermute | solution.py:916
  8.7 27.3 %collective-permute-start.8 = (bf16[512,768]{1,0:T(8,128)(2,1)}, bf16[512,768]{1,0:T(8,128)(2,1)S(1)}, u32[]{:S(2)}, u32[]{:S(2)}) collective-permute-start(bf16[512,768]{1,0:T(8,128)(2,1)} %param.14), channel_id=1, source_target_pairs={{0,1},{1,0},{2,3},{3,2},{4,5},{5,4},{6,7},{7,6},{8,9},{9,8},{10,11... | collective-permute-start | bytes 2359304 | tf_op jit(solution)/shard_map/ppermute | solution.py:916
  13.0 27.3 %collective-permute-start.10 = (bf16[48,3072]{1,0:T(8,128)(2,1)S(1)}, bf16[48,3072]{1,0:T(8,128)(2,1)S(1)}, u32[]{:S(2)}, u32[]{:S(2)}) collective-permute-start(bf16[48,3072]{1,0:T(8,128)(2,1)S(1)} %pad_maximum_fusion.7), channel_id=1, source_target_pairs={{0,16},{2,18},{4,20},{6,22},{8,24},{10,26},{12,28},{14,30},{16,0},... | collective-permute-start | bytes 884744 | tf_op jit(solution)/shard_map/ppermute | solution.py:394
  29.8 12.3 %collective-permute-start.11 = (bf16[48,3072]{1,0:T(8,128)(2,1)S(1)}, bf16[48,3072]{1,0:T(8,128)(2,1)S(1)}, u32[]{:S(2)}, u32[]{:S(2)}) collective-permute-start(bf16[48,3072]{1,0:T(8,128)(2,1)S(1)} %pad_maximum_fusion.7), channel_id=1, source_target_pairs={{0,24},{2,26},{4,28},{6,30},{8,0},{10,2},{12,4},{14,6},{16,8},{18,... | collective-permute-start | bytes 884744 | tf_op jit(solution)/shard_map/ppermute | solution.py:394
  33.9 12.8 %collective-permute-start.9 = (bf16[48,3072]{1,0:T(8,128)(2,1)S(1)}, bf16[48,3072]{1,0:T(8,128)(2,1)S(1)}, u32[]{:S(2)}, u32[]{:S(2)}) collective-permute-start(bf16[48,3072]{1,0:T(8,128)(2,1)S(1)} %pad_maximum_fusion.7), channel_id=1, source_target_pairs={{0,8},{2,10},{4,12},{6,14},{8,16},{10,18},{12,20},{14,22},{16,24},... | collective-permute-start | bytes 884744 | tf_op jit(solution)/shard_map/ppermute | solution.py:394
  35.4 13.8 %collective-permute-start.6 = (bf16[384,768]{1,0:T(8,128)(2,1)S(1)}, bf16[384,768]{1,0:T(8,128)(2,1)S(1)}, u32[]{:S(2)}, u32[]{:S(2)}) collective-permute-start(bf16[384,768]{1,0:T(8,128)(2,1)S(1)} %pad_maximum_fusion.5.vo_own_ref), channel_id=1, source_target_pairs={{0,4},{2,6},{4,0},{6,2},{8,12},{10,14},{12,8},{14,10},{16,20},{18,... | collective-permute-start | bytes 1769480 | tf_op jit(solution)/shard_map/ppermute | solution.py:386
  36.0 13.5 %collective-permute-start.5 = (bf16[384,768]{1,0:T(8,128)(2,1)S(1)}, bf16[384,768]{1,0:T(8,128)(2,1)S(1)}, u32[]{:S(2)}, u32[]{:S(2)}) collective-permute-start(bf16[384,768]{1,0:T(8,128)(2,1)S(1)} %pad_maximum_fusion.4.qk_own_ref), channel_id=1, source_target_pairs={{0,2},{2,0},{4,6},{6,4},{8,10},{10,8},{12,14},{14,12},{16,18},{18,... | collective-permute-start | bytes 1769480 | tf_op jit(solution)/shard_map/ppermute | solution.py:382
  50.4 12.7 %collective-permute-start.12 = (bf16[192,1536]{1,0:T(8,128)(2,1)S(1)}, bf16[192,1536]{1,0:T(8,128)(2,1)S(1)}, u32[]{:S(2)}, u32[]{:S(2)}) collective-permute-start(bf16[192,1536]{1,0:T(8,128)(2,1)S(1)} %get-tuple-element.209), channel_id=1, source_target_pairs={{0,4},{2,6},{4,0},{6,2},{8,12},{10,14},{12,8},{14,10},{16,20},{18,... | collective-permute-start | bytes 1769480 | tf_op jit(solution)/shard_map/ppermute | solution.py:386
  51.8 12.2 %collective-permute-start.13 = (bf16[192,1536]{1,0:T(8,128)(2,1)S(1)}, bf16[192,1536]{1,0:T(8,128)(2,1)S(1)}, u32[]{:S(2)}, u32[]{:S(2)}) collective-permute-start(bf16[192,1536]{1,0:T(8,128)(2,1)S(1)} %get-tuple-element.208), channel_id=1, source_target_pairs={{0,2},{2,0},{4,6},{6,4},{8,10},{10,8},{12,14},{14,12},{16,18},{18,... | collective-permute-start | bytes 1769480 | tf_op jit(solution)/shard_map/ppermute | solution.py:382
  64.3 24.0 %collective-permute-start.15 = (bf16[384,1536]{1,0:T(8,128)(2,1)S(1)}, bf16[384,1536]{1,0:T(8,128)(2,1)S(1)}, u32[]{:S(2)}, u32[]{:S(2)}) collective-permute-start(bf16[384,1536]{1,0:T(8,128)(2,1)S(1)} %pad_maximum_fusion.3.ud_own_ref), channel_id=1, source_target_pairs={{0,4},{2,6},{4,0},{6,2},{8,12},{10,14},{12,8},{14,10},{16,20},{18,... | collective-permute-start | bytes 3538952 | tf_op jit(solution)/shard_map/ppermute | solution.py:386
  65.3 24.0 %collective-permute-start.14 = (bf16[384,1536]{1,0:T(8,128)(2,1)S(1)}, bf16[384,1536]{1,0:T(8,128)(2,1)S(1)}, u32[]{:S(2)}, u32[]{:S(2)}) collective-permute-start(bf16[384,1536]{1,0:T(8,128)(2,1)S(1)} %pad_maximum_fusion.2.gu_own_ref), channel_id=1, source_target_pairs={{0,2},{2,0},{4,6},{6,4},{8,10},{10,8},{12,14},{14,12},{16,18},{18,... | collective-permute-start | bytes 3538952 | tf_op jit(solution)/shard_map/ppermute | solution.py:382
  119.0 28.4 %collective-permute-start.18 = (bf16[384,1536]{1,0:T(8,128)(2,1)}, bf16[384,1536]{1,0:T(8,128)(2,1)S(1)}, u32[]{:S(2)}, u32[]{:S(2)}) collective-permute-start(bf16[384,1536]{1,0:T(8,128)(2,1)} %get-tuple-element.119), channel_id=1, source_target_pairs={{0,2},{2,0},{4,6},{6,4},{8,10},{10,8},{12,14},{14,12},{16,18},{18,... | collective-permute-start | bytes 3538952 | tf_op jit(solution)/shard_map/ppermute | solution.py:382
  120.3 28.2 %collective-permute-start.19 = (bf16[384,1536]{1,0:T(8,128)(2,1)}, bf16[384,1536]{1,0:T(8,128)(2,1)S(1)}, u32[]{:S(2)}, u32[]{:S(2)}) collective-permute-start(bf16[384,1536]{1,0:T(8,128)(2,1)} %get-tuple-element.120), channel_id=1, source_target_pairs={{0,4},{2,6},{4,0},{6,2},{8,12},{10,14},{12,8},{14,10},{16,20},{18,... | collective-permute-start | bytes 3538952 | tf_op jit(solution)/shard_map/ppermute | solution.py:386
  121.6 25.3 %collective-permute-start.20 = (bf16[512,768]{1,0:T(8,128)(2,1)}, bf16[512,768]{1,0:T(8,128)(2,1)S(1)}, u32[]{:S(2)}, u32[]{:S(2)}) collective-permute-start(bf16[512,768]{1,0:T(8,128)(2,1)} %get-tuple-element.121), channel_id=1, source_target_pairs={{0,1},{1,0},{2,3},{3,2},{4,5},{5,4},{6,7},{7,6},{8,9},{9,8},{10,11... | collective-permute-start | bytes 2359304 | tf_op jit(solution)/shard_map/ppermute | solution.py:916
  149.7 14.8 %collective-permute-start.23 = (bf16[192,1536]{1,0:T(8,128)(2,1)}, bf16[192,1536]{1,0:T(8,128)(2,1)S(1)}, u32[]{:S(2)}, u32[]{:S(2)}) collective-permute-start(bf16[192,1536]{1,0:T(8,128)(2,1)} %get-tuple-element.189), channel_id=1, source_target_pairs={{0,2},{2,0},{4,6},{6,4},{8,10},{10,8},{12,14},{14,12},{16,18},{18,... | collective-permute-start | bytes 1769480 | tf_op jit(solution)/shard_map/ppermute | solution.py:382
  150.6 15.1 %collective-permute-start.22 = (bf16[192,1536]{1,0:T(8,128)(2,1)S(1)}, bf16[192,1536]{1,0:T(8,128)(2,1)S(1)}, u32[]{:S(2)}, u32[]{:S(2)}) collective-permute-start(bf16[192,1536]{1,0:T(8,128)(2,1)S(1)} %get-tuple-element.187), channel_id=1, source_target_pairs={{0,4},{2,6},{4,0},{6,2},{8,12},{10,14},{12,8},{14,10},{16,20},{18,... | collective-permute-start | bytes 1769480 | tf_op jit(solution)/shard_map/ppermute | solution.py:386
  166.1 14.3 %collective-permute-start.26 = (bf16[96,3072]{1,0:T(8,128)(2,1)S(1)}, bf16[96,3072]{1,0:T(8,128)(2,1)S(1)}, u32[]{:S(2)}, u32[]{:S(2)}) collective-permute-start(bf16[96,3072]{1,0:T(8,128)(2,1)S(1)} %pad_maximum_fusion.6), channel_id=1, source_target_pairs={{0,8},{2,10},{4,12},{6,14},{8,0},{10,2},{12,4},{14,6},{16,24},{18,... | collective-permute-start | bytes 1769480 | tf_op jit(solution)/shard_map/ppermute | solution.py:422
  167.8 13.9 %collective-permute-start.24 = (bf16[384,768]{1,0:T(8,128)(2,1)S(1)}, bf16[384,768]{1,0:T(8,128)(2,1)S(1)}, u32[]{:S(2)}, u32[]{:S(2)}) collective-permute-start(bf16[384,768]{1,0:T(8,128)(2,1)S(1)} %copy-done.33), channel_id=1, source_target_pairs={{0,2},{2,0},{4,6},{6,4},{8,10},{10,8},{12,14},{14,12},{16,18},{18,... | collective-permute-start | bytes 1769480 | tf_op jit(solution)/shard_map/ppermute | solution.py:382
  168.4 13.4 %collective-permute-start.25 = (bf16[384,768]{1,0:T(8,128)(2,1)S(1)}, bf16[384,768]{1,0:T(8,128)(2,1)S(1)}, u32[]{:S(2)}, u32[]{:S(2)}) collective-permute-start(bf16[384,768]{1,0:T(8,128)(2,1)S(1)} %copy-done.34), channel_id=1, source_target_pairs={{0,4},{2,6},{4,0},{6,2},{8,12},{10,14},{12,8},{14,10},{16,20},{18,... | collective-permute-start | bytes 1769480 | tf_op jit(solution)/shard_map/ppermute | solution.py:386
  184.3 16.3 %collective-permute-start.29 = (bf16[48,3072]{1,0:T(8,128)(2,1)S(1)}, bf16[48,3072]{1,0:T(8,128)(2,1)S(1)}, u32[]{:S(2)}, u32[]{:S(2)}) collective-permute-start(bf16[48,3072]{1,0:T(8,128)(2,1)S(1)} %add_convert_fusion.9), channel_id=1, source_target_pairs={{0,16},{2,18},{4,20},{6,22},{8,24},{10,26},{12,28},{14,30},{16,0},... | collective-permute-start | bytes 884744 | tf_op jit(solution)/shard_map/ppermute | solution.py:422
  201.0 15.2 %collective-permute-start.36 = (bf16[56,1536]{1,0:T(8,128)(2,1)S(1)}, bf16[56,1536]{1,0:T(8,128)(2,1)S(1)}, u32[]{:S(2)}, u32[]{:S(2)}) collective-permute-start(bf16[56,1536]{1,0:T(8,128)(2,1)S(1)} %get-tuple-element.229), channel_id=1, source_target_pairs={{0,16},{2,18},{4,20},{6,22},{8,24},{10,26},{12,28},{14,30},{16,0},... | collective-permute-start | bytes 516104 | tf_op jit(solution)/shard_map/ppermute | solution.py:394
  203.2 12.9 %collective-permute-start.37 = (bf16[56,1536]{1,0:T(8,128)(2,1)S(1)}, bf16[56,1536]{1,0:T(8,128)(2,1)S(1)}, u32[]{:S(2)}, u32[]{:S(2)}) collective-permute-start(bf16[56,1536]{1,0:T(8,128)(2,1)S(1)} %get-tuple-element.230), channel_id=1, source_target_pairs={{0,24},{2,26},{4,28},{6,30},{8,0},{10,2},{12,4},{14,6},{16,8},{18,... | collective-permute-start | bytes 516104 | tf_op jit(solution)/shard_map/ppermute | solution.py:394
  (49 other events, 307.8 us)

commit v6 on v5

--- a/solution.py
+++ b/solution.py
@@ -1127,10 +1127,15 @@
     qk_came = over_x(qk_send)
     vo_came = over_y(vo_send)
     gu_own, gu_send = next_half(gu_own, gu_came, far_bit % 2)
-    ud_own, ud_send = next_half(ud_own, ud_came, far_bit % 2)
-    unit_own = jnp.concatenate([gu_own, ud_own], axis=1)
-    unit_send = jnp.concatenate([gu_send, ud_send], axis=1)
-    unit_came = over_far_bit(unit_send, 0)
+    gu_came = over_far_bit(gu_send, 0)
+
+    def inner_part(array, index):
+        blocks = array.reshape(2, 2, block_rows, -1)
+        return lax.dynamic_index_in_dim(blocks, index, 1, False).reshape(2 * block_rows, -1)
+
+    ud_send = add_low(inner_part(ud_own, 1 - far_bit // 2), inner_part(ud_came, 1 - far_bit // 2))
+    ud_own = add_low(inner_part(ud_own, far_bit // 2), inner_part(ud_came, far_bit // 2))
+    ud_came = over_far_bit(ud_send, 1)
 
     dna_send, dna_own, d_gain_a = call(
         spread_body,
@@ -1143,13 +1148,15 @@
             shaped((1, features), HIGH),
         ],
         prefetch=1,
-        micros=7,
+        micros=2,
     )(place, x_all, d_query, d_key, d_value, w_qkv)
-    qk_came, vo_came, unit_came, dna_send, d_gain_a, d_strip = together(
-        qk_came, vo_came, unit_came, dna_send, d_gain_a, d_strip
-    )
-    unit_own, unit_send = next_half(unit_own, unit_came, far_bit // 2)
-    unit_came = over_far_bit(unit_send, 1)
+    qk_came, vo_came, gu_came, ud_came, dna_send, d_gain_a, d_strip = together(
+        qk_came, vo_came, gu_came, ud_came, dna_send, d_gain_a, d_strip
+    )
+    gu_own, gu_send = next_half(gu_own, gu_came, far_bit // 2)
+    ud_own, ud_send = next_half(ud_own, ud_came, far_bit % 2)
+    gu_came = over_far_bit(gu_send, 1)
+    ud_came = over_far_bit(ud_send, 0)
     dna_other = swapped(dna_send)
     qk_own, qk_send = next_half(qk_own, qk_came, y_bit)
     vo_own, vo_send = next_half(vo_own, vo_came, x_bit)
@@ -1177,8 +1184,8 @@
         micros=3.5,
     )(tokens, dna_own, dna_other, d_attended, gain_a)
 
-    qk_came, vo_came, unit_came, d_tokens, small = together(
-        qk_came, vo_came, unit_came, d_tokens, small
+    qk_came, vo_came, gu_came, ud_came, small = together(
+        qk_came, vo_came, gu_came, ud_came, small
     )
     head_own = jnp.concatenate([qk_own, vo_own], axis=-1)
     head_came = jnp.concatenate([qk_came, vo_came], axis=-1)
@@ -1192,12 +1199,14 @@
         over_far(jnp.concatenate([far_part((far_bit + k) % 4), small_rows], axis=0), k)
         for k in range(1, 4)
     ]
+    *pieces, d_tokens = together(*pieces, d_tokens)
     small = sum((from_terms(piece[block_rows:], small.shape[0]) for piece in pieces), small)
     small = small.reshape(-1)
     pieces = [piece[:block_rows] for piece in pieces]
     grads_head = sum((piece.astype(HIGH) for piece in pieces), far_part(far_bit).astype(HIGH))
     grads_qk, grads_vo = grads_head[:, : 2 * width], grads_head[:, 2 * width :]
-    grads_unit = unit_own.astype(HIGH) + unit_came.astype(HIGH)
+    grads_gu = gu_own.astype(HIGH) + gu_came.astype(HIGH)
+    grads_ud = ud_own.astype(HIGH) + ud_came.astype(HIGH)
     return (
         output,
         d_tokens,
@@ -1208,9 +1217,9 @@
         grads_vo[:, width:].T,
         small[2 * features : 2 * features + rel_table.size].reshape(rel_table.shape),
         small[features : 2 * features],
-        grads_unit[:, :units],
-        grads_unit[:, units : 2 * units],
-        grads_unit[:, 2 * units :].T,
+        grads_gu[:, :units],
+        jnp.concatenate([grads_gu[:, units:], grads_ud[:, :chunk]], axis=1),
+        grads_ud[:, chunk:].T,
     )
 
 

time: 219 us -> 217 us (level)
  waiting for transfers between devices: 43.2 us -> 36.6 us
  starting transfers between devices: 52.5 us -> 55.8 us
    ppermute x9, waiting for transfers between devices: 16.8 us -> 10.3 us  [over_far(): return lax.ppermute(array, 'dp', ring_shift(4 * steps, lax.axis_size('dp')))]
    ppermute x2 -> x4, waiting for transfers between devices: 6.46 us -> 3.34 us  [over_far_bit(): return lax.ppermute(array, 'dp', flip(4 << bit, lax.axis_size('dp')))]
    ppermute x2 -> x4, starting transfers between devices: 2.94 us -> 5.98 us  [over_far_bit(): return lax.ppermute(array, 'dp', flip(4 << bit, lax.axis_size('dp')))]
  transfers between devices with their start and end apart: 38 -> 40, of which waited for: 24 -> 25; matrix products, arithmetic and copies ran while one was open for 5% -> 6% of each run, Pallas kernels for 33% -> 33%
where the time goes in v6:
time: 217 us; the launch traced here: 216 us
  Pallas kernels  101 us (47%)
  starting transfers between devices  55.8 us (26%)
  waiting for transfers between devices  36.6 us (17%)
  local copies, waits for them, and re-layouts  10.3 us (5%)
  other arithmetic  10 us (5%)
    pallas_call x1, Pallas kernels, on_core_pair(): call(functools.partial(feed_body, steps), (steps + 6,), [turned_row(featu...  28.3 us
    ppermute x9, starting transfers between devices, over_far(): return lax.ppermute(array, 'dp', ring_shift(4 * steps, lax.axis_size('dp')))  25.5 us
    pallas_call x1, Pallas kernels, on_core_pair(): call(attend_body, (pairs,), [pair_block, pair_block, pair_block, strip_bl...  17.7 us
    pallas_call x1, Pallas kernels, on_core_pair(): call(backward_body, (pairs,), [pair_block, pair_block, pair_block, e_bloc...  16.7 us
    ppermute x9, starting transfers between devices, over_x(): return lax.ppermute(array, 'dp', flip(1, lax.axis_size('dp')))  11.8 us
    ppermute x9, waiting for transfers between devices, over_y(): return lax.ppermute(array, 'dp', flip(2, lax.axis_size('dp')))  11.1 us
    pallas_call x2, Pallas kernels, weight_grads(): call(functools.partial(grads_body, count0), (steps,), [whole((height, dep...  10.6 us
    ppermute x9, waiting for transfers between devices, over_far(): return lax.ppermute(array, 'dp', ring_shift(4 * steps, lax.axis_size('dp')))  10.3 us
  transfers between devices with their start and end apart: 40, of which 25 were waited for; matrix products, arithmetic and copies ran while one was open for 6% of the time, Pallas kernels for 33%

profile of v6, /device:TPU:0, one launch (start us, length us, event | category | flops | bytes accessed | tf_op | source)
XLA Modules:
  0.0 216.1 jit_solution(513267546631252173)
XLA Ops:
  1.7 3.1 %collective-permute-start = (bf16[48,1536]{1,0:T(8,128)(2,1)S(1)}, bf16[48,1536]{1,0:T(8,128)(2,1)S(1)}, u32[]{:S(2)}, u32[]{:S(2)}) collective-permute-start(bf16[48,1536]{1,0:T(8,128)(2,1)S(1)} %pad_maximum_fusion.11), channel_id=1, source_target_pairs={{0,8},{2,10},{4,12},{6,14},{8,16},{10,18},{12,20},{14,22},{16,24},... | collective-permute-start | bytes 442376 | tf_op jit(solution)/shard_map/ppermute | solution.py:394
  4.7 2.6 %collective-permute-start.1 = (bf16[48,1536]{1,0:T(8,128)(2,1)S(1)}, bf16[48,1536]{1,0:T(8,128)(2,1)S(1)}, u32[]{:S(2)}, u32[]{:S(2)}) collective-permute-start(bf16[48,1536]{1,0:T(8,128)(2,1)S(1)} %pad_maximum_fusion.11), channel_id=1, source_target_pairs={{0,16},{2,18},{4,20},{6,22},{8,24},{10,26},{12,28},{14,30},{16,0},... | collective-permute-start | bytes 442376 | tf_op jit(solution)/shard_map/ppermute | solution.py:394
  13.0 9.0 %collective-permute-start.10 = (bf16[48,3072]{1,0:T(8,128)(2,1)S(1)}, bf16[48,3072]{1,0:T(8,128)(2,1)S(1)}, u32[]{:S(2)}, u32[]{:S(2)}) collective-permute-start(bf16[48,3072]{1,0:T(8,128)(2,1)S(1)} %pad_maximum_fusion.6), channel_id=1, source_target_pairs={{0,16},{2,18},{4,20},{6,22},{8,24},{10,26},{12,28},{14,30},{16,0},... | collective-permute-start | bytes 884744 | tf_op jit(solution)/shard_map/ppermute | solution.py:394
  26.2 3.6 %collective-permute-done.3 = bf16[192,768]{1,0:T(8,128)(2,1)S(1)} collective-permute-done((bf16[192,768]{1,0:T(8,128)(2,1)S(1)}, bf16[192,768]{1,0:T(8,128)(2,1)S(1)}, u32[]{:S(2)}, u32[]{:S(2)}) %collective-permute-start.3) | collective-permute-done | bytes 294944 | tf_op jit(solution)/shard_map/ppermute | solution.py:386
  29.8 4.1 %collective-permute-start.11 = (bf16[48,3072]{1,0:T(8,128)(2,1)S(1)}, bf16[48,3072]{1,0:T(8,128)(2,1)S(1)}, u32[]{:S(2)}, u32[]{:S(2)}) collective-permute-start(bf16[48,3072]{1,0:T(8,128)(2,1)S(1)} %pad_maximum_fusion.6), channel_id=1, source_target_pairs={{0,24},{2,26},{4,28},{6,30},{8,0},{10,2},{12,4},{14,6},{16,8},{18,... | collective-permute-start | bytes 884744 | tf_op jit(solution)/shard_map/ppermute | solution.py:394
  40.3 1.8 collective-permute-done.11
  42.1 4.6 %collective-permute-done.9 = bf16[48,3072]{1,0:T(8,128)(2,1)S(1)} collective-permute-done((bf16[48,3072]{1,0:T(8,128)(2,1)S(1)}, bf16[48,3072]{1,0:T(8,128)(2,1)S(1)}, u32[]{:S(2)}, u32[]{:S(2)}) %collective-permute-start.9) | collective-permute-done | bytes 294944 | tf_op jit(solution)/shard_map/ppermute | solution.py:394
  46.7 2.5 %collective-permute-done.6.vo_other_ref = bf16[384,768]{1,0:T(8,128)(2,1)S(1)} collective-permute-done((bf16[384,768]{1,0:T(8,128)(2,1)S(1)}, bf16[384,768]{1,0:T(8,128)(2,1)S(1)}, u32[]{:S(2)}, u32[]{:S(2)}) %collective-permute-start.6) | collective-permute-done | bytes 589856 | tf_op jit(solution)/shard_map/ppermute | solution.py:386
  53.3 8.5 %shard_map.220 = (bf16[2,2,2,2,48,1024]{5,4,3,2,1,0:T(8,128)(2,1)}, bf16[2,2,2,2,48,1024]{5,4,3,2,1,0:T(8,128)(2,1)}, bf16[1024,384]{1,0:T(8,128)(2,1)}, bf16[10...) custom-call(s32[4]{0:T(128)} %pad_add_fusion.place_ref, ...), custom_call_target="tpu_custom_call" | custom-call | flops 8074500096 | tf_op jit(solution)/shard_map/pallas_call | solution.py:965
  66.8 17.7 %shard_map.221 = (bf16[6,1024,1024]{2,1,0:T(8,128)(2,1)}, f32[1024,384]{1,0:T(8,128)}, bf16[1024,384]{1,0:T(8,128)(2,1)}, f32[1024,384]{1,0:T(8,128)}, bf16[512,...) custom-call(bf16[1024,384]{1,0:T(8,128)(2,1)} %get-tuple-element.110.q_ref, bf16[1024,384]{1,0:T(8,128)(2,1)} %get-tuple-element.111.k_ref, ...), custom_call_target="tpu_custom_call" | custom-call | flops 23069999104 | tf_op jit(solution)/shard_map/pallas_call | solution.py:990
  90.6 28.3 %shard_map.222 = (bf16[1024,768]{1,0:T(8,128)(2,1)}, f32[1024,128]{1,0:T(8,128)}, bf16[1024,768]{1,0:T(8,128)(2,1)}, bf16[512,768]{1,0:T(8,128)(2,1)}, f32[512,7...) custom-call(s32[4]{0:T(128)} %pad_add_fusion.place_ref, ...), custom_call_target="tpu_custom_call" | custom-call | flops 32298000384 | tf_op jit(solution)/shard_map/pallas_call | solution.py:1044
  122.6 7.6 %shard_map.223 = (f32[512,768]{1,0:T(8,128)}, bf16[2,2,2,2,48,1024]{5,4,3,2,1,0:T(8,128)(2,1)}, bf16[1024,384]{1,0:T(8,128)(2,1)}, f32[1,768]{1,0:T(1,128)}) custom-call(s32[4]{0:T(128)} %pad_add_fusion.place_ref, bf16[1024,768]{1,0:T(8,128)(2,1)} %get-tuple-element.128.unit_ref, f32[1024,128]{1,0:T(8,128)} %get-tuple-element.129.scale_ref, ...), custom_call_target="tpu_custom_call" | custom-call | flops 4614000128 | tf_op jit(solution)/shard_map/pallas_call | solution.py:1072
  130.2 16.7 %shard_map.224 = (bf16[1024,384]{1,0:T(8,128)(2,1)}, bf16[1024,384]{1,0:T(8,128)(2,1)}, bf16[1024,384]{1,0:T(8,128)(2,1)}, f32[3,2,2048]{2,1,0:T(2,128)}) custom-call(bf16[1024,384]{1,0:T(8,128)(2,1)} %get-tuple-element.110.q_ref, bf16[1024,384]{1,0:T(8,128)(2,1)} %get-tuple-element.111.k_ref, bf16[1024,384]{1,0:T(8,128)(2,1)} %get-tuple-element.112.v_ref, ...), custom_call_target="tpu_custom_call" | custom-call | flops 4614000128 | tf_op jit(solution)/shard_map/pallas_call | solution.py:1090
  151.4 5.3 %shard_map.225 = (bf16[384,768]{1,0:T(8,128)(2,1)}, bf16[384,768]{1,0:T(8,128)(2,1)}) custom-call(bf16[768,1024]{1,0:T(8,128)(2,1)} %bitcast.50, bf16[768,1024]{1,0:T(8,128)(2,1)} %bitcast.51, bf16[1024,384]{1,0:T(8,128)(2,1)} %get-tuple-element.159.right0_ref.dq_ref, bf16[1024,384]{1,0:T(8,128)(2,1)} %get-tuple-element.141.right1_ref.dk_ref), custom_call_target="tpu_custom_call" | custom-call | flops 5767499776 | tf_op jit(solution)/shard_map/pallas_call | solution.py:868
  157.8 5.2 %shard_map.226 = (bf16[384,768]{1,0:T(8,128)(2,1)}, bf16[384,768]{1,0:T(8,128)(2,1)}) custom-call(bf16[768,1024]{1,0:T(8,128)(2,1)} %bitcast.49, bf16[768,1024]{1,0:T(8,128)(2,1)} %bitcast.52, bf16[1024,384]{1,0:T(8,128)(2,1)} %get-tuple-element.152.right0_ref.dv_ref, bf16[1024,384]{1,0:T(8,128)(2,1)} %get-tuple-element.153.right1_ref), custom_call_target="tpu_custom_call" | custom-call | flops 5767499776 | tf_op jit(solution)/shard_map/pallas_call | solution.py:868
  164.9 1.7 collective-permute-start.27
  169.8 7.8 %shard_map.227 = (bf16[512,768]{1,0:T(8,128)(2,1)}, f32[512,768]{1,0:T(8,128)}, f32[1,768]{1,0:T(1,128)}) custom-call(s32[4]{0:T(128)} %pad_add_fusion.place_ref, bf16[1024,768]{1,0:T(8,128)(2,1)} %pad_maximum_fusion.x_ref, bf16[1024,384]{1,0:T(8,128)(2,1)} %get-tuple-element.159.right0_ref.dq_ref, bf16[1024,384]{1,0:T(8,128)(2,1)} %get-tuple-element.141.right1_ref.dk_ref, ...), custom_call_target="tpu_custom_call" | custom-call | flops 2307000064 | tf_op jit(solution)/shard_map/pallas_call | solution.py:1140
  177.6 2.0 collective-permute-done.27
  183.7 1.9 collective-permute-start.30
  193.8 3.9 %collective-permute-done.29 = bf16[192,768]{1,0:T(8,128)(2,1)S(1)} collective-permute-done((bf16[192,768]{1,0:T(8,128)(2,1)S(1)}, bf16[192,768]{1,0:T(8,128)(2,1)S(1)}, u32[]{:S(2)}, u32[]{:S(2)}) %collective-permute-start.29) | collective-permute-done | bytes 294944 | tf_op jit(solution)/shard_map/ppermute | solution.py:382
  200.4 1.7 collective-permute-start.37
  202.1 2.0 collective-permute-start.38
  206.4 3.5 %shard_map.228 = bf16[512,768]{1,0:T(8,128)(2,1)} custom-call(bf16[512,768]{1,0:T(8,128)(2,1)} %x_ref.1, f32[512,768]{1,0:T(8,128)} %get-tuple-element.175.own_ref, bf16[512,768]{1,0:T(8,128)(2,1)} %copy-done.27, f32[512,768]{1,0:T(8,128)} %get-tuple-element.177.datt_ref, f32[1,768]{1,0:T(1,128)} %reshape.91.gain_ref), custom_call_target="tpu_custom_call" | custom-call | flops 4037250048 | tf_op jit(solution)/shard_map/pallas_call | solution.py:1178
  209.8 3.9 %collective-permute-done.37 = bf16[56,1536]{1,0:T(8,128)(2,1)S(1)} collective-permute-done((bf16[56,1536]{1,0:T(8,128)(2,1)S(1)}, bf16[56,1536]{1,0:T(8,128)(2,1)S(1)}, u32[]{:S(2)}, u32[]{:S(2)}) %collective-permute-start.37) | collective-permute-done | bytes 172064 | tf_op jit(solution)/shard_map/ppermute | solution.py:394
  (200 shorter events, 65.7 us)
Async XLA Ops:
  4.7 17.2 %collective-permute-start.1 = (bf16[48,1536]{1,0:T(8,128)(2,1)S(1)}, bf16[48,1536]{1,0:T(8,128)(2,1)S(1)}, u32[]{:S(2)}, u32[]{:S(2)}) collective-permute-start(bf16[48,1536]{1,0:T(8,128)(2,1)S(1)} %pad_maximum_fusion.11), channel_id=1, source_target_pairs={{0,16},{2,18},{4,20},{6,22},{8,24},{10,26},{12,28},{14,30},{16,0},... | collective-permute-start | bytes 442376 | tf_op jit(solution)/shard_map/ppermute | solution.py:394
  7.3 14.6 %collective-permute-start.2 = (bf16[48,1536]{1,0:T(8,128)(2,1)S(1)}, bf16[48,1536]{1,0:T(8,128)(2,1)}, u32[]{:S(2)}, u32[]{:S(2)}) collective-permute-start(bf16[48,1536]{1,0:T(8,128)(2,1)S(1)} %pad_maximum_fusion.11), channel_id=1, source_target_pairs={{0,24},{2,26},{4,28},{6,30},{8,0},{10,2},{12,4},{14,6},{16,8},{18,... | collective-permute-start | bytes 442376 | tf_op jit(solution)/shard_map/ppermute | solution.py:394
  8.7 26.8 %collective-permute-start.7 = (bf16[512,768]{1,0:T(8,128)(2,1)}, bf16[512,768]{1,0:T(8,128)(2,1)S(1)}, u32[]{:S(2)}, u32[]{:S(2)}) collective-permute-start(bf16[512,768]{1,0:T(8,128)(2,1)} %x_ref.1), channel_id=1, source_target_pairs={{0,1},{1,0},{2,3},{3,2},{4,5},{5,4},{6,7},{7,6},{8,9},{9,8},{10,11... | collective-permute-start | bytes 2359304 | tf_op jit(solution)/shard_map/ppermute | solution.py:916
  8.7 27.3 %collective-permute-start.8 = (bf16[512,768]{1,0:T(8,128)(2,1)}, bf16[512,768]{1,0:T(8,128)(2,1)S(1)}, u32[]{:S(2)}, u32[]{:S(2)}) collective-permute-start(bf16[512,768]{1,0:T(8,128)(2,1)} %param.14), channel_id=1, source_target_pairs={{0,1},{1,0},{2,3},{3,2},{4,5},{5,4},{6,7},{7,6},{8,9},{9,8},{10,11... | collective-permute-start | bytes 2359304 | tf_op jit(solution)/shard_map/ppermute | solution.py:916
  13.0 27.3 %collective-permute-start.10 = (bf16[48,3072]{1,0:T(8,128)(2,1)S(1)}, bf16[48,3072]{1,0:T(8,128)(2,1)S(1)}, u32[]{:S(2)}, u32[]{:S(2)}) collective-permute-start(bf16[48,3072]{1,0:T(8,128)(2,1)S(1)} %pad_maximum_fusion.6), channel_id=1, source_target_pairs={{0,16},{2,18},{4,20},{6,22},{8,24},{10,26},{12,28},{14,30},{16,0},... | collective-permute-start | bytes 884744 | tf_op jit(solution)/shard_map/ppermute | solution.py:394
  29.8 12.3 %collective-permute-start.11 = (bf16[48,3072]{1,0:T(8,128)(2,1)S(1)}, bf16[48,3072]{1,0:T(8,128)(2,1)S(1)}, u32[]{:S(2)}, u32[]{:S(2)}) collective-permute-start(bf16[48,3072]{1,0:T(8,128)(2,1)S(1)} %pad_maximum_fusion.6), channel_id=1, source_target_pairs={{0,24},{2,26},{4,28},{6,30},{8,0},{10,2},{12,4},{14,6},{16,8},{18,... | collective-permute-start | bytes 884744 | tf_op jit(solution)/shard_map/ppermute | solution.py:394
  33.9 12.8 %collective-permute-start.9 = (bf16[48,3072]{1,0:T(8,128)(2,1)S(1)}, bf16[48,3072]{1,0:T(8,128)(2,1)S(1)}, u32[]{:S(2)}, u32[]{:S(2)}) collective-permute-start(bf16[48,3072]{1,0:T(8,128)(2,1)S(1)} %pad_maximum_fusion.6), channel_id=1, source_target_pairs={{0,8},{2,10},{4,12},{6,14},{8,16},{10,18},{12,20},{14,22},{16,24},... | collective-permute-start | bytes 884744 | tf_op jit(solution)/shard_map/ppermute | solution.py:394
  35.4 13.8 %collective-permute-start.6 = (bf16[384,768]{1,0:T(8,128)(2,1)S(1)}, bf16[384,768]{1,0:T(8,128)(2,1)S(1)}, u32[]{:S(2)}, u32[]{:S(2)}) collective-permute-start(bf16[384,768]{1,0:T(8,128)(2,1)S(1)} %pad_maximum_fusion.5.vo_own_ref), channel_id=1, source_target_pairs={{0,4},{2,6},{4,0},{6,2},{8,12},{10,14},{12,8},{14,10},{16,20},{18,... | collective-permute-start | bytes 1769480 | tf_op jit(solution)/shard_map/ppermute | solution.py:386
  36.0 13.5 %collective-permute-start.5 = (bf16[384,768]{1,0:T(8,128)(2,1)S(1)}, bf16[384,768]{1,0:T(8,128)(2,1)S(1)}, u32[]{:S(2)}, u32[]{:S(2)}) collective-permute-start(bf16[384,768]{1,0:T(8,128)(2,1)S(1)} %pad_maximum_fusion.4.qk_own_ref), channel_id=1, source_target_pairs={{0,2},{2,0},{4,6},{6,4},{8,10},{10,8},{12,14},{14,12},{16,18},{18,... | collective-permute-start | bytes 1769480 | tf_op jit(solution)/shard_map/ppermute | solution.py:382
  50.4 12.7 %collective-permute-start.12 = (bf16[192,1536]{1,0:T(8,128)(2,1)S(1)}, bf16[192,1536]{1,0:T(8,128)(2,1)S(1)}, u32[]{:S(2)}, u32[]{:S(2)}) collective-permute-start(bf16[192,1536]{1,0:T(8,128)(2,1)S(1)} %get-tuple-element.219), channel_id=1, source_target_pairs={{0,4},{2,6},{4,0},{6,2},{8,12},{10,14},{12,8},{14,10},{16,20},{18,... | collective-permute-start | bytes 1769480 | tf_op jit(solution)/shard_map/ppermute | solution.py:386
  51.8 12.2 %collective-permute-start.13 = (bf16[192,1536]{1,0:T(8,128)(2,1)S(1)}, bf16[192,1536]{1,0:T(8,128)(2,1)S(1)}, u32[]{:S(2)}, u32[]{:S(2)}) collective-permute-start(bf16[192,1536]{1,0:T(8,128)(2,1)S(1)} %get-tuple-element.218), channel_id=1, source_target_pairs={{0,2},{2,0},{4,6},{6,4},{8,10},{10,8},{12,14},{14,12},{16,18},{18,... | collective-permute-start | bytes 1769480 | tf_op jit(solution)/shard_map/ppermute | solution.py:382
  64.3 24.0 %collective-permute-start.15 = (bf16[384,1536]{1,0:T(8,128)(2,1)S(1)}, bf16[384,1536]{1,0:T(8,128)(2,1)S(1)}, u32[]{:S(2)}, u32[]{:S(2)}) collective-permute-start(bf16[384,1536]{1,0:T(8,128)(2,1)S(1)} %pad_maximum_fusion.3.ud_own_ref), channel_id=1, source_target_pairs={{0,4},{2,6},{4,0},{6,2},{8,12},{10,14},{12,8},{14,10},{16,20},{18,... | collective-permute-start | bytes 3538952 | tf_op jit(solution)/shard_map/ppermute | solution.py:386
  65.3 24.0 %collective-permute-start.14 = (bf16[384,1536]{1,0:T(8,128)(2,1)S(1)}, bf16[384,1536]{1,0:T(8,128)(2,1)S(1)}, u32[]{:S(2)}, u32[]{:S(2)}) collective-permute-start(bf16[384,1536]{1,0:T(8,128)(2,1)S(1)} %pad_maximum_fusion.2.gu_own_ref), channel_id=1, source_target_pairs={{0,2},{2,0},{4,6},{6,4},{8,10},{10,8},{12,14},{14,12},{16,18},{18,... | collective-permute-start | bytes 3538952 | tf_op jit(solution)/shard_map/ppermute | solution.py:382
  119.0 28.5 %collective-permute-start.18 = (bf16[384,1536]{1,0:T(8,128)(2,1)}, bf16[384,1536]{1,0:T(8,128)(2,1)S(1)}, u32[]{:S(2)}, u32[]{:S(2)}) collective-permute-start(bf16[384,1536]{1,0:T(8,128)(2,1)} %get-tuple-element.124), channel_id=1, source_target_pairs={{0,2},{2,0},{4,6},{6,4},{8,10},{10,8},{12,14},{14,12},{16,18},{18,... | collective-permute-start | bytes 3538952 | tf_op jit(solution)/shard_map/ppermute | solution.py:382
  120.3 28.2 %collective-permute-start.19 = (bf16[384,1536]{1,0:T(8,128)(2,1)}, bf16[384,1536]{1,0:T(8,128)(2,1)S(1)}, u32[]{:S(2)}, u32[]{:S(2)}) collective-permute-start(bf16[384,1536]{1,0:T(8,128)(2,1)} %get-tuple-element.125), channel_id=1, source_target_pairs={{0,4},{2,6},{4,0},{6,2},{8,12},{10,14},{12,8},{14,10},{16,20},{18,... | collective-permute-start | bytes 3538952 | tf_op jit(solution)/shard_map/ppermute | solution.py:386
  121.5 25.4 %collective-permute-start.20 = (bf16[512,768]{1,0:T(8,128)(2,1)}, bf16[512,768]{1,0:T(8,128)(2,1)S(1)}, u32[]{:S(2)}, u32[]{:S(2)}) collective-permute-start(bf16[512,768]{1,0:T(8,128)(2,1)} %get-tuple-element.126), channel_id=1, source_target_pairs={{0,1},{1,0},{2,3},{3,2},{4,5},{5,4},{6,7},{7,6},{8,9},{9,8},{10,11... | collective-permute-start | bytes 2359304 | tf_op jit(solution)/shard_map/ppermute | solution.py:916
  148.9 14.6 %collective-permute-start.23 = (bf16[192,1536]{1,0:T(8,128)(2,1)S(1)}, bf16[192,1536]{1,0:T(8,128)(2,1)S(1)}, u32[]{:S(2)}, u32[]{:S(2)}) collective-permute-start(bf16[192,1536]{1,0:T(8,128)(2,1)S(1)} %get-tuple-element.197), channel_id=1, source_target_pairs={{0,2},{2,0},{4,6},{6,4},{8,10},{10,8},{12,14},{14,12},{16,18},{18,... | collective-permute-start | bytes 1769480 | tf_op jit(solution)/shard_map/ppermute | solution.py:382
  150.1 14.6 %collective-permute-start.22 = (bf16[192,1536]{1,0:T(8,128)(2,1)S(1)}, bf16[192,1536]{1,0:T(8,128)(2,1)S(1)}, u32[]{:S(2)}, u32[]{:S(2)}) collective-permute-start(bf16[192,1536]{1,0:T(8,128)(2,1)S(1)} %get-tuple-element.199), channel_id=1, source_target_pairs={{0,4},{2,6},{4,0},{6,2},{8,12},{10,14},{12,8},{14,10},{16,20},{18,... | collective-permute-start | bytes 1769480 | tf_op jit(solution)/shard_map/ppermute | solution.py:386
  164.9 14.7 %collective-permute-start.27 = (bf16[96,1536]{1,0:T(8,128)(2,1)S(1)}, bf16[96,1536]{1,0:T(8,128)(2,1)S(1)}, u32[]{:S(2)}, u32[]{:S(2)}) collective-permute-start(bf16[96,1536]{1,0:T(8,128)(2,1)S(1)} %bitcast.46), channel_id=1, source_target_pairs={{0,16},{2,18},{4,20},{6,22},{8,24},{10,26},{12,28},{14,30},{16,0},... | collective-permute-start | bytes 884744 | tf_op jit(solution)/shard_map/ppermute | solution.py:422
  166.7 13.7 %collective-permute-start.24 = (bf16[384,768]{1,0:T(8,128)(2,1)}, bf16[384,768]{1,0:T(8,128)(2,1)S(1)}, u32[]{:S(2)}, u32[]{:S(2)}) collective-permute-start(bf16[384,768]{1,0:T(8,128)(2,1)} %get-tuple-element.155), channel_id=1, source_target_pairs={{0,2},{2,0},{4,6},{6,4},{8,10},{10,8},{12,14},{14,12},{16,18},{18,... | collective-permute-start | bytes 1769480 | tf_op jit(solution)/shard_map/ppermute | solution.py:382
  167.5 13.0 %collective-permute-start.25 = (bf16[384,768]{1,0:T(8,128)(2,1)}, bf16[384,768]{1,0:T(8,128)(2,1)S(1)}, u32[]{:S(2)}, u32[]{:S(2)}) collective-permute-start(bf16[384,768]{1,0:T(8,128)(2,1)} %get-tuple-element.156), channel_id=1, source_target_pairs={{0,4},{2,6},{4,0},{6,2},{8,12},{10,14},{12,8},{14,10},{16,20},{18,... | collective-permute-start | bytes 1769480 | tf_op jit(solution)/shard_map/ppermute | solution.py:386
  168.6 11.8 %collective-permute-start.26 = (bf16[96,1536]{1,0:T(8,128)(2,1)S(1)}, bf16[96,1536]{1,0:T(8,128)(2,1)S(1)}, u32[]{:S(2)}, u32[]{:S(2)}) collective-permute-start(bf16[96,1536]{1,0:T(8,128)(2,1)S(1)} %get-tuple-element.215), channel_id=1, source_target_pairs={{0,8},{2,10},{4,12},{6,14},{8,0},{10,2},{12,4},{14,6},{16,24},{18,... | collective-permute-start | bytes 884744 | tf_op jit(solution)/shard_map/ppermute | solution.py:422
  193.2 12.3 %collective-permute-start.39 = (bf16[512,768]{1,0:T(8,128)(2,1)S(1)}, bf16[512,768]{1,0:T(8,128)(2,1)S(1)}, u32[]{:S(2)}, u32[]{:S(2)}) collective-permute-start(bf16[512,768]{1,0:T(8,128)(2,1)S(1)} %copy-done.26), channel_id=1, source_target_pairs={{0,1},{1,0},{2,3},{3,2},{4,5},{5,4},{6,7},{7,6},{8,9},{9,8},{10,11... | collective-permute-start | bytes 2359304 | tf_op jit(solution)/shard_map/ppermute | solution.py:916
  200.4 13.3 %collective-permute-start.37 = (bf16[56,1536]{1,0:T(8,128)(2,1)S(1)}, bf16[56,1536]{1,0:T(8,128)(2,1)S(1)}, u32[]{:S(2)}, u32[]{:S(2)}) collective-permute-start(bf16[56,1536]{1,0:T(8,128)(2,1)S(1)} %get-tuple-element.236), channel_id=1, source_target_pairs={{0,16},{2,18},{4,20},{6,22},{8,24},{10,26},{12,28},{14,30},{16,0},... | collective-permute-start | bytes 516104 | tf_op jit(solution)/shard_map/ppermute | solution.py:394
  (48 other events, 326.5 us)

commit v7 on v6

--- a/solution.py
+++ b/solution.py
@@ -1181,7 +1181,7 @@
         [row_block(features)] * 4 + [whole((1, features))],
         row_block(features),
         shaped((own_rows, features), LOW),
-        micros=3.5,
+        micros=0.5,
     )(tokens, dna_own, dna_other, d_attended, gain_a)
 
     qk_came, vo_came, gu_came, ud_came, small = together(

time: 217 us -> 216 us (level)
  transfers between devices with their start and end apart: 40 -> 40, of which waited for: 25 -> 23; matrix products, arithmetic and copies ran while one was open for 6% -> 6% of each run, Pallas kernels for 33% -> 34%
where the time goes in v7:
time: 216 us; the launch traced here: 215 us
  Pallas kernels  101 us (47%)
  starting transfers between devices  55.8 us (26%)
  waiting for transfers between devices  35.9 us (17%)
  local copies, waits for them, and re-layouts  10.3 us (5%)
  other arithmetic  10.1 us (5%)
    pallas_call x1, Pallas kernels, on_core_pair(): call(functools.partial(feed_body, steps), (steps + 6,), [turned_row(featu...  28.3 us
    ppermute x9, starting transfers between devices, over_far(): return lax.ppermute(array, 'dp', ring_shift(4 * steps, lax.axis_size('dp')))  25.3 us
    pallas_call x1, Pallas kernels, on_core_pair(): call(attend_body, (pairs,), [pair_block, pair_block, pair_block, strip_bl...  17.6 us
    pallas_call x1, Pallas kernels, on_core_pair(): call(backward_body, (pairs,), [pair_block, pair_block, pair_block, e_bloc...  16.7 us
    ppermute x9, starting transfers between devices, over_x(): return lax.ppermute(array, 'dp', flip(1, lax.axis_size('dp')))  11.8 us
    ppermute x9, waiting for transfers between devices, over_y(): return lax.ppermute(array, 'dp', flip(2, lax.axis_size('dp')))  11.2 us
    pallas_call x2, Pallas kernels, weight_grads(): call(functools.partial(grads_body, count0), (steps,), [whole((height, dep...  10.6 us
    ppermute x9, starting transfers between devices, over_y(): return lax.ppermute(array, 'dp', flip(2, lax.axis_size('dp')))  10.3 us
  transfers between devices with their start and end apart: 40, of which 23 were waited for; matrix products, arithmetic and copies ran while one was open for 6% of the time, Pallas kernels for 34%

profile of v7, /device:TPU:0, one launch (start us, length us, event | category | flops | bytes accessed | tf_op | source)
XLA Modules:
  0.0 215.3 jit_solution(11882406182154551397)
XLA Ops:
  1.7 3.1 %collective-permute-start = (bf16[48,1536]{1,0:T(8,128)(2,1)S(1)}, bf16[48,1536]{1,0:T(8,128)(2,1)S(1)}, u32[]{:S(2)}, u32[]{:S(2)}) collective-permute-start(bf16[48,1536]{1,0:T(8,128)(2,1)S(1)} %pad_maximum_fusion.11), channel_id=1, source_target_pairs={{0,8},{2,10},{4,12},{6,14},{8,16},{10,18},{12,20},{14,22},{16,24},... | collective-permute-start | bytes 442376 | tf_op jit(solution)/shard_map/ppermute | solution.py:394
  4.7 2.6 %collective-permute-start.1 = (bf16[48,1536]{1,0:T(8,128)(2,1)S(1)}, bf16[48,1536]{1,0:T(8,128)(2,1)S(1)}, u32[]{:S(2)}, u32[]{:S(2)}) collective-permute-start(bf16[48,1536]{1,0:T(8,128)(2,1)S(1)} %pad_maximum_fusion.11), channel_id=1, source_target_pairs={{0,16},{2,18},{4,20},{6,22},{8,24},{10,26},{12,28},{14,30},{16,0},... | collective-permute-start | bytes 442376 | tf_op jit(solution)/shard_map/ppermute | solution.py:394
  13.0 9.0 %collective-permute-start.10 = (bf16[48,3072]{1,0:T(8,128)(2,1)S(1)}, bf16[48,3072]{1,0:T(8,128)(2,1)S(1)}, u32[]{:S(2)}, u32[]{:S(2)}) collective-permute-start(bf16[48,3072]{1,0:T(8,128)(2,1)S(1)} %pad_maximum_fusion.6), channel_id=1, source_target_pairs={{0,16},{2,18},{4,20},{6,22},{8,24},{10,26},{12,28},{14,30},{16,0},... | collective-permute-start | bytes 884744 | tf_op jit(solution)/shard_map/ppermute | solution.py:394
  23.0 1.6 collective-permute-start.3
  26.2 3.6 %collective-permute-done.3 = bf16[192,768]{1,0:T(8,128)(2,1)S(1)} collective-permute-done((bf16[192,768]{1,0:T(8,128)(2,1)S(1)}, bf16[192,768]{1,0:T(8,128)(2,1)S(1)}, u32[]{:S(2)}, u32[]{:S(2)}) %collective-permute-start.3) | collective-permute-done | bytes 294944 | tf_op jit(solution)/shard_map/ppermute | solution.py:386
  29.8 4.1 %collective-permute-start.11 = (bf16[48,3072]{1,0:T(8,128)(2,1)S(1)}, bf16[48,3072]{1,0:T(8,128)(2,1)S(1)}, u32[]{:S(2)}, u32[]{:S(2)}) collective-permute-start(bf16[48,3072]{1,0:T(8,128)(2,1)S(1)} %pad_maximum_fusion.6), channel_id=1, source_target_pairs={{0,24},{2,26},{4,28},{6,30},{8,0},{10,2},{12,4},{14,6},{16,8},{18,... | collective-permute-start | bytes 884744 | tf_op jit(solution)/shard_map/ppermute | solution.py:394
  40.3 1.8 collective-permute-done.11
  42.1 4.6 %collective-permute-done.9 = bf16[48,3072]{1,0:T(8,128)(2,1)S(1)} collective-permute-done((bf16[48,3072]{1,0:T(8,128)(2,1)S(1)}, bf16[48,3072]{1,0:T(8,128)(2,1)S(1)}, u32[]{:S(2)}, u32[]{:S(2)}) %collective-permute-start.9) | collective-permute-done | bytes 294944 | tf_op jit(solution)/shard_map/ppermute | solution.py:394
  46.7 2.5 %collective-permute-done.6.vo_other_ref = bf16[384,768]{1,0:T(8,128)(2,1)S(1)} collective-permute-done((bf16[384,768]{1,0:T(8,128)(2,1)S(1)}, bf16[384,768]{1,0:T(8,128)(2,1)S(1)}, u32[]{:S(2)}, u32[]{:S(2)}) %collective-permute-start.6) | collective-permute-done | bytes 589856 | tf_op jit(solution)/shard_map/ppermute | solution.py:386
  53.3 8.5 %shard_map.220 = (bf16[2,2,2,2,48,1024]{5,4,3,2,1,0:T(8,128)(2,1)}, bf16[2,2,2,2,48,1024]{5,4,3,2,1,0:T(8,128)(2,1)}, bf16[1024,384]{1,0:T(8,128)(2,1)}, bf16[10...) custom-call(s32[4]{0:T(128)} %pad_add_fusion.place_ref, ...), custom_call_target="tpu_custom_call" | custom-call | flops 8074500096 | tf_op jit(solution)/shard_map/pallas_call | solution.py:965
  66.8 17.6 %shard_map.221 = (bf16[6,1024,1024]{2,1,0:T(8,128)(2,1)}, f32[1024,384]{1,0:T(8,128)}, bf16[1024,384]{1,0:T(8,128)(2,1)}, f32[1024,384]{1,0:T(8,128)}, bf16[512,...) custom-call(bf16[1024,384]{1,0:T(8,128)(2,1)} %get-tuple-element.110.q_ref, bf16[1024,384]{1,0:T(8,128)(2,1)} %get-tuple-element.111.k_ref, ...), custom_call_target="tpu_custom_call" | custom-call | flops 23069999104 | tf_op jit(solution)/shard_map/pallas_call | solution.py:990
  90.4 28.3 %shard_map.222 = (bf16[1024,768]{1,0:T(8,128)(2,1)}, f32[1024,128]{1,0:T(8,128)}, bf16[1024,768]{1,0:T(8,128)(2,1)}, bf16[512,768]{1,0:T(8,128)(2,1)}, f32[512,7...) custom-call(s32[4]{0:T(128)} %pad_add_fusion.place_ref, ...), custom_call_target="tpu_custom_call" | custom-call | flops 32298000384 | tf_op jit(solution)/shard_map/pallas_call | solution.py:1044
  122.5 7.6 %shard_map.223 = (f32[512,768]{1,0:T(8,128)}, bf16[2,2,2,2,48,1024]{5,4,3,2,1,0:T(8,128)(2,1)}, bf16[1024,384]{1,0:T(8,128)(2,1)}, f32[1,768]{1,0:T(1,128)}) custom-call(s32[4]{0:T(128)} %pad_add_fusion.place_ref, bf16[1024,768]{1,0:T(8,128)(2,1)} %get-tuple-element.128.unit_ref, f32[1024,128]{1,0:T(8,128)} %get-tuple-element.129.scale_ref, ...), custom_call_target="tpu_custom_call" | custom-call | flops 4614000128 | tf_op jit(solution)/shard_map/pallas_call | solution.py:1072
  130.1 16.7 %shard_map.224 = (bf16[1024,384]{1,0:T(8,128)(2,1)}, bf16[1024,384]{1,0:T(8,128)(2,1)}, bf16[1024,384]{1,0:T(8,128)(2,1)}, f32[3,2,2048]{2,1,0:T(2,128)}) custom-call(bf16[1024,384]{1,0:T(8,128)(2,1)} %get-tuple-element.110.q_ref, bf16[1024,384]{1,0:T(8,128)(2,1)} %get-tuple-element.111.k_ref, bf16[1024,384]{1,0:T(8,128)(2,1)} %get-tuple-element.112.v_ref, ...), custom_call_target="tpu_custom_call" | custom-call | flops 4614000128 | tf_op jit(solution)/shard_map/pallas_call | solution.py:1090
  151.5 5.4 %shard_map.225 = (bf16[384,768]{1,0:T(8,128)(2,1)}, bf16[384,768]{1,0:T(8,128)(2,1)}) custom-call(bf16[768,1024]{1,0:T(8,128)(2,1)} %bitcast.50, bf16[768,1024]{1,0:T(8,128)(2,1)} %bitcast.51, bf16[1024,384]{1,0:T(8,128)(2,1)} %get-tuple-element.159.right0_ref.dq_ref, bf16[1024,384]{1,0:T(8,128)(2,1)} %get-tuple-element.141.right1_ref.dk_ref), custom_call_target="tpu_custom_call" | custom-call | flops 5767499776 | tf_op jit(solution)/shard_map/pallas_call | solution.py:868
  157.9 5.2 %shard_map.226 = (bf16[384,768]{1,0:T(8,128)(2,1)}, bf16[384,768]{1,0:T(8,128)(2,1)}) custom-call(bf16[768,1024]{1,0:T(8,128)(2,1)} %bitcast.49, bf16[768,1024]{1,0:T(8,128)(2,1)} %bitcast.52, bf16[1024,384]{1,0:T(8,128)(2,1)} %get-tuple-element.152.right0_ref.dv_ref, bf16[1024,384]{1,0:T(8,128)(2,1)} %get-tuple-element.153.right1_ref), custom_call_target="tpu_custom_call" | custom-call | flops 5767499776 | tf_op jit(solution)/shard_map/pallas_call | solution.py:868
  165.0 1.7 collective-permute-start.27
  169.8 7.8 %shard_map.227 = (bf16[512,768]{1,0:T(8,128)(2,1)}, f32[512,768]{1,0:T(8,128)}, f32[1,768]{1,0:T(1,128)}) custom-call(s32[4]{0:T(128)} %pad_add_fusion.place_ref, bf16[1024,768]{1,0:T(8,128)(2,1)} %pad_maximum_fusion.x_ref, bf16[1024,384]{1,0:T(8,128)(2,1)} %get-tuple-element.159.right0_ref.dq_ref, bf16[1024,384]{1,0:T(8,128)(2,1)} %get-tuple-element.141.right1_ref.dk_ref, ...), custom_call_target="tpu_custom_call" | custom-call | flops 2307000064 | tf_op jit(solution)/shard_map/pallas_call | solution.py:1140
  177.7 2.0 collective-permute-done.27
  183.5 2.1 collective-permute-start.30
  193.6 4.1 %collective-permute-done.29 = bf16[192,768]{1,0:T(8,128)(2,1)S(1)} collective-permute-done((bf16[192,768]{1,0:T(8,128)(2,1)S(1)}, bf16[192,768]{1,0:T(8,128)(2,1)S(1)}, u32[]{:S(2)}, u32[]{:S(2)}) %collective-permute-start.29) | collective-permute-done | bytes 294944 | tf_op jit(solution)/shard_map/ppermute | solution.py:382
  201.1 2.0 collective-permute-start.38
  206.2 3.5 %shard_map.228 = bf16[512,768]{1,0:T(8,128)(2,1)} custom-call(bf16[512,768]{1,0:T(8,128)(2,1)} %x_ref.1, f32[512,768]{1,0:T(8,128)} %get-tuple-element.175.own_ref, bf16[512,768]{1,0:T(8,128)(2,1)} %copy-done.9, f32[512,768]{1,0:T(8,128)} %get-tuple-element.177.datt_ref, f32[1,768]{1,0:T(1,128)} %reshape.91.gain_ref), custom_call_target="tpu_custom_call" | custom-call | flops 576750016 | tf_op jit(solution)/shard_map/pallas_call | solution.py:1178
  209.7 3.3 %collective-permute-done.37 = bf16[56,1536]{1,0:T(8,128)(2,1)S(1)} collective-permute-done((bf16[56,1536]{1,0:T(8,128)(2,1)S(1)}, bf16[56,1536]{1,0:T(8,128)(2,1)S(1)}, u32[]{:S(2)}, u32[]{:S(2)}) %collective-permute-start.37) | collective-permute-done | bytes 172064 | tf_op jit(solution)/shard_map/ppermute | solution.py:394
  (204 shorter events, 65.3 us)
Async XLA Ops:
  4.7 17.2 %collective-permute-start.1 = (bf16[48,1536]{1,0:T(8,128)(2,1)S(1)}, bf16[48,1536]{1,0:T(8,128)(2,1)S(1)}, u32[]{:S(2)}, u32[]{:S(2)}) collective-permute-start(bf16[48,1536]{1,0:T(8,128)(2,1)S(1)} %pad_maximum_fusion.11), channel_id=1, source_target_pairs={{0,16},{2,18},{4,20},{6,22},{8,24},{10,26},{12,28},{14,30},{16,0},... | collective-permute-start | bytes 442376 | tf_op jit(solution)/shard_map/ppermute | solution.py:394
  7.3 14.6 %collective-permute-start.2 = (bf16[48,1536]{1,0:T(8,128)(2,1)S(1)}, bf16[48,1536]{1,0:T(8,128)(2,1)}, u32[]{:S(2)}, u32[]{:S(2)}) collective-permute-start(bf16[48,1536]{1,0:T(8,128)(2,1)S(1)} %pad_maximum_fusion.11), channel_id=1, source_target_pairs={{0,24},{2,26},{4,28},{6,30},{8,0},{10,2},{12,4},{14,6},{16,8},{18,... | collective-permute-start | bytes 442376 | tf_op jit(solution)/shard_map/ppermute | solution.py:394
  8.7 26.8 %collective-permute-start.7 = (bf16[512,768]{1,0:T(8,128)(2,1)}, bf16[512,768]{1,0:T(8,128)(2,1)S(1)}, u32[]{:S(2)}, u32[]{:S(2)}) collective-permute-start(bf16[512,768]{1,0:T(8,128)(2,1)} %x_ref.1), channel_id=1, source_target_pairs={{0,1},{1,0},{2,3},{3,2},{4,5},{5,4},{6,7},{7,6},{8,9},{9,8},{10,11... | collective-permute-start | bytes 2359304 | tf_op jit(solution)/shard_map/ppermute | solution.py:916
  8.7 27.3 %collective-permute-start.8 = (bf16[512,768]{1,0:T(8,128)(2,1)}, bf16[512,768]{1,0:T(8,128)(2,1)S(1)}, u32[]{:S(2)}, u32[]{:S(2)}) collective-permute-start(bf16[512,768]{1,0:T(8,128)(2,1)} %param.14), channel_id=1, source_target_pairs={{0,1},{1,0},{2,3},{3,2},{4,5},{5,4},{6,7},{7,6},{8,9},{9,8},{10,11... | collective-permute-start | bytes 2359304 | tf_op jit(solution)/shard_map/ppermute | solution.py:916
  13.0 27.3 %collective-permute-start.10 = (bf16[48,3072]{1,0:T(8,128)(2,1)S(1)}, bf16[48,3072]{1,0:T(8,128)(2,1)S(1)}, u32[]{:S(2)}, u32[]{:S(2)}) collective-permute-start(bf16[48,3072]{1,0:T(8,128)(2,1)S(1)} %pad_maximum_fusion.6), channel_id=1, source_target_pairs={{0,16},{2,18},{4,20},{6,22},{8,24},{10,26},{12,28},{14,30},{16,0},... | collective-permute-start | bytes 884744 | tf_op jit(solution)/shard_map/ppermute | solution.py:394
  29.8 12.3 %collective-permute-start.11 = (bf16[48,3072]{1,0:T(8,128)(2,1)S(1)}, bf16[48,3072]{1,0:T(8,128)(2,1)S(1)}, u32[]{:S(2)}, u32[]{:S(2)}) collective-permute-start(bf16[48,3072]{1,0:T(8,128)(2,1)S(1)} %pad_maximum_fusion.6), channel_id=1, source_target_pairs={{0,24},{2,26},{4,28},{6,30},{8,0},{10,2},{12,4},{14,6},{16,8},{18,... | collective-permute-start | bytes 884744 | tf_op jit(solution)/shard_map/ppermute | solution.py:394
  33.9 12.8 %collective-permute-start.9 = (bf16[48,3072]{1,0:T(8,128)(2,1)S(1)}, bf16[48,3072]{1,0:T(8,128)(2,1)S(1)}, u32[]{:S(2)}, u32[]{:S(2)}) collective-permute-start(bf16[48,3072]{1,0:T(8,128)(2,1)S(1)} %pad_maximum_fusion.6), channel_id=1, source_target_pairs={{0,8},{2,10},{4,12},{6,14},{8,16},{10,18},{12,20},{14,22},{16,24},... | collective-permute-start | bytes 884744 | tf_op jit(solution)/shard_map/ppermute | solution.py:394
  35.4 13.8 %collective-permute-start.6 = (bf16[384,768]{1,0:T(8,128)(2,1)S(1)}, bf16[384,768]{1,0:T(8,128)(2,1)S(1)}, u32[]{:S(2)}, u32[]{:S(2)}) collective-permute-start(bf16[384,768]{1,0:T(8,128)(2,1)S(1)} %pad_maximum_fusion.5.vo_own_ref), channel_id=1, source_target_pairs={{0,4},{2,6},{4,0},{6,2},{8,12},{10,14},{12,8},{14,10},{16,20},{18,... | collective-permute-start | bytes 1769480 | tf_op jit(solution)/shard_map/ppermute | solution.py:386
  36.0 13.5 %collective-permute-start.5 = (bf16[384,768]{1,0:T(8,128)(2,1)S(1)}, bf16[384,768]{1,0:T(8,128)(2,1)S(1)}, u32[]{:S(2)}, u32[]{:S(2)}) collective-permute-start(bf16[384,768]{1,0:T(8,128)(2,1)S(1)} %pad_maximum_fusion.4.qk_own_ref), channel_id=1, source_target_pairs={{0,2},{2,0},{4,6},{6,4},{8,10},{10,8},{12,14},{14,12},{16,18},{18,... | collective-permute-start | bytes 1769480 | tf_op jit(solution)/shard_map/ppermute | solution.py:382
  50.4 12.7 %collective-permute-start.12 = (bf16[192,1536]{1,0:T(8,128)(2,1)S(1)}, bf16[192,1536]{1,0:T(8,128)(2,1)S(1)}, u32[]{:S(2)}, u32[]{:S(2)}) collective-permute-start(bf16[192,1536]{1,0:T(8,128)(2,1)S(1)} %get-tuple-element.219), channel_id=1, source_target_pairs={{0,4},{2,6},{4,0},{6,2},{8,12},{10,14},{12,8},{14,10},{16,20},{18,... | collective-permute-start | bytes 1769480 | tf_op jit(solution)/shard_map/ppermute | solution.py:386
  51.8 12.2 %collective-permute-start.13 = (bf16[192,1536]{1,0:T(8,128)(2,1)S(1)}, bf16[192,1536]{1,0:T(8,128)(2,1)S(1)}, u32[]{:S(2)}, u32[]{:S(2)}) collective-permute-start(bf16[192,1536]{1,0:T(8,128)(2,1)S(1)} %get-tuple-element.218), channel_id=1, source_target_pairs={{0,2},{2,0},{4,6},{6,4},{8,10},{10,8},{12,14},{14,12},{16,18},{18,... | collective-permute-start | bytes 1769480 | tf_op jit(solution)/shard_map/ppermute | solution.py:382
  64.3 24.0 %collective-permute-start.15 = (bf16[384,1536]{1,0:T(8,128)(2,1)S(1)}, bf16[384,1536]{1,0:T(8,128)(2,1)S(1)}, u32[]{:S(2)}, u32[]{:S(2)}) collective-permute-start(bf16[384,1536]{1,0:T(8,128)(2,1)S(1)} %pad_maximum_fusion.3.ud_own_ref), channel_id=1, source_target_pairs={{0,4},{2,6},{4,0},{6,2},{8,12},{10,14},{12,8},{14,10},{16,20},{18,... | collective-permute-start | bytes 3538952 | tf_op jit(solution)/shard_map/ppermute | solution.py:386
  65.3 24.0 %collective-permute-start.14 = (bf16[384,1536]{1,0:T(8,128)(2,1)S(1)}, bf16[384,1536]{1,0:T(8,128)(2,1)S(1)}, u32[]{:S(2)}, u32[]{:S(2)}) collective-permute-start(bf16[384,1536]{1,0:T(8,128)(2,1)S(1)} %pad_maximum_fusion.2.gu_own_ref), channel_id=1, source_target_pairs={{0,2},{2,0},{4,6},{6,4},{8,10},{10,8},{12,14},{14,12},{16,18},{18,... | collective-permute-start | bytes 3538952 | tf_op jit(solution)/shard_map/ppermute | solution.py:382
  118.9 28.4 %collective-permute-start.18 = (bf16[384,1536]{1,0:T(8,128)(2,1)}, bf16[384,1536]{1,0:T(8,128)(2,1)S(1)}, u32[]{:S(2)}, u32[]{:S(2)}) collective-permute-start(bf16[384,1536]{1,0:T(8,128)(2,1)} %get-tuple-element.124), channel_id=1, source_target_pairs={{0,2},{2,0},{4,6},{6,4},{8,10},{10,8},{12,14},{14,12},{16,18},{18,... | collective-permute-start | bytes 3538952 | tf_op jit(solution)/shard_map/ppermute | solution.py:382
  120.3 28.2 %collective-permute-start.19 = (bf16[384,1536]{1,0:T(8,128)(2,1)}, bf16[384,1536]{1,0:T(8,128)(2,1)S(1)}, u32[]{:S(2)}, u32[]{:S(2)}) collective-permute-start(bf16[384,1536]{1,0:T(8,128)(2,1)} %get-tuple-element.125), channel_id=1, source_target_pairs={{0,4},{2,6},{4,0},{6,2},{8,12},{10,14},{12,8},{14,10},{16,20},{18,... | collective-permute-start | bytes 3538952 | tf_op jit(solution)/shard_map/ppermute | solution.py:386
  121.6 25.2 %collective-permute-start.20 = (bf16[512,768]{1,0:T(8,128)(2,1)}, bf16[512,768]{1,0:T(8,128)(2,1)S(1)}, u32[]{:S(2)}, u32[]{:S(2)}) collective-permute-start(bf16[512,768]{1,0:T(8,128)(2,1)} %get-tuple-element.126), channel_id=1, source_target_pairs={{0,1},{1,0},{2,3},{3,2},{4,5},{5,4},{6,7},{7,6},{8,9},{9,8},{10,11... | collective-permute-start | bytes 2359304 | tf_op jit(solution)/shard_map/ppermute | solution.py:916
  148.9 14.6 %collective-permute-start.23 = (bf16[192,1536]{1,0:T(8,128)(2,1)S(1)}, bf16[192,1536]{1,0:T(8,128)(2,1)S(1)}, u32[]{:S(2)}, u32[]{:S(2)}) collective-permute-start(bf16[192,1536]{1,0:T(8,128)(2,1)S(1)} %get-tuple-element.197), channel_id=1, source_target_pairs={{0,2},{2,0},{4,6},{6,4},{8,10},{10,8},{12,14},{14,12},{16,18},{18,... | collective-permute-start | bytes 1769480 | tf_op jit(solution)/shard_map/ppermute | solution.py:382
  150.2 14.6 %collective-permute-start.22 = (bf16[192,1536]{1,0:T(8,128)(2,1)S(1)}, bf16[192,1536]{1,0:T(8,128)(2,1)S(1)}, u32[]{:S(2)}, u32[]{:S(2)}) collective-permute-start(bf16[192,1536]{1,0:T(8,128)(2,1)S(1)} %get-tuple-element.199), channel_id=1, source_target_pairs={{0,4},{2,6},{4,0},{6,2},{8,12},{10,14},{12,8},{14,10},{16,20},{18,... | collective-permute-start | bytes 1769480 | tf_op jit(solution)/shard_map/ppermute | solution.py:386
  165.0 14.7 %collective-permute-start.27 = (bf16[96,1536]{1,0:T(8,128)(2,1)S(1)}, bf16[96,1536]{1,0:T(8,128)(2,1)S(1)}, u32[]{:S(2)}, u32[]{:S(2)}) collective-permute-start(bf16[96,1536]{1,0:T(8,128)(2,1)S(1)} %bitcast.46), channel_id=1, source_target_pairs={{0,16},{2,18},{4,20},{6,22},{8,24},{10,26},{12,28},{14,30},{16,0},... | collective-permute-start | bytes 884744 | tf_op jit(solution)/shard_map/ppermute | solution.py:422
  166.7 13.7 %collective-permute-start.24 = (bf16[384,768]{1,0:T(8,128)(2,1)S(1)}, bf16[384,768]{1,0:T(8,128)(2,1)S(1)}, u32[]{:S(2)}, u32[]{:S(2)}) collective-permute-start(bf16[384,768]{1,0:T(8,128)(2,1)S(1)} %copy-done.30), channel_id=1, source_target_pairs={{0,2},{2,0},{4,6},{6,4},{8,10},{10,8},{12,14},{14,12},{16,18},{18,... | collective-permute-start | bytes 1769480 | tf_op jit(solution)/shard_map/ppermute | solution.py:382
  167.6 12.9 %collective-permute-start.25 = (bf16[384,768]{1,0:T(8,128)(2,1)S(1)}, bf16[384,768]{1,0:T(8,128)(2,1)S(1)}, u32[]{:S(2)}, u32[]{:S(2)}) collective-permute-start(bf16[384,768]{1,0:T(8,128)(2,1)S(1)} %copy-done.32), channel_id=1, source_target_pairs={{0,4},{2,6},{4,0},{6,2},{8,12},{10,14},{12,8},{14,10},{16,20},{18,... | collective-permute-start | bytes 1769480 | tf_op jit(solution)/shard_map/ppermute | solution.py:386
  193.2 12.1 %collective-permute-start.39 = (bf16[512,768]{1,0:T(8,128)(2,1)S(1)}, bf16[512,768]{1,0:T(8,128)(2,1)S(1)}, u32[]{:S(2)}, u32[]{:S(2)}) collective-permute-start(bf16[512,768]{1,0:T(8,128)(2,1)S(1)} %copy-done.27), channel_id=1, source_target_pairs={{0,1},{1,0},{2,3},{3,2},{4,5},{5,4},{6,7},{7,6},{8,9},{9,8},{10,11... | collective-permute-start | bytes 2359304 | tf_op jit(solution)/shard_map/ppermute | solution.py:916
  199.6 13.4 %collective-permute-start.37 = (bf16[56,1536]{1,0:T(8,128)(2,1)S(1)}, bf16[56,1536]{1,0:T(8,128)(2,1)S(1)}, u32[]{:S(2)}, u32[]{:S(2)}) collective-permute-start(bf16[56,1536]{1,0:T(8,128)(2,1)S(1)} %get-tuple-element.236), channel_id=1, source_target_pairs={{0,16},{2,18},{4,20},{6,22},{8,24},{10,26},{12,28},{14,30},{16,0},... | collective-permute-start | bytes 516104 | tf_op jit(solution)/shard_map/ppermute | solution.py:394
  201.1 11.9 %collective-permute-start.38 = (bf16[56,1536]{1,0:T(8,128)(2,1)S(1)}, bf16[56,1536]{1,0:T(8,128)(2,1)S(1)}, u32[]{:S(2)}, u32[]{:S(2)}) collective-permute-start(bf16[56,1536]{1,0:T(8,128)(2,1)S(1)} %get-tuple-element.235), channel_id=1, source_target_pairs={{0,24},{2,26},{4,28},{6,30},{8,0},{10,2},{12,4},{14,6},{16,8},{18,... | collective-permute-start | bytes 516104 | tf_op jit(solution)/shard_map/ppermute | solution.py:394
  (50 other events, 335.0 us)
